TPU v7x, 32 devices: a whole 2x2x4 slice. The times are simulated.
32 devices in a mesh: stream: 8 (over z, y), vert: 4 (over x, core).
Axes of the slice: x: 2, y: 2, z: 4, core: 2. Of those that a mesh axis runs over, the one named last changes fastest.
Arguments:
- particles: float32 [256, 4, 7, 128], P('stream', 'vert'), may hold values from -4 to 4, as said below
- phase_flags: int32 [256, 4, 128], P('stream', 'vert'), may hold values 0 or 1
- neighbours: int32 [256, 4, 4], P('stream', 'vert'), may hold values from 0 to 7, as said below
- history: bfloat16 [256, 4, 3, 126, 128], P('stream', 'vert'), may hold values from -160 to 160
- basis_start: float32 [128, 64], replicated, may hold values from -0.5 to 0.5
Outputs:
- new_state: float32 [256, 4, 7, 128], P('stream', 'vert')
- filtered: float32 [256, 4, 3, 128], P('stream', 'vert')
Inputs may be any that keep to these rules, and one draw needn't show every extreme that they name: `particles`: rows 0 to 2 of a particle lie in 0 to 2, rows 3 to 5 in -4 to 4, row 6 in 0.97 to 1.03. `neighbours`: the 4 codes of one block are distinct.
All inputs are finite; a program needn't handle non-finite values. No bound on the sum of `phase_flags` on one device may be relied on, other than what follows from the above.
Results may differ from a plain program's by a relative error of at most 0.0003.
Values sent between devices are 32-bit elements; how exact they have to be, the bound alone decides.
No kernel may reach another device: no remote copies, remote signals or barrier semaphores. Data moves between devices by JAX's collectives and lax.ppermute only.
A program may use at most 64 MiB of HBM per device.

v0:
```python
import functools
import math

import jax
import jax.numpy as jnp
from jax import lax
from jax.experimental import pallas as pl
from jax.experimental.pallas import tpu as pltpu
from jax.sharding import PartitionSpec as P

POD_ITERS = 4
SEDIMENT_EXTRA = 1.65


ALPHA_KERNEL = 21.0 / (16.0 * math.pi)
VOLUME = 1.0 / 16.0
STIFFNESS = 100.0 / 7.0
TIME_STEP = 0.02
GRAVITY = 1.0
F32, BF16 = jnp.float32, jnp.bfloat16

def pieces(x):
    a = x.astype(BF16).astype(F32)
    r = x - a
    b = r.astype(BF16).astype(F32)
    return a, b, r - b

def rows(*parts):
    return jnp.concatenate(parts, axis=0)

def features(state):
    x, y, z = (state[i:i + 1] - 1.0 for i in range(3))
    u, v, w = (state[i:i + 1] for i in range(3, 6))
    r, rho = state[6:7], state[7:8]
    live = rho > 0.0
    mass = rho * VOLUME
    safe_rho = jnp.where(live, rho, 1.0)
    r2 = r * r
    pressure = jnp.where(live, STIFFNESS * (r2 * r2 * r2 * r - 1.0) / (safe_rho * r2), 0.0)
    zero, one = jnp.zeros_like(x), jnp.ones_like(x)
    norm = 0.25 * (x * x + y * y + z * z)
    mp = mass * pressure
    near = rows(-0.5 * x, -0.5 * y, -0.5 * z, one, norm, zero, zero, zero)
    near_x = rows(-0.5 * one, zero, zero, zero, 0.5 * x, zero, zero, zero)
    near_z = rows(zero, zero, -0.5 * one, zero, 0.5 * z, zero, zero, zero)
    mu, mv, mw = mass * u, mass * v, mass * w
    flux = mu * x + mv * y + mw * z
    sums_a = rows(mass, mass * x, mass * y, mass * z, mu, mv, mw, flux)
    sums_b = rows(mp, mp * x, mp * y, mp * z, zero, zero, zero, zero)
    sums_ax = rows(zero, mass, zero, zero, zero, zero, zero, mu)
    sums_az = rows(zero, zero, zero, mass, zero, zero, zero, mw)
    sums_bx = rows(zero, mp, zero, zero, zero, zero, zero, zero)
    sums_bz = rows(zero, zero, zero, mp, zero, zero, zero, zero)
    own = rows(x, y, z, norm, one, zero, zero, zero)
    return own, rows(near, sums_a, sums_b), rows(near_x, sums_ax, sums_bx), rows(near_z, sums_az, sums_bz), pressure

def step_kernel(codes_ref, edge_ref, mid_ref, low_ref, high_ref, out_ref, b0, b1, b2, nst, fst):
    count = out_ref.shape[0]
    ext = count + 2
    for col, ref in ((0, low_ref), (1, mid_ref), (2, high_ref)):
        def prep(i, _):
            st = ref[i]
            on = edge_ref[col]
            rowon = jnp.where(i == 0, edge_ref[3], jnp.where(i == ext - 1, edge_ref[4], 1))
            keep = (on * rowon).astype(F32)
            sel = lax.broadcasted_iota(jnp.int32, (8, 1), 0) == 7
            st = jnp.where(sel, st * keep, st)
            _, a, b, c, _ = features(st)
            b0[col * ext + i] = a
            b1[col * ext + i] = b
            b2[col * ext + i] = c
            return 0
        lax.fori_loop(0, ext, prep, 0, unroll=2)
    row = lax.broadcasted_iota(jnp.int32, (24, 1), 0)
    normrow = (row == 4).astype(F32)

    def block(b, _):
        st = mid_ref[b + 1]
        own, g_self, _, _, pressure = features(st)
        o1, o2, o3 = pieces(own)
        lhs = rows(o1, o1, o2, o2, o1, o3).astype(BF16)
        for n in range(5):
            if n == 0:
                g = b0[ext + b + 1]
            else:
                c = codes_ref[b, n - 1]
                o = c + jnp.where(c >= 4, 1, 0)
                ds1 = (o * 11) >> 5
                dv1 = o - 3 * ds1
                idx = dv1 * ext + b + ds1
                tx = 2.0 * (ds1 - 1).astype(F32)
                tz = 2.0 * (dv1 - 1).astype(F32)
                g = b0[idx] + tx * b1[idx] + tz * b2[idx] + normrow * (0.25 * (tx * tx + tz * tz))
            p1, p2, p3 = pieces(g[0:8])
            f1, f2, f3 = pieces(g[8:24])
            sl = slice(n * 128, (n + 1) * 128)
            nst[:, sl] = rows(p1, p2, p1, p2, p3, p1).astype(BF16)
            fst[:, sl] = rows(f1, f2, f3).astype(BF16)
        s = lax.dot_general(lhs, nst[...], (((0,), (0,)), ((), ())), preferred_element_type=F32)
        s = jnp.maximum(s, 1e-20)
        k = jnp.maximum(1.0 - s * lax.rsqrt(s), 0.0)
        wgt = k * k * k
        wh = wgt.astype(BF16)
        wl = (wgt - wh.astype(F32)).astype(BF16)
        f = fst[...]
        acc = lax.dot_general(wh, f, (((1,), (1,)), ((), ())), preferred_element_type=F32)
        acc = acc + lax.dot_general(wl, f, (((1,), (1,)), ((), ())), preferred_element_type=F32)
        acc = acc.T
        t = acc[0:16] + acc[16:32] + acc[32:48]
        x, vel = st[0:3] - 1.0, st[3:6]
        coef = -5.0 * ALPHA_KERNEL
        sw, swx, swv, swf = t[0:1], t[1:4], t[4:7], t[7:8]
        swp, swpx = t[8:9], t[9:12]
        dens = coef * (jnp.sum(vel * (x * sw - swx) - x * swv, axis=0, keepdims=True) + swf)
        acc3 = -coef * (pressure * (x * sw - swx) + x * swp - swpx)
        grav = jnp.where(lax.broadcasted_iota(jnp.int32, (3, 1), 0) == 2, -GRAVITY, 0.0)
        vel2 = vel + TIME_STEP * (acc3 + grav)
        pos2 = st[0:3] + TIME_STEP * vel2
        rho = st[7:8]
        r2 = st[6:7] + TIME_STEP * dens / rho
        out_ref[b] = rows(pos2, vel2, r2, rho)
        return 0
    lax.fori_loop(0, count, block, 0, unroll=1)

def sph_step(codes, edges, low, mid, high):
    ext, _, part = mid.shape
    count = ext - 2
    v = pl.BlockSpec(memory_space=pltpu.VMEM)
    sm = pl.BlockSpec(memory_space=pltpu.SMEM)
    return pl.pallas_call(step_kernel, out_shape=jax.ShapeDtypeStruct((count, 8, part), F32),
        in_specs=[sm, sm, v, v, v], out_specs=v,
        scratch_shapes=[pltpu.VMEM((3 * ext, 24, part), F32)] * 3 + [pltpu.VMEM((48, 5 * part), BF16)] * 2,
        compiler_params=pltpu.CompilerParams(vmem_limit_bytes=48 << 20),
    )(codes, edges, mid, low, high)


HI=lax.Precision.HIGHEST
def nt(a,b): return lax.dot_general(a,b,(((1,),(1,)),((),())),precision=HI,preferred_element_type=jnp.float32)
def diag_col(s):
    n=s.shape[0]
    eq=lax.broadcasted_iota(jnp.int32,s.shape,0)==lax.broadcasted_iota(jnp.int32,s.shape,1)
    return jnp.sum(jnp.where(eq,s,0.0),axis=1,keepdims=True)
def elim1(s,m):
    n=s.shape[0]
    sb=[s[8*k:8*k+8] for k in range(n//8)]; mb=[m[8*k:8*k+8] for k in range(n//8)]
    sub=lax.broadcasted_iota(jnp.int32,(8,1),0)
    for j in range(n):
        k,r=divmod(j,8)
        rs=sb[k][r:r+1]; rm=mb[k][r:r+1]
        inv=1.0/rs[:,j:j+1]
        us=rs*inv; um=rm*inv
        for i in range(k,n//8):
            c=sb[i][:,j:j+1]
            if i==k:
                if r==7: continue
                c=jnp.where(sub>r,c,0.0)
            sb[i]=sb[i]-c*us; mb[i]=mb[i]-c*um
    return jnp.concatenate(sb,0),jnp.concatenate(mb,0)
def ortho(m,elim):
    s=nt(m,m)
    d0=diag_col(s)
    s,m=elim(s,m)
    d=diag_col(s)
    return m*lax.rsqrt(d),jnp.min(d/d0)
def weights_kernel(elim,iters,g_ref,b_ref,w_ref,r_ref):
    g=g_ref[...]
    q=b_ref[...]
    q,r=ortho(q,elim)
    def it(i,c):
        q,r=c
        m=jnp.dot(q,g,precision=HI,preferred_element_type=jnp.float32)
        q,r2=ortho(m,elim)
        return q,jnp.minimum(r,r2)
    q,r=lax.fori_loop(0,iters,it,(q,r))
    n=q.shape[1]
    e=(lax.broadcasted_iota(jnp.int32,(1,n),1)==n-1).astype(jnp.float32)
    w=jnp.zeros((1,n),jnp.float32)
    for k in range(3):
        y=jnp.sum(q*(e-w),axis=1,keepdims=True)
        w=w+jnp.sum(q*y,axis=0,keepdims=True)
    w_ref[...]=jnp.broadcast_to(w,w_ref.shape)
    r_ref[...]=jnp.full(r_ref.shape,r)
def weights(elim,g,bt,iters=4):
    return pl.pallas_call(functools.partial(weights_kernel,elim,iters),out_shape=(jax.ShapeDtypeStruct((8,128),jnp.float32),jax.ShapeDtypeStruct((8,128),jnp.float32)),
      in_specs=[pl.BlockSpec(memory_space=pltpu.VMEM)]*2,out_specs=(pl.BlockSpec(memory_space=pltpu.VMEM),)*2)(g,bt)


def snapshot(hist_ref, first_ref, second_ref, b, c):
    new = rows(first_ref[b, 3 + c:4 + c], second_ref[b, 3 + c:4 + c])
    return rows(hist_ref[b, 0, c].astype(F32), new).astype(BF16)


def gram_kernel(hist_ref, first_ref, second_ref, g_ref):
    @pl.when(pl.program_id(0) == 0)
    def _():
        g_ref[...] = jnp.zeros_like(g_ref)
    total = g_ref[...]
    for b in range(hist_ref.shape[0]):
        for c in range(3):
            x = snapshot(hist_ref, first_ref, second_ref, b, c)
            total = total + lax.dot_general(x, x, (((1,), (1,)), ((), ())), preferred_element_type=F32)
    g_ref[...] = total


def filter_kernel(hist_ref, first_ref, second_ref, w_ref, out_ref):
    w1, w2, w3 = pieces(w_ref[0:1])
    zero = jnp.zeros_like(w1)
    w = rows(w1, w2, w3, zero, zero, zero, zero, zero).astype(BF16)
    for b in range(hist_ref.shape[0]):
        for c in range(3):
            x = snapshot(hist_ref, first_ref, second_ref, b, c)
            f = jnp.dot(w, x, preferred_element_type=F32)
            out_ref[b, 0, c:c + 1] = f[0:1] + f[1:2] + f[2:3]


def hist_specs(history, first, group):
    return [
        pl.BlockSpec((group,) + history.shape[1:], lambda i: (i, 0, 0, 0, 0)),
        pl.BlockSpec((group,) + first.shape[1:], lambda i: (i, 0, 0)),
        pl.BlockSpec((group,) + first.shape[1:], lambda i: (i, 0, 0)),
    ]


def local_gram(history, first, second):
    snaps = history.shape[3] + 2
    group = math.gcd(history.shape[0], 4)
    return pl.pallas_call(
        gram_kernel, grid=(history.shape[0] // group,),
        out_shape=jax.ShapeDtypeStruct((snaps, snaps), F32),
        in_specs=hist_specs(history, first, group),
        out_specs=pl.BlockSpec((snaps, snaps), lambda i: (0, 0)),
    )(history, first, second)


def local_filter(history, first, second, weights):
    group = math.gcd(history.shape[0], 4)
    count, _, comps, _, part = history.shape
    return pl.pallas_call(
        filter_kernel, grid=(count // group,),
        out_shape=jax.ShapeDtypeStruct((count, 1, comps, part), F32),
        in_specs=hist_specs(history, first, group) + [pl.BlockSpec(weights.shape, lambda i: (0, 0))],
        out_specs=pl.BlockSpec((group, 1, comps, part), lambda i: (i, 0, 0, 0)),
    )(history, first, second, weights)


def shift(x, axis, by):
    count = lax.axis_size(axis)
    return lax.ppermute(x, axis, [(i, (i + by) % count) for i in range(count)])


def reduce_all(x):
    for axis in ("vert", "stream"):
        count = lax.axis_size(axis)
        if count & (count - 1):
            x = lax.psum(x, axis)
            continue
        k = 1
        while k < count:
            x = x + lax.ppermute(x, axis, [(i, i ^ k) for i in range(count)])
            k *= 2
    return x


def advance(codes, edges, state):
    low_row = shift(state[-1:], "stream", 1)
    high_row = shift(state[:1], "stream", -1)
    mid = jnp.concatenate([low_row, state, high_row], axis=0)
    low = shift(mid, "vert", 1)
    high = shift(mid, "vert", -1)
    return sph_step(codes, edges, low, mid, high)


def body(particles, phase_flags, neighbours, history, basis_start):
    rest_density = 1.0 + SEDIMENT_EXTRA * phase_flags.astype(F32)
    state = jnp.concatenate([particles[:, 0], rest_density], axis=1)
    codes = neighbours[:, 0]
    s, v = lax.axis_index("stream"), lax.axis_index("vert")
    ns, nv = lax.axis_size("stream"), lax.axis_size("vert")
    one = jnp.ones((), jnp.int32)
    edges = jnp.stack([v > 0, one, v < nv - 1, s > 0, s < ns - 1, one, one, one]).astype(jnp.int32)
    first = advance(codes, edges, state)
    second = advance(codes, edges, first)
    gram = reduce_all(local_gram(history, first, second))
    w = weights(elim1, gram, basis_start.T, POD_ITERS)[0]
    return (second[:, None, 0:7], local_filter(history, first, second, w))


def solution(mesh):
    in_specs = (
        P("stream", "vert", None, None),
        P("stream", "vert", None),
        P("stream", "vert", None),
        P("stream", "vert", None, None, None),
        P(),
    )
    out_specs = (P("stream", "vert", None, None), P("stream", "vert", None, None))
    return jax.shard_map(body, mesh=mesh, in_specs=in_specs, out_specs=out_specs, check_vma=False)
```

profile of v0, /device:TPU:0, one launch (start us, length us, event | category | flops | bytes accessed | tf_op | source)
XLA Modules:
  0.0 138.0 jit_solution(10719174086042245582)
XLA Ops:
  0.6 0.9 copy.35
  1.6 0.7 multiply_add_fusion
  2.3 3.0 %collective-permute-start = (f32[1,8,128]{2,1,0:T(8,128)S(1)}, f32[1,8,128]{2,1,0:T(8,128)S(1)}, u32[]{:S(2)}, u32[]{:S(2)}) collective-permute-start(f32[1,8,128]{2,1,0:T(8,128)S(1)} %get-tuple-element.10), channel_id=1, source_target_pairs={{0,4},{4,8},{8,12},{12,16},{16,20},{20,24},{24,28},{28,0},{1,5},{5... | collective-permute-start | bytes 12296 | tf_op jit(solution)/shard_map/ppermute | solution.py:248
  5.3 3.1 %collective-permute-start.1 = (f32[1,8,128]{2,1,0:T(8,128)S(1)}, f32[1,8,128]{2,1,0:T(8,128)S(1)}, u32[]{:S(2)}, u32[]{:S(2)}) collective-permute-start(f32[1,8,128]{2,1,0:T(8,128)S(1)} %get-tuple-element.11), channel_id=1, source_target_pairs={{0,28},{4,0},{8,4},{12,8},{16,12},{20,16},{24,20},{28,24},{1,29},{... | collective-permute-start | bytes 12296 | tf_op jit(solution)/shard_map/ppermute | solution.py:248
  8.4 1.5 %collective-permute-done = f32[1,8,128]{2,1,0:T(8,128)S(1)} collective-permute-done((f32[1,8,128]{2,1,0:T(8,128)S(1)}, f32[1,8,128]{2,1,0:T(8,128)S(1)}, u32[]{:S(2)}, u32[]{:S(2)}) %collective-permute-start) | collective-permute-done | bytes 4128 | tf_op jit(solution)/shard_map/ppermute | solution.py:248
  10.0 0.0 collective-permute-done.1
  10.0 0.1 collective-permute-start.2
  10.1 1.7 %collective-permute-start.3 = (f32[34,8,128]{2,1,0:T(8,128)S(1)}, f32[34,8,128]{2,1,0:T(8,128)S(1)}, u32[]{:S(2)}, u32[]{:S(2)}) collective-permute-start(f32[34,8,128]{2,1,0:T(8,128)S(1)} %pad_maximum_fusion.mid_ref), channel_id=1, source_target_pairs={{0,3},{1,0},{2,1},{3,2},{4,7},{5,4},{6,5},{7,6},{8,11},{9,8},{10,9... | collective-permute-start | bytes 417800 | tf_op jit(solution)/shard_map/ppermute | solution.py:248
  11.8 0.8 copy.28.codes_ref
  12.6 0.1 stack.35.edge_ref
  12.7 1.9 %collective-permute-done.2.low_ref = f32[34,8,128]{2,1,0:T(8,128)S(1)} collective-permute-done((f32[34,8,128]{2,1,0:T(8,128)S(1)}, f32[34,8,128]{2,1,0:T(8,128)S(1)}, u32[]{:S(2)}, u32[]{:S(2)}) %collective-permute-start.2) | collective-permute-done | bytes 139296 | tf_op jit(solution)/shard_map/ppermute | solution.py:248
  14.5 0.7 collective-permute-done.3.high_ref
  15.2 21.2 %shard_map.68.first_ref = f32[32,8,128]{2,1,0:T(8,128)S(1)} custom-call(s32[32,4]{1,0:T(8,128)S(1)} %copy.28.codes_ref, s32[8]{0:T(128)S(1)} %stack.35.edge_ref, f32[34,8,128]{2,1,0:T(8,128)S(1)} %pad_maximum_fusion.mid_ref, f32[34,8,128]{2,1,0:T(8,128)S(1)} %collective-permute-done.2.low_ref, f32[34,8,128]{2,1,0:T(8,128)S(1)} %collective-permute-done.3.high_ref), custom_call_target="tpu_custom_call" | custom-call | tf_op jit(solution)/shard_map/pallas_call | solution.py:130
  36.4 0.0 copy-start
  36.4 1.3 collective-permute-start.4
  37.7 3.6 %collective-permute-start.5 = (f32[1,8,128]{2,1,0:T(8,128)S(1)}, f32[1,8,128]{2,1,0:T(8,128)S(1)}, u32[]{:S(2)}, u32[]{:S(2)}) collective-permute-start(f32[1,8,128]{2,1,0:T(8,128)S(1)} %get-tuple-element.13), channel_id=1, source_target_pairs={{0,28},{4,0},{8,4},{12,8},{16,12},{20,16},{24,20},{28,24},{1,29},{... | collective-permute-start | bytes 12296 | tf_op jit(solution)/shard_map/ppermute | solution.py:248
  41.3 1.5 %collective-permute-done.4 = f32[1,8,128]{2,1,0:T(8,128)S(1)} collective-permute-done((f32[1,8,128]{2,1,0:T(8,128)S(1)}, f32[1,8,128]{2,1,0:T(8,128)S(1)}, u32[]{:S(2)}, u32[]{:S(2)}) %collective-permute-start.4) | collective-permute-done | bytes 4128 | tf_op jit(solution)/shard_map/ppermute | solution.py:248
  42.8 0.0 collective-permute-done.5
  42.8 0.3 collective-permute-start.6
  43.1 1.5 %collective-permute-start.7 = (f32[34,8,128]{2,1,0:T(8,128)S(1)}, f32[34,8,128]{2,1,0:T(8,128)S(1)}, u32[]{:S(2)}, u32[]{:S(2)}) collective-permute-start(f32[34,8,128]{2,1,0:T(8,128)S(1)} %pad_maximum_fusion.1.mid_ref), channel_id=1, source_target_pairs={{0,3},{1,0},{2,1},{3,2},{4,7},{5,4},{6,5},{7,6},{8,11},{9,8},{10,9... | collective-permute-start | bytes 417800 | tf_op jit(solution)/shard_map/ppermute | solution.py:248
  44.6 4.7 %copy.30.hist_ref = bf16[32,1,3,126,128]{4,3,2,1,0:T(8,128)(2,1)} copy(bf16[32,1,3,126,128]{4,0,3,2,1:T(8,128)(2,1)} %param.8) | data formatting | bytes 6193152 | tf_op args[3]
  49.3 0.0 copy-done
  49.3 0.0 collective-permute-done.6.low_ref
  49.4 0.0 collective-permute-done.7.high_ref
  49.4 21.2 %shard_map.69.second_ref = f32[32,8,128]{2,1,0:T(8,128)S(1)} custom-call(s32[32,4]{1,0:T(8,128)S(1)} %copy.28.codes_ref, s32[8]{0:T(128)S(1)} %stack.35.edge_ref, f32[34,8,128]{2,1,0:T(8,128)S(1)} %pad_maximum_fusion.1.mid_ref, f32[34,8,128]{2,1,0:T(8,128)S(1)} %collective-permute-done.6.low_ref, f32[34,8,128]{2,1,0:T(8,128)S(1)} %collective-permute-done.7.high_ref), custom_call_target="tpu_custom_call" | custom-call | tf_op jit(solution)/shard_map/pallas_call | solution.py:130
  70.6 0.0 copy-start.1
  70.6 0.7 copy-done.1
  71.2 6.8 %shard_map.70 = f32[128,128]{1,0:T(8,128)} custom-call(bf16[32,1,3,126,128]{4,3,2,1,0:T(8,128)(2,1)} %copy.30.hist_ref, f32[32,8,128]{2,1,0:T(8,128)} %copy-done, f32[32,8,128]{2,1,0:T(8,128)} %copy-done.1), custom_call_target="tpu_custom_call" | custom-call | tf_op jit(solution)/shard_map/pallas_call | solution.py:227
  78.0 0.2 collective-permute-start.8
  78.3 1.2 collective-permute-done.8
  79.5 0.9 add.23
  80.3 1.9 %collective-permute-start.9 = (f32[128,128]{1,0:T(8,128)S(1)}, f32[128,128]{1,0:T(8,128)S(1)}, u32[]{:S(2)}, u32[]{:S(2)}) collective-permute-start(f32[128,128]{1,0:T(8,128)S(1)} %add.23), channel_id=1, source_target_pairs={{0,2},{1,3},{2,0},{3,1},{4,6},{5,7},{6,4},{7,5},{8,10},{9,11},{10,... | collective-permute-start | bytes 196616 | tf_op jit(solution)/shard_map/ppermute | solution.py:259
  82.3 2.4 %collective-permute-done.9 = f32[128,128]{1,0:T(8,128)S(1)} collective-permute-done((f32[128,128]{1,0:T(8,128)S(1)}, f32[128,128]{1,0:T(8,128)S(1)}, u32[]{:S(2)}, u32[]{:S(2)}) %collective-permute-start.9) | collective-permute-done | bytes 65568 | tf_op jit(solution)/shard_map/ppermute | solution.py:259
  84.7 0.1 collective-permute-start.10
  84.8 4.2 %collective-permute-done.10 = f32[128,128]{1,0:T(8,128)S(1)} collective-permute-done((f32[128,128]{1,0:T(8,128)S(1)}, f32[128,128]{1,0:T(8,128)S(1)}, u32[]{:S(2)}, u32[]{:S(2)}) %collective-permute-start.10) | collective-permute-done | bytes 65568 | tf_op jit(solution)/shard_map/ppermute | solution.py:259
  89.0 0.2 collective-permute-start.11
  89.2 4.2 %collective-permute-done.11 = f32[128,128]{1,0:T(8,128)S(1)} collective-permute-done((f32[128,128]{1,0:T(8,128)S(1)}, f32[128,128]{1,0:T(8,128)S(1)}, u32[]{:S(2)}, u32[]{:S(2)}) %collective-permute-start.11) | collective-permute-done | bytes 65568 | tf_op jit(solution)/shard_map/ppermute | solution.py:259
  93.4 1.9 %collective-permute-start.12 = (f32[128,128]{1,0:T(8,128)S(1)}, f32[128,128]{1,0:T(8,128)S(1)}, u32[]{:S(2)}, u32[]{:S(2)}) collective-permute-start(f32[128,128]{1,0:T(8,128)S(1)} %add.26), channel_id=1, source_target_pairs={{0,16},{4,20},{8,24},{12,28},{16,0},{20,4},{24,8},{28,12},{1,17},{... | collective-permute-start | bytes 196616 | tf_op jit(solution)/shard_map/ppermute | solution.py:259
  95.3 0.9 slice_bitcast_fusion
  96.2 0.8 copy.31
  97.0 2.3 %collective-permute-done.12 = f32[128,128]{1,0:T(8,128)S(1)} collective-permute-done((f32[128,128]{1,0:T(8,128)S(1)}, f32[128,128]{1,0:T(8,128)S(1)}, u32[]{:S(2)}, u32[]{:S(2)}) %collective-permute-start.12) | collective-permute-done | bytes 65568 | tf_op jit(solution)/shard_map/ppermute | solution.py:259
  99.3 0.6 add.27.g_ref
  99.9 30.4 %shard_map.71 = (f32[8,128]{1,0:T(8,128)}, f32[8,128]{1,0:T(8,128)}) custom-call(f32[128,128]{1,0:T(8,128)} %add.27.g_ref, f32[64,128]{1,0:T(8,128)} %bitcast.22), custom_call_target="tpu_custom_call" | custom-call | tf_op jit(solution)/shard_map/pallas_call | solution.py:184
  130.3 6.2 %shard_map.72 = f32[32,1,3,128]{3,2,1,0:T(4,128)} custom-call(bf16[32,1,3,126,128]{4,3,2,1,0:T(8,128)(2,1)} %copy.30.hist_ref, f32[32,8,128]{2,1,0:T(8,128)} %copy-done, f32[32,8,128]{2,1,0:T(8,128)} %copy-done.1, f32[8,128]{1,0:T(8,128)} %get-tuple-element.3.w_ref), custom_call_target="tpu_custom_call" | custom-call | tf_op jit(solution)/shard_map/pallas_call | solution.py:238
  136.5 1.5 %copy.32 = f32[32,1,3,128]{3,1,2,0:T(1,128)} copy(f32[32,1,3,128]{3,2,1,0:T(4,128)} %shard_map.72) | data formatting | bytes 98304
  (10 shorter events, 0.1 us)
Async XLA Ops:
  2.3 7.6 %collective-permute-start = (f32[1,8,128]{2,1,0:T(8,128)S(1)}, f32[1,8,128]{2,1,0:T(8,128)S(1)}, u32[]{:S(2)}, u32[]{:S(2)}) collective-permute-start(f32[1,8,128]{2,1,0:T(8,128)S(1)} %get-tuple-element.10), channel_id=1, source_target_pairs={{0,4},{4,8},{8,12},{12,16},{16,20},{20,24},{24,28},{28,0},{1,5},{5... | collective-permute-start | bytes 12296 | tf_op jit(solution)/shard_map/ppermute | solution.py:248
  5.3 4.6 %collective-permute-start.1 = (f32[1,8,128]{2,1,0:T(8,128)S(1)}, f32[1,8,128]{2,1,0:T(8,128)S(1)}, u32[]{:S(2)}, u32[]{:S(2)}) collective-permute-start(f32[1,8,128]{2,1,0:T(8,128)S(1)} %get-tuple-element.11), channel_id=1, source_target_pairs={{0,28},{4,0},{8,4},{12,8},{16,12},{20,16},{24,20},{28,24},{1,29},{... | collective-permute-start | bytes 12296 | tf_op jit(solution)/shard_map/ppermute | solution.py:248
  10.0 4.5 %collective-permute-start.2 = (f32[34,8,128]{2,1,0:T(8,128)S(1)}, f32[34,8,128]{2,1,0:T(8,128)S(1)}, u32[]{:S(2)}, u32[]{:S(2)}) collective-permute-start(f32[34,8,128]{2,1,0:T(8,128)S(1)} %pad_maximum_fusion.mid_ref), channel_id=1, source_target_pairs={{0,1},{1,2},{2,3},{3,0},{4,5},{5,6},{6,7},{7,4},{8,9},{9,10},{10,1... | collective-permute-start | bytes 417800 | tf_op jit(solution)/shard_map/ppermute | solution.py:248
  10.1 5.1 %collective-permute-start.3 = (f32[34,8,128]{2,1,0:T(8,128)S(1)}, f32[34,8,128]{2,1,0:T(8,128)S(1)}, u32[]{:S(2)}, u32[]{:S(2)}) collective-permute-start(f32[34,8,128]{2,1,0:T(8,128)S(1)} %pad_maximum_fusion.mid_ref), channel_id=1, source_target_pairs={{0,3},{1,0},{2,1},{3,2},{4,7},{5,4},{6,5},{7,6},{8,11},{9,8},{10,9... | collective-permute-start | bytes 417800 | tf_op jit(solution)/shard_map/ppermute | solution.py:248
  36.4 12.9 %copy-start = (f32[32,8,128]{2,1,0:T(8,128)}, f32[32,8,128]{2,1,0:T(8,128)S(1)}, u32[]{:S(2)}) copy-start(f32[32,8,128]{2,1,0:T(8,128)S(1)} %shard_map.68.first_ref) | copy-start | bytes 393220
  36.4 6.4 %collective-permute-start.4 = (f32[1,8,128]{2,1,0:T(8,128)S(1)}, f32[1,8,128]{2,1,0:T(8,128)S(1)}, u32[]{:S(2)}, u32[]{:S(2)}) collective-permute-start(f32[1,8,128]{2,1,0:T(8,128)S(1)} %get-tuple-element.12), channel_id=1, source_target_pairs={{0,4},{4,8},{8,12},{12,16},{16,20},{20,24},{24,28},{28,0},{1,5},{5... | collective-permute-start | bytes 12296 | tf_op jit(solution)/shard_map/ppermute | solution.py:248
  37.7 5.1 %collective-permute-start.5 = (f32[1,8,128]{2,1,0:T(8,128)S(1)}, f32[1,8,128]{2,1,0:T(8,128)S(1)}, u32[]{:S(2)}, u32[]{:S(2)}) collective-permute-start(f32[1,8,128]{2,1,0:T(8,128)S(1)} %get-tuple-element.13), channel_id=1, source_target_pairs={{0,28},{4,0},{8,4},{12,8},{16,12},{20,16},{24,20},{28,24},{1,29},{... | collective-permute-start | bytes 12296 | tf_op jit(solution)/shard_map/ppermute | solution.py:248
  42.8 6.5 %collective-permute-start.6 = (f32[34,8,128]{2,1,0:T(8,128)S(1)}, f32[34,8,128]{2,1,0:T(8,128)S(1)}, u32[]{:S(2)}, u32[]{:S(2)}) collective-permute-start(f32[34,8,128]{2,1,0:T(8,128)S(1)} %pad_maximum_fusion.1.mid_ref), channel_id=1, source_target_pairs={{0,1},{1,2},{2,3},{3,0},{4,5},{5,6},{6,7},{7,4},{8,9},{9,10},{10,1... | collective-permute-start | bytes 417800 | tf_op jit(solution)/shard_map/ppermute | solution.py:248
  43.1 6.2 %collective-permute-start.7 = (f32[34,8,128]{2,1,0:T(8,128)S(1)}, f32[34,8,128]{2,1,0:T(8,128)S(1)}, u32[]{:S(2)}, u32[]{:S(2)}) collective-permute-start(f32[34,8,128]{2,1,0:T(8,128)S(1)} %pad_maximum_fusion.1.mid_ref), channel_id=1, source_target_pairs={{0,3},{1,0},{2,1},{3,2},{4,7},{5,4},{6,5},{7,6},{8,11},{9,8},{10,9... | collective-permute-start | bytes 417800 | tf_op jit(solution)/shard_map/ppermute | solution.py:248
  70.6 0.7 copy-start.1
  78.0 1.5 %collective-permute-start.8 = (f32[128,128]{1,0:T(8,128)}, f32[128,128]{1,0:T(8,128)S(1)}, u32[]{:S(2)}, u32[]{:S(2)}) collective-permute-start(f32[128,128]{1,0:T(8,128)} %shard_map.70), channel_id=1, source_target_pairs={{0,1},{1,0},{2,3},{3,2},{4,5},{5,4},{6,7},{7,6},{8,9},{9,8},{10,11... | collective-permute-start | bytes 196616 | tf_op jit(solution)/shard_map/ppermute | solution.py:259
  80.3 4.3 %collective-permute-start.9 = (f32[128,128]{1,0:T(8,128)S(1)}, f32[128,128]{1,0:T(8,128)S(1)}, u32[]{:S(2)}, u32[]{:S(2)}) collective-permute-start(f32[128,128]{1,0:T(8,128)S(1)} %add.23), channel_id=1, source_target_pairs={{0,2},{1,3},{2,0},{3,1},{4,6},{5,7},{6,4},{7,5},{8,10},{9,11},{10,... | collective-permute-start | bytes 196616 | tf_op jit(solution)/shard_map/ppermute | solution.py:259
  84.7 4.3 %collective-permute-start.10 = (f32[128,128]{1,0:T(8,128)S(1)}, f32[128,128]{1,0:T(8,128)S(1)}, u32[]{:S(2)}, u32[]{:S(2)}) collective-permute-start(f32[128,128]{1,0:T(8,128)S(1)} %add.24), channel_id=1, source_target_pairs={{0,4},{4,0},{8,12},{12,8},{16,20},{20,16},{24,28},{28,24},{1,5},{5... | collective-permute-start | bytes 196616 | tf_op jit(solution)/shard_map/ppermute | solution.py:259
  89.0 4.3 %collective-permute-start.11 = (f32[128,128]{1,0:T(8,128)S(1)}, f32[128,128]{1,0:T(8,128)S(1)}, u32[]{:S(2)}, u32[]{:S(2)}) collective-permute-start(f32[128,128]{1,0:T(8,128)S(1)} %add.25), channel_id=1, source_target_pairs={{0,8},{4,12},{8,0},{12,4},{16,24},{20,28},{24,16},{28,20},{1,9},{5... | collective-permute-start | bytes 196616 | tf_op jit(solution)/shard_map/ppermute | solution.py:259
  93.4 5.9 %collective-permute-start.12 = (f32[128,128]{1,0:T(8,128)S(1)}, f32[128,128]{1,0:T(8,128)S(1)}, u32[]{:S(2)}, u32[]{:S(2)}) collective-permute-start(f32[128,128]{1,0:T(8,128)S(1)} %add.26), channel_id=1, source_target_pairs={{0,16},{4,20},{8,24},{12,28},{16,0},{20,4},{24,8},{28,12},{1,17},{... | collective-permute-start | bytes 196616 | tf_op jit(solution)/shard_map/ppermute | solution.py:259
where the time goes:
time: 139 us; the launch traced here: 138 us
  Pallas kernels  85.8 us (62%)
  waiting for transfers between devices  20 us (14%)
  starting transfers between devices  18.9 us (14%)
  local copies, waits for them, and re-layouts  10.4 us (7%)
  other arithmetic  2.29 us (2%)
    pallas_call x2, Pallas kernels, sph_step(): pl.pallas_call(step_kernel, out_shape=jax.ShapeDtypeStruct((count, 8, par...  42.4 us
    pallas_call x1, Pallas kernels, weights(): pl.pallas_call(functools.partial(weights_kernel, elim, iters), out_shape=...  30.4 us
    ppermute x8, starting transfers between devices, shift(): return lax.ppermute(x, axis, [(i, (i + by) % count) for i in range(count)])  14.5 us
    ppermute x5, waiting for transfers between devices, reduce_all(): x = x + lax.ppermute(x, axis, [(i, i ^ k) for i in range(count)])  14.4 us
    unnamed x7, local copies, waits for them, and re-layouts  7.66 us
    pallas_call x1, Pallas kernels, local_gram(): pl.pallas_call(gram_kernel, grid=(history.shape[0] // group,), out_shape=...  6.78 us
    pallas_call x1, Pallas kernels, local_filter(): pl.pallas_call(filter_kernel, grid=(count // group,), out_shape=jax.Shape...  6.23 us
    ppermute x8, waiting for transfers between devices, shift(): return lax.ppermute(x, axis, [(i, (i + by) % count) for i in range(count)])  5.6 us
  transfers between devices with their start and end apart: 13, of which 9 were waited for; matrix products, arithmetic and copies ran while one was open for 5% of the time, Pallas kernels for 0%

commit v1 on v0

--- a/solution.py
+++ b/solution.py
@@ -28,33 +28,42 @@
 def rows(*parts):
     return jnp.concatenate(parts, axis=0)
 
+def row_is(*which):
+    index = lax.broadcasted_iota(jnp.int32, (8, 128), 0)
+    hit = index == which[0]
+    for w in which[1:]:
+        hit = hit | (index == w)
+    return hit
+
+def spread(row):
+    return jnp.broadcast_to(row, (8, row.shape[1]))
+
 def features(state):
-    x, y, z = (state[i:i + 1] - 1.0 for i in range(3))
-    u, v, w = (state[i:i + 1] for i in range(3, 6))
-    r, rho = state[6:7], state[7:8]
+    centred = jnp.where(row_is(0, 1, 2), state - 1.0, state)
+    r, rho = spread(state[6:7]), spread(state[7:8])
     live = rho > 0.0
     mass = rho * VOLUME
-    safe_rho = jnp.where(live, rho, 1.0)
     r2 = r * r
-    pressure = jnp.where(live, STIFFNESS * (r2 * r2 * r2 * r - 1.0) / (safe_rho * r2), 0.0)
-    zero, one = jnp.zeros_like(x), jnp.ones_like(x)
-    norm = 0.25 * (x * x + y * y + z * z)
+    pressure = jnp.where(live, STIFFNESS * (r2 * r2 * r2 * r - 1.0) / (jnp.where(live, rho, 1.0) * r2), 0.0)
     mp = mass * pressure
-    near = rows(-0.5 * x, -0.5 * y, -0.5 * z, one, norm, zero, zero, zero)
-    near_x = rows(-0.5 * one, zero, zero, zero, 0.5 * x, zero, zero, zero)
-    near_z = rows(zero, zero, -0.5 * one, zero, 0.5 * z, zero, zero, zero)
-    mu, mv, mw = mass * u, mass * v, mass * w
-    flux = mu * x + mv * y + mw * z
-    sums_a = rows(mass, mass * x, mass * y, mass * z, mu, mv, mw, flux)
-    sums_b = rows(mp, mp * x, mp * y, mp * z, zero, zero, zero, zero)
-    sums_ax = rows(zero, mass, zero, zero, zero, zero, zero, mu)
-    sums_az = rows(zero, zero, zero, mass, zero, zero, zero, mw)
-    sums_bx = rows(zero, mp, zero, zero, zero, zero, zero, zero)
-    sums_bz = rows(zero, zero, zero, mp, zero, zero, zero, zero)
-    own = rows(x, y, z, norm, one, zero, zero, zero)
-    return own, rows(near, sums_a, sums_b), rows(near_x, sums_ax, sums_bx), rows(near_z, sums_az, sums_bz), pressure
-
-def step_kernel(codes_ref, edge_ref, mid_ref, low_ref, high_ref, out_ref, b0, b1, b2, nst, fst):
+    place = jnp.where(row_is(0, 1, 2), centred, 0.0)
+    norm = 0.25 * jnp.sum(place * place, axis=0, keepdims=True)
+    speed = jnp.where(row_is(0, 1, 2), pltpu.roll(centred, 5, 0), 0.0)
+    flux = jnp.sum(place * speed, axis=0, keepdims=True)
+    own = jnp.where(row_is(3), norm, jnp.where(row_is(4), 1.0, place))
+    near = jnp.where(row_is(3), 1.0, jnp.where(row_is(4), norm, -0.5 * place))
+    moved = jnp.where(row_is(0), 1.0, jnp.where(row_is(7), flux, pltpu.roll(centred, 1, 0)))
+    sums_a = mass * moved
+    sums_b = jnp.where(row_is(0, 1, 2, 3), mp * moved, 0.0)
+    near_x = jnp.where(row_is(0), -0.5, jnp.where(row_is(4), 0.5 * centred[0:1], 0.0))
+    near_z = jnp.where(row_is(2), -0.5, jnp.where(row_is(4), 0.5 * centred[2:3], 0.0))
+    sums_ax = mass * jnp.where(row_is(1), 1.0, jnp.where(row_is(7), centred[3:4], 0.0))
+    sums_az = mass * jnp.where(row_is(3), 1.0, jnp.where(row_is(7), centred[5:6], 0.0))
+    sums_bx = jnp.where(row_is(1), mp, 0.0)
+    sums_bz = jnp.where(row_is(3), mp, 0.0)
+    return own, rows(near, sums_a, sums_b), rows(near_x, sums_ax, sums_bx), rows(near_z, sums_az, sums_bz), pressure[0:1]
+
+def step_kernel(codes_ref, edge_ref, mid_ref, low_ref, high_ref, out_ref, b0, b1, b2):
     count = out_ref.shape[0]
     ext = count + 2
     for col, ref in ((0, low_ref), (1, mid_ref), (2, high_ref)):
@@ -70,7 +79,7 @@
             b1[col * ext + i] = b
             b2[col * ext + i] = c
             return 0
-        lax.fori_loop(0, ext, prep, 0, unroll=2)
+        lax.fori_loop(0, ext, prep, 0, unroll=2 if ext % 2 == 0 else 1)
     row = lax.broadcasted_iota(jnp.int32, (24, 1), 0)
     normrow = (row == 4).astype(F32)
 
@@ -79,6 +88,7 @@
         own, g_self, _, _, pressure = features(st)
         o1, o2, o3 = pieces(own)
         lhs = rows(o1, o1, o2, o2, o1, o3).astype(BF16)
+        ns, fs = [], []
         for n in range(5):
             if n == 0:
                 g = b0[ext + b + 1]
@@ -93,19 +103,17 @@
                 g = b0[idx] + tx * b1[idx] + tz * b2[idx] + normrow * (0.25 * (tx * tx + tz * tz))
             p1, p2, p3 = pieces(g[0:8])
             f1, f2, f3 = pieces(g[8:24])
-            sl = slice(n * 128, (n + 1) * 128)
-            nst[:, sl] = rows(p1, p2, p1, p2, p3, p1).astype(BF16)
-            fst[:, sl] = rows(f1, f2, f3).astype(BF16)
-        s = lax.dot_general(lhs, nst[...], (((0,), (0,)), ((), ())), preferred_element_type=F32)
+            ns.append(rows(p1, p2, p1, p2, p3, p1).astype(BF16))
+            fs.append(rows(f1, f2, f3).astype(BF16))
+        nall = jnp.concatenate(ns, axis=1)
+        f = jnp.concatenate(fs+fs, axis=1)
+        s = lax.dot_general(nall, lhs, (((0,), (0,)), ((), ())), preferred_element_type=F32)
         s = jnp.maximum(s, 1e-20)
         k = jnp.maximum(1.0 - s * lax.rsqrt(s), 0.0)
         wgt = k * k * k
         wh = wgt.astype(BF16)
         wl = (wgt - wh.astype(F32)).astype(BF16)
-        f = fst[...]
-        acc = lax.dot_general(wh, f, (((1,), (1,)), ((), ())), preferred_element_type=F32)
-        acc = acc + lax.dot_general(wl, f, (((1,), (1,)), ((), ())), preferred_element_type=F32)
-        acc = acc.T
+        acc = jnp.dot(f, jnp.concatenate([wh,wl],0), preferred_element_type=F32)
         t = acc[0:16] + acc[16:32] + acc[32:48]
         x, vel = st[0:3] - 1.0, st[3:6]
         coef = -5.0 * ALPHA_KERNEL
@@ -120,7 +128,7 @@
         r2 = st[6:7] + TIME_STEP * dens / rho
         out_ref[b] = rows(pos2, vel2, r2, rho)
         return 0
-    lax.fori_loop(0, count, block, 0, unroll=1)
+    lax.fori_loop(0, count, block, 0, unroll=math.gcd(count, 8))
 
 def sph_step(codes, edges, low, mid, high):
     ext, _, part = mid.shape
@@ -129,60 +137,104 @@
     sm = pl.BlockSpec(memory_space=pltpu.SMEM)
     return pl.pallas_call(step_kernel, out_shape=jax.ShapeDtypeStruct((count, 8, part), F32),
         in_specs=[sm, sm, v, v, v], out_specs=v,
-        scratch_shapes=[pltpu.VMEM((3 * ext, 24, part), F32)] * 3 + [pltpu.VMEM((48, 5 * part), BF16)] * 2,
+        scratch_shapes=[pltpu.VMEM((3 * ext, 24, part), F32)] * 3,
         compiler_params=pltpu.CompilerParams(vmem_limit_bytes=48 << 20),
     )(codes, edges, mid, low, high)
 
 
-HI=lax.Precision.HIGHEST
-def nt(a,b): return lax.dot_general(a,b,(((1,),(1,)),((),())),precision=HI,preferred_element_type=jnp.float32)
-def diag_col(s):
-    n=s.shape[0]
-    eq=lax.broadcasted_iota(jnp.int32,s.shape,0)==lax.broadcasted_iota(jnp.int32,s.shape,1)
-    return jnp.sum(jnp.where(eq,s,0.0),axis=1,keepdims=True)
-def elim1(s,m):
-    n=s.shape[0]
-    sb=[s[8*k:8*k+8] for k in range(n//8)]; mb=[m[8*k:8*k+8] for k in range(n//8)]
-    sub=lax.broadcasted_iota(jnp.int32,(8,1),0)
-    for j in range(n):
-        k,r=divmod(j,8)
-        rs=sb[k][r:r+1]; rm=mb[k][r:r+1]
-        inv=1.0/rs[:,j:j+1]
-        us=rs*inv; um=rm*inv
-        for i in range(k,n//8):
-            c=sb[i][:,j:j+1]
-            if i==k:
-                if r==7: continue
-                c=jnp.where(sub>r,c,0.0)
-            sb[i]=sb[i]-c*us; mb[i]=mb[i]-c*um
-    return jnp.concatenate(sb,0),jnp.concatenate(mb,0)
-def ortho(m,elim):
-    s=nt(m,m)
-    d0=diag_col(s)
-    s,m=elim(s,m)
-    d=diag_col(s)
-    return m*lax.rsqrt(d),jnp.min(d/d0)
-def weights_kernel(elim,iters,g_ref,b_ref,w_ref,r_ref):
-    g=g_ref[...]
-    q=b_ref[...]
-    q,r=ortho(q,elim)
-    def it(i,c):
-        q,r=c
-        m=jnp.dot(q,g,precision=HI,preferred_element_type=jnp.float32)
-        q,r2=ortho(m,elim)
-        return q,jnp.minimum(r,r2)
-    q,r=lax.fori_loop(0,iters,it,(q,r))
-    n=q.shape[1]
-    e=(lax.broadcasted_iota(jnp.int32,(1,n),1)==n-1).astype(jnp.float32)
-    w=jnp.zeros((1,n),jnp.float32)
-    for k in range(3):
-        y=jnp.sum(q*(e-w),axis=1,keepdims=True)
-        w=w+jnp.sum(q*y,axis=0,keepdims=True)
-    w_ref[...]=jnp.broadcast_to(w,w_ref.shape)
-    r_ref[...]=jnp.full(r_ref.shape,r)
-def weights(elim,g,bt,iters=4):
-    return pl.pallas_call(functools.partial(weights_kernel,elim,iters),out_shape=(jax.ShapeDtypeStruct((8,128),jnp.float32),jax.ShapeDtypeStruct((8,128),jnp.float32)),
-      in_specs=[pl.BlockSpec(memory_space=pltpu.VMEM)]*2,out_specs=(pl.BlockSpec(memory_space=pltpu.VMEM),)*2)(g,bt)
+HIGHEST = lax.Precision.HIGHEST
+REPEAT_BELOW = 1e-5
+
+
+def gram_of(m):
+    return lax.dot_general(m, m, (((1,), (1,)), ((), ())), precision=HIGHEST, preferred_element_type=F32)
+
+
+def orthonormal(m):
+    n, wide = m.shape
+    nb = n // 8
+    s = gram_of(m)
+    s = jnp.concatenate([s, jnp.zeros((n, wide - n), F32)], axis=1)
+    sb = [s[8 * k:8 * k + 8] for k in range(nb)]
+    mb = [m[8 * k:8 * k + 8] for k in range(nb)]
+    sub = lax.broadcasted_iota(jnp.int32, (8, wide), 0)
+    full = lambda x: jnp.broadcast_to(x, (8, wide))
+    worst = None
+    for k in range(nb):
+        p = 8 * k
+        norm0 = jnp.sum(m[8 * k:8 * k + 8] * m[8 * k:8 * k + 8], axis=1, keepdims=True)
+        rs = [full(sb[k][i:i + 1]) for i in range(8)]
+        rm = [full(mb[k][i:i + 1]) for i in range(8)]
+        e = [[full(rs[i][:, p + j:p + j + 1]) for j in range(i + 1)] for i in range(8)]
+        cols = [[full(sb[t][:, p + j:p + j + 1]) for j in range(8)] for t in range(k + 1, nb)]
+        inv, low = [], [[None] * 8 for _ in range(8)]
+        for j in range(8):
+            inv.append(1.0 / e[j][j])
+            for i in range(j + 1, 8):
+                for t in range(j + 1, i + 1):
+                    e[i][t] = e[i][t] - (e[i][j] * e[t][j]) * inv[j]
+            for i in range(j + 1, 8):
+                low[i][j] = e[i][j] * inv[j]
+            for i in range(j + 1, 8):
+                rs[i] = rs[i] - low[i][j] * rs[j]
+                rm[i] = rm[i] - low[i][j] * rm[j]
+        d = e[0][0]
+        out = rm[0]
+        for i in range(1, 8):
+            d = jnp.where(sub == i, e[i][i], d)
+            out = jnp.where(sub == i, rm[i], out)
+        mb[k] = out * lax.rsqrt(d)
+        ratio = d / norm0
+        worst = ratio if worst is None else jnp.minimum(worst, ratio)
+        if k == nb - 1:
+            break
+        us = [rs[j] * inv[j] for j in range(8)]
+        um = [rm[j] * inv[j] for j in range(8)]
+        for t in range(k + 1, nb):
+            c = cols[t - k - 1]
+            for j in range(8):
+                for i in range(j + 1, 8):
+                    c[i] = c[i] - low[i][j] * c[j]
+                sb[t] = sb[t] - c[j] * us[j]
+                mb[t] = mb[t] - c[j] * um[j]
+    return jnp.concatenate(mb, 0), jnp.min(worst)
+
+
+def repeated(m, q_ref):
+    q, worst = orthonormal(m)
+    q_ref[...] = q
+
+    @pl.when(jnp.logical_not(worst >= REPEAT_BELOW))
+    def _():
+        q_ref[...] = orthonormal(q_ref[...])[0]
+
+
+def weights_kernel(iters, g_ref, b_ref, w_ref, q_ref):
+    repeated(b_ref[...], q_ref)
+
+    def iterate(i, _):
+        repeated(jnp.dot(q_ref[...], g_ref[...], precision=HIGHEST, preferred_element_type=F32), q_ref)
+        return 0
+
+    lax.fori_loop(0, iters, iterate, 0)
+    q = q_ref[...]
+    n = q.shape[1]
+    last = (lax.broadcasted_iota(jnp.int32, (1, n), 1) == n - 1).astype(F32)
+    w = jnp.zeros((1, n), F32)
+    for _ in range(3):
+        y = jnp.sum(q * (last - w), axis=1, keepdims=True)
+        w = w + jnp.sum(q * y, axis=0, keepdims=True)
+    w_ref[...] = jnp.broadcast_to(w, w_ref.shape)
+
+
+def weights(gram, basis_t):
+    v = pl.BlockSpec(memory_space=pltpu.VMEM)
+    return pl.pallas_call(
+        functools.partial(weights_kernel, POD_ITERS),
+        out_shape=jax.ShapeDtypeStruct((8, gram.shape[0]), F32),
+        in_specs=[v, v], out_specs=v,
+        scratch_shapes=[pltpu.VMEM(basis_t.shape, F32)],
+    )(gram, basis_t)
 
 
 def snapshot(hist_ref, first_ref, second_ref, b, c):
@@ -281,7 +333,7 @@
     first = advance(codes, edges, state)
     second = advance(codes, edges, first)
     gram = reduce_all(local_gram(history, first, second))
-    w = weights(elim1, gram, basis_start.T, POD_ITERS)[0]
+    w = weights(gram, basis_start.T)
     return (second[:, None, 0:7], local_filter(history, first, second, w))
 
 

time: 139 us -> 96.7 us (0.70)
  Pallas kernels: 85.8 us -> 43.8 us
    pallas_call x2, Pallas kernels: 42.4 us -> 17.6 us  [sph_step(): pl.pallas_call(step_kernel, out_shape=jax.ShapeDtypeStruct((count, 8, par...]
    pallas_call x1, Pallas kernels: 30.4 us -> 13.2 us  [weights(): pl.pallas_call(functools.partial(weights_kernel, POD_ITERS), out_shape=ja...]
  transfers between devices with their start and end apart: 13 -> 13, of which waited for: 9 -> 9; matrix products, arithmetic and copies ran while one was open for 5% -> 8% of each run, Pallas kernels for 0% -> 0%
where the time goes in v1:
time: 96.7 us; the launch traced here: 96 us
  Pallas kernels  43.8 us (45%)
  waiting for transfers between devices  19.9 us (21%)
  starting transfers between devices  18.9 us (20%)
  local copies, waits for them, and re-layouts  10.4 us (11%)
  other arithmetic  2.3 us (2%)
    pallas_call x2, Pallas kernels, sph_step(): pl.pallas_call(step_kernel, out_shape=jax.ShapeDtypeStruct((count, 8, par...  17.6 us
    ppermute x8, starting transfers between devices, shift(): return lax.ppermute(x, axis, [(i, (i + by) % count) for i in range(count)])  14.5 us
    ppermute x5, waiting for transfers between devices, reduce_all(): x = x + lax.ppermute(x, axis, [(i, i ^ k) for i in range(count)])  14.4 us
    pallas_call x1, Pallas kernels, weights(): pl.pallas_call(functools.partial(weights_kernel, POD_ITERS), out_shape=ja...  13.2 us
    unnamed x7, local copies, waits for them, and re-layouts  7.67 us
    pallas_call x1, Pallas kernels, local_gram(): pl.pallas_call(gram_kernel, grid=(history.shape[0] // group,), out_shape=...  6.77 us
    pallas_call x1, Pallas kernels, local_filter(): pl.pallas_call(filter_kernel, grid=(count // group,), out_shape=jax.Shape...  6.23 us
    ppermute x8, waiting for transfers between devices, shift(): return lax.ppermute(x, axis, [(i, (i + by) % count) for i in range(count)])  5.6 us
  transfers between devices with their start and end apart: 13, of which 9 were waited for; matrix products, arithmetic and copies ran while one was open for 8% of the time, Pallas kernels for 0%

profile of v1, /device:TPU:0, one launch (start us, length us, event | category | flops | bytes accessed | tf_op | source)
XLA Modules:
  0.0 96.0 jit_solution(13139225969432475039)
XLA Ops:
  0.6 0.9 copy.35
  1.6 0.7 multiply_add_fusion
  2.3 3.0 %collective-permute-start = (f32[1,8,128]{2,1,0:T(8,128)S(1)}, f32[1,8,128]{2,1,0:T(8,128)S(1)}, u32[]{:S(2)}, u32[]{:S(2)}) collective-permute-start(f32[1,8,128]{2,1,0:T(8,128)S(1)} %get-tuple-element.8), channel_id=1, source_target_pairs={{0,4},{4,8},{8,12},{12,16},{16,20},{20,24},{24,28},{28,0},{1,5},{5... | collective-permute-start | bytes 12296 | tf_op jit(solution)/shard_map/ppermute | solution.py:300
  5.3 3.1 %collective-permute-start.1 = (f32[1,8,128]{2,1,0:T(8,128)S(1)}, f32[1,8,128]{2,1,0:T(8,128)S(1)}, u32[]{:S(2)}, u32[]{:S(2)}) collective-permute-start(f32[1,8,128]{2,1,0:T(8,128)S(1)} %get-tuple-element.9), channel_id=1, source_target_pairs={{0,28},{4,0},{8,4},{12,8},{16,12},{20,16},{24,20},{28,24},{1,29},{... | collective-permute-start | bytes 12296 | tf_op jit(solution)/shard_map/ppermute | solution.py:300
  8.4 1.5 %collective-permute-done = f32[1,8,128]{2,1,0:T(8,128)S(1)} collective-permute-done((f32[1,8,128]{2,1,0:T(8,128)S(1)}, f32[1,8,128]{2,1,0:T(8,128)S(1)}, u32[]{:S(2)}, u32[]{:S(2)}) %collective-permute-start) | collective-permute-done | bytes 4128 | tf_op jit(solution)/shard_map/ppermute | solution.py:300
  10.0 0.0 collective-permute-done.1
  10.0 0.1 collective-permute-start.2
  10.1 1.7 %collective-permute-start.3 = (f32[34,8,128]{2,1,0:T(8,128)S(1)}, f32[34,8,128]{2,1,0:T(8,128)S(1)}, u32[]{:S(2)}, u32[]{:S(2)}) collective-permute-start(f32[34,8,128]{2,1,0:T(8,128)S(1)} %pad_maximum_fusion.mid_ref), channel_id=1, source_target_pairs={{0,3},{1,0},{2,1},{3,2},{4,7},{5,4},{6,5},{7,6},{8,11},{9,8},{10,9... | collective-permute-start | bytes 417800 | tf_op jit(solution)/shard_map/ppermute | solution.py:300
  11.8 0.8 copy.28.codes_ref
  12.6 0.1 stack.35.edge_ref
  12.7 1.9 %collective-permute-done.2.low_ref = f32[34,8,128]{2,1,0:T(8,128)S(1)} collective-permute-done((f32[34,8,128]{2,1,0:T(8,128)S(1)}, f32[34,8,128]{2,1,0:T(8,128)S(1)}, u32[]{:S(2)}, u32[]{:S(2)}) %collective-permute-start.2) | collective-permute-done | bytes 139296 | tf_op jit(solution)/shard_map/ppermute | solution.py:300
  14.5 0.7 collective-permute-done.3.high_ref
  15.2 8.8 %shard_map.68.first_ref = f32[32,8,128]{2,1,0:T(8,128)S(1)} custom-call(s32[32,4]{1,0:T(8,128)S(1)} %copy.28.codes_ref, s32[8]{0:T(128)S(1)} %stack.35.edge_ref, f32[34,8,128]{2,1,0:T(8,128)S(1)} %pad_maximum_fusion.mid_ref, f32[34,8,128]{2,1,0:T(8,128)S(1)} %collective-permute-done.2.low_ref, f32[34,8,128]{2,1,0:T(8,128)S(1)} %collective-permute-done.3.high_ref), custom_call_target="tpu_custom_call" | custom-call | tf_op jit(solution)/shard_map/pallas_call | solution.py:138
  24.0 0.0 copy-start
  24.0 1.3 %collective-permute-start.4 = (f32[1,8,128]{2,1,0:T(8,128)S(1)}, f32[1,8,128]{2,1,0:T(8,128)S(1)}, u32[]{:S(2)}, u32[]{:S(2)}) collective-permute-start(f32[1,8,128]{2,1,0:T(8,128)S(1)} %get-tuple-element.10), channel_id=1, source_target_pairs={{0,4},{4,8},{8,12},{12,16},{16,20},{20,24},{24,28},{28,0},{1,5},{5... | collective-permute-start | bytes 12296 | tf_op jit(solution)/shard_map/ppermute | solution.py:300
  25.3 3.6 %collective-permute-start.5 = (f32[1,8,128]{2,1,0:T(8,128)S(1)}, f32[1,8,128]{2,1,0:T(8,128)S(1)}, u32[]{:S(2)}, u32[]{:S(2)}) collective-permute-start(f32[1,8,128]{2,1,0:T(8,128)S(1)} %get-tuple-element.11), channel_id=1, source_target_pairs={{0,28},{4,0},{8,4},{12,8},{16,12},{20,16},{24,20},{28,24},{1,29},{... | collective-permute-start | bytes 12296 | tf_op jit(solution)/shard_map/ppermute | solution.py:300
  28.9 1.5 %collective-permute-done.4 = f32[1,8,128]{2,1,0:T(8,128)S(1)} collective-permute-done((f32[1,8,128]{2,1,0:T(8,128)S(1)}, f32[1,8,128]{2,1,0:T(8,128)S(1)}, u32[]{:S(2)}, u32[]{:S(2)}) %collective-permute-start.4) | collective-permute-done | bytes 4128 | tf_op jit(solution)/shard_map/ppermute | solution.py:300
  30.4 0.0 collective-permute-done.5
  30.4 0.3 collective-permute-start.6
  30.7 1.5 %collective-permute-start.7 = (f32[34,8,128]{2,1,0:T(8,128)S(1)}, f32[34,8,128]{2,1,0:T(8,128)S(1)}, u32[]{:S(2)}, u32[]{:S(2)}) collective-permute-start(f32[34,8,128]{2,1,0:T(8,128)S(1)} %pad_maximum_fusion.1.mid_ref), channel_id=1, source_target_pairs={{0,3},{1,0},{2,1},{3,2},{4,7},{5,4},{6,5},{7,6},{8,11},{9,8},{10,9... | collective-permute-start | bytes 417800 | tf_op jit(solution)/shard_map/ppermute | solution.py:300
  32.2 4.7 %copy.30.hist_ref = bf16[32,1,3,126,128]{4,3,2,1,0:T(8,128)(2,1)} copy(bf16[32,1,3,126,128]{4,0,3,2,1:T(8,128)(2,1)} %param.8) | data formatting | bytes 6193152 | tf_op args[3]
  36.9 0.0 copy-done
  36.9 0.0 collective-permute-done.6.low_ref
  36.9 0.0 collective-permute-done.7.high_ref
  36.9 8.8 %shard_map.69.second_ref = f32[32,8,128]{2,1,0:T(8,128)S(1)} custom-call(s32[32,4]{1,0:T(8,128)S(1)} %copy.28.codes_ref, s32[8]{0:T(128)S(1)} %stack.35.edge_ref, f32[34,8,128]{2,1,0:T(8,128)S(1)} %pad_maximum_fusion.1.mid_ref, f32[34,8,128]{2,1,0:T(8,128)S(1)} %collective-permute-done.6.low_ref, f32[34,8,128]{2,1,0:T(8,128)S(1)} %collective-permute-done.7.high_ref), custom_call_target="tpu_custom_call" | custom-call | tf_op jit(solution)/shard_map/pallas_call | solution.py:138
  45.7 0.0 copy-start.1
  45.7 0.7 copy-done.1
  46.4 6.8 %shard_map.70 = f32[128,128]{1,0:T(8,128)} custom-call(bf16[32,1,3,126,128]{4,3,2,1,0:T(8,128)(2,1)} %copy.30.hist_ref, f32[32,8,128]{2,1,0:T(8,128)} %copy-done, f32[32,8,128]{2,1,0:T(8,128)} %copy-done.1), custom_call_target="tpu_custom_call" | custom-call | tf_op jit(solution)/shard_map/pallas_call | solution.py:279
  53.2 0.2 collective-permute-start.8
  53.4 1.2 %collective-permute-done.8 = f32[128,128]{1,0:T(8,128)S(1)} collective-permute-done((f32[128,128]{1,0:T(8,128)}, f32[128,128]{1,0:T(8,128)S(1)}, u32[]{:S(2)}, u32[]{:S(2)}) %collective-permute-start.8) | collective-permute-done | bytes 65568 | tf_op jit(solution)/shard_map/ppermute | solution.py:311
  54.6 0.9 add.23
  55.5 1.9 %collective-permute-start.9 = (f32[128,128]{1,0:T(8,128)S(1)}, f32[128,128]{1,0:T(8,128)S(1)}, u32[]{:S(2)}, u32[]{:S(2)}) collective-permute-start(f32[128,128]{1,0:T(8,128)S(1)} %add.23), channel_id=1, source_target_pairs={{0,2},{1,3},{2,0},{3,1},{4,6},{5,7},{6,4},{7,5},{8,10},{9,11},{10,... | collective-permute-start | bytes 196616 | tf_op jit(solution)/shard_map/ppermute | solution.py:311
  57.4 2.4 %collective-permute-done.9 = f32[128,128]{1,0:T(8,128)S(1)} collective-permute-done((f32[128,128]{1,0:T(8,128)S(1)}, f32[128,128]{1,0:T(8,128)S(1)}, u32[]{:S(2)}, u32[]{:S(2)}) %collective-permute-start.9) | collective-permute-done | bytes 65568 | tf_op jit(solution)/shard_map/ppermute | solution.py:311
  59.8 0.1 collective-permute-start.10
  59.9 4.2 %collective-permute-done.10 = f32[128,128]{1,0:T(8,128)S(1)} collective-permute-done((f32[128,128]{1,0:T(8,128)S(1)}, f32[128,128]{1,0:T(8,128)S(1)}, u32[]{:S(2)}, u32[]{:S(2)}) %collective-permute-start.10) | collective-permute-done | bytes 65568 | tf_op jit(solution)/shard_map/ppermute | solution.py:311
  64.2 0.2 collective-permute-start.11
  64.3 4.2 %collective-permute-done.11 = f32[128,128]{1,0:T(8,128)S(1)} collective-permute-done((f32[128,128]{1,0:T(8,128)S(1)}, f32[128,128]{1,0:T(8,128)S(1)}, u32[]{:S(2)}, u32[]{:S(2)}) %collective-permute-start.11) | collective-permute-done | bytes 65568 | tf_op jit(solution)/shard_map/ppermute | solution.py:311
  68.5 2.0 %collective-permute-start.12 = (f32[128,128]{1,0:T(8,128)S(1)}, f32[128,128]{1,0:T(8,128)S(1)}, u32[]{:S(2)}, u32[]{:S(2)}) collective-permute-start(f32[128,128]{1,0:T(8,128)S(1)} %add.26), channel_id=1, source_target_pairs={{0,16},{4,20},{8,24},{12,28},{16,0},{20,4},{24,8},{28,12},{1,17},{... | collective-permute-start | bytes 196616 | tf_op jit(solution)/shard_map/ppermute | solution.py:311
  70.5 0.9 slice_bitcast_fusion
  71.4 0.8 copy.31
  72.2 2.3 %collective-permute-done.12 = f32[128,128]{1,0:T(8,128)S(1)} collective-permute-done((f32[128,128]{1,0:T(8,128)S(1)}, f32[128,128]{1,0:T(8,128)S(1)}, u32[]{:S(2)}, u32[]{:S(2)}) %collective-permute-start.12) | collective-permute-done | bytes 65568 | tf_op jit(solution)/shard_map/ppermute | solution.py:311
  74.4 0.6 add.27.g_ref
  75.1 13.2 %shard_map.71.w_ref = f32[8,128]{1,0:T(8,128)} custom-call(f32[128,128]{1,0:T(8,128)} %add.27.g_ref, f32[64,128]{1,0:T(8,128)} %bitcast.22), custom_call_target="tpu_custom_call" | custom-call | tf_op jit(solution)/shard_map/pallas_call | solution.py:232
  88.3 6.2 %shard_map.72 = f32[32,1,3,128]{3,2,1,0:T(4,128)} custom-call(bf16[32,1,3,126,128]{4,3,2,1,0:T(8,128)(2,1)} %copy.30.hist_ref, f32[32,8,128]{2,1,0:T(8,128)} %copy-done, f32[32,8,128]{2,1,0:T(8,128)} %copy-done.1, f32[8,128]{1,0:T(8,128)} %shard_map.71.w_ref), custom_call_target="tpu_custom_call" | custom-call | tf_op jit(solution)/shard_map/pallas_call | solution.py:290
  94.5 1.5 %copy.32 = f32[32,1,3,128]{3,1,2,0:T(1,128)} copy(f32[32,1,3,128]{3,2,1,0:T(4,128)} %shard_map.72) | data formatting | bytes 98304
  (10 shorter events, 0.1 us)
Async XLA Ops:
  2.3 7.6 %collective-permute-start = (f32[1,8,128]{2,1,0:T(8,128)S(1)}, f32[1,8,128]{2,1,0:T(8,128)S(1)}, u32[]{:S(2)}, u32[]{:S(2)}) collective-permute-start(f32[1,8,128]{2,1,0:T(8,128)S(1)} %get-tuple-element.8), channel_id=1, source_target_pairs={{0,4},{4,8},{8,12},{12,16},{16,20},{20,24},{24,28},{28,0},{1,5},{5... | collective-permute-start | bytes 12296 | tf_op jit(solution)/shard_map/ppermute | solution.py:300
  5.3 4.6 %collective-permute-start.1 = (f32[1,8,128]{2,1,0:T(8,128)S(1)}, f32[1,8,128]{2,1,0:T(8,128)S(1)}, u32[]{:S(2)}, u32[]{:S(2)}) collective-permute-start(f32[1,8,128]{2,1,0:T(8,128)S(1)} %get-tuple-element.9), channel_id=1, source_target_pairs={{0,28},{4,0},{8,4},{12,8},{16,12},{20,16},{24,20},{28,24},{1,29},{... | collective-permute-start | bytes 12296 | tf_op jit(solution)/shard_map/ppermute | solution.py:300
  10.0 4.5 %collective-permute-start.2 = (f32[34,8,128]{2,1,0:T(8,128)S(1)}, f32[34,8,128]{2,1,0:T(8,128)S(1)}, u32[]{:S(2)}, u32[]{:S(2)}) collective-permute-start(f32[34,8,128]{2,1,0:T(8,128)S(1)} %pad_maximum_fusion.mid_ref), channel_id=1, source_target_pairs={{0,1},{1,2},{2,3},{3,0},{4,5},{5,6},{6,7},{7,4},{8,9},{9,10},{10,1... | collective-permute-start | bytes 417800 | tf_op jit(solution)/shard_map/ppermute | solution.py:300
  10.1 5.1 %collective-permute-start.3 = (f32[34,8,128]{2,1,0:T(8,128)S(1)}, f32[34,8,128]{2,1,0:T(8,128)S(1)}, u32[]{:S(2)}, u32[]{:S(2)}) collective-permute-start(f32[34,8,128]{2,1,0:T(8,128)S(1)} %pad_maximum_fusion.mid_ref), channel_id=1, source_target_pairs={{0,3},{1,0},{2,1},{3,2},{4,7},{5,4},{6,5},{7,6},{8,11},{9,8},{10,9... | collective-permute-start | bytes 417800 | tf_op jit(solution)/shard_map/ppermute | solution.py:300
  24.0 12.9 %copy-start = (f32[32,8,128]{2,1,0:T(8,128)}, f32[32,8,128]{2,1,0:T(8,128)S(1)}, u32[]{:S(2)}) copy-start(f32[32,8,128]{2,1,0:T(8,128)S(1)} %shard_map.68.first_ref) | copy-start | bytes 393220
  24.0 6.4 %collective-permute-start.4 = (f32[1,8,128]{2,1,0:T(8,128)S(1)}, f32[1,8,128]{2,1,0:T(8,128)S(1)}, u32[]{:S(2)}, u32[]{:S(2)}) collective-permute-start(f32[1,8,128]{2,1,0:T(8,128)S(1)} %get-tuple-element.10), channel_id=1, source_target_pairs={{0,4},{4,8},{8,12},{12,16},{16,20},{20,24},{24,28},{28,0},{1,5},{5... | collective-permute-start | bytes 12296 | tf_op jit(solution)/shard_map/ppermute | solution.py:300
  25.3 5.1 %collective-permute-start.5 = (f32[1,8,128]{2,1,0:T(8,128)S(1)}, f32[1,8,128]{2,1,0:T(8,128)S(1)}, u32[]{:S(2)}, u32[]{:S(2)}) collective-permute-start(f32[1,8,128]{2,1,0:T(8,128)S(1)} %get-tuple-element.11), channel_id=1, source_target_pairs={{0,28},{4,0},{8,4},{12,8},{16,12},{20,16},{24,20},{28,24},{1,29},{... | collective-permute-start | bytes 12296 | tf_op jit(solution)/shard_map/ppermute | solution.py:300
  30.4 6.5 %collective-permute-start.6 = (f32[34,8,128]{2,1,0:T(8,128)S(1)}, f32[34,8,128]{2,1,0:T(8,128)S(1)}, u32[]{:S(2)}, u32[]{:S(2)}) collective-permute-start(f32[34,8,128]{2,1,0:T(8,128)S(1)} %pad_maximum_fusion.1.mid_ref), channel_id=1, source_target_pairs={{0,1},{1,2},{2,3},{3,0},{4,5},{5,6},{6,7},{7,4},{8,9},{9,10},{10,1... | collective-permute-start | bytes 417800 | tf_op jit(solution)/shard_map/ppermute | solution.py:300
  30.7 6.3 %collective-permute-start.7 = (f32[34,8,128]{2,1,0:T(8,128)S(1)}, f32[34,8,128]{2,1,0:T(8,128)S(1)}, u32[]{:S(2)}, u32[]{:S(2)}) collective-permute-start(f32[34,8,128]{2,1,0:T(8,128)S(1)} %pad_maximum_fusion.1.mid_ref), channel_id=1, source_target_pairs={{0,3},{1,0},{2,1},{3,2},{4,7},{5,4},{6,5},{7,6},{8,11},{9,8},{10,9... | collective-permute-start | bytes 417800 | tf_op jit(solution)/shard_map/ppermute | solution.py:300
  45.7 0.7 copy-start.1
  53.2 1.5 %collective-permute-start.8 = (f32[128,128]{1,0:T(8,128)}, f32[128,128]{1,0:T(8,128)S(1)}, u32[]{:S(2)}, u32[]{:S(2)}) collective-permute-start(f32[128,128]{1,0:T(8,128)} %shard_map.70), channel_id=1, source_target_pairs={{0,1},{1,0},{2,3},{3,2},{4,5},{5,4},{6,7},{7,6},{8,9},{9,8},{10,11... | collective-permute-start | bytes 196616 | tf_op jit(solution)/shard_map/ppermute | solution.py:311
  55.5 4.3 %collective-permute-start.9 = (f32[128,128]{1,0:T(8,128)S(1)}, f32[128,128]{1,0:T(8,128)S(1)}, u32[]{:S(2)}, u32[]{:S(2)}) collective-permute-start(f32[128,128]{1,0:T(8,128)S(1)} %add.23), channel_id=1, source_target_pairs={{0,2},{1,3},{2,0},{3,1},{4,6},{5,7},{6,4},{7,5},{8,10},{9,11},{10,... | collective-permute-start | bytes 196616 | tf_op jit(solution)/shard_map/ppermute | solution.py:311
  59.8 4.3 %collective-permute-start.10 = (f32[128,128]{1,0:T(8,128)S(1)}, f32[128,128]{1,0:T(8,128)S(1)}, u32[]{:S(2)}, u32[]{:S(2)}) collective-permute-start(f32[128,128]{1,0:T(8,128)S(1)} %add.24), channel_id=1, source_target_pairs={{0,4},{4,0},{8,12},{12,8},{16,20},{20,16},{24,28},{28,24},{1,5},{5... | collective-permute-start | bytes 196616 | tf_op jit(solution)/shard_map/ppermute | solution.py:311
  64.2 4.3 %collective-permute-start.11 = (f32[128,128]{1,0:T(8,128)S(1)}, f32[128,128]{1,0:T(8,128)S(1)}, u32[]{:S(2)}, u32[]{:S(2)}) collective-permute-start(f32[128,128]{1,0:T(8,128)S(1)} %add.25), channel_id=1, source_target_pairs={{0,8},{4,12},{8,0},{12,4},{16,24},{20,28},{24,16},{28,20},{1,9},{5... | collective-permute-start | bytes 196616 | tf_op jit(solution)/shard_map/ppermute | solution.py:311
  68.5 5.9 %collective-permute-start.12 = (f32[128,128]{1,0:T(8,128)S(1)}, f32[128,128]{1,0:T(8,128)S(1)}, u32[]{:S(2)}, u32[]{:S(2)}) collective-permute-start(f32[128,128]{1,0:T(8,128)S(1)} %add.26), channel_id=1, source_target_pairs={{0,16},{4,20},{8,24},{12,28},{16,0},{20,4},{24,8},{28,12},{1,17},{... | collective-permute-start | bytes 196616 | tf_op jit(solution)/shard_map/ppermute | solution.py:311

commit v2 on v1

v2 whole, which is shorter than its diff:
```python
import functools
import math

import jax
import jax.numpy as jnp
from jax import lax
from jax.experimental import pallas as pl
from jax.experimental.pallas import tpu as pltpu
from jax.sharding import PartitionSpec as P

POD_ITERS = 4
SEDIMENT_EXTRA = 1.65


ALPHA_KERNEL = 21.0 / (16.0 * math.pi)
VOLUME = 1.0 / 16.0
STIFFNESS = 100.0 / 7.0
TIME_STEP = 0.02
GRAVITY = 1.0
F32, BF16 = jnp.float32, jnp.bfloat16

def pieces(x):
    a = x.astype(BF16).astype(F32)
    r = x - a
    b = r.astype(BF16).astype(F32)
    return a, b, r - b

def rows(*parts):
    return jnp.concatenate(parts, axis=0)

def row_is(*which):
    index = lax.broadcasted_iota(jnp.int32, (8, 128), 0)
    hit = index == which[0]
    for w in which[1:]:
        hit = hit | (index == w)
    return hit

def spread(row):
    return jnp.broadcast_to(row, (8, row.shape[1]))

def features(state):
    centred = jnp.where(row_is(0, 1, 2), state - 1.0, state)
    r, rho = spread(state[6:7]), spread(state[7:8])
    live = rho > 0.0
    mass = rho * VOLUME
    r2 = r * r
    pressure = jnp.where(live, STIFFNESS * (r2 * r2 * r2 * r - 1.0) / (jnp.where(live, rho, 1.0) * r2), 0.0)
    mp = mass * pressure
    place = jnp.where(row_is(0, 1, 2), centred, 0.0)
    norm = 0.25 * jnp.sum(place * place, axis=0, keepdims=True)
    speed = jnp.where(row_is(0, 1, 2), pltpu.roll(centred, 5, 0), 0.0)
    flux = jnp.sum(place * speed, axis=0, keepdims=True)
    own = jnp.where(row_is(3), norm, jnp.where(row_is(4), 1.0, place))
    near = jnp.where(row_is(3), 1.0, jnp.where(row_is(4), norm, -0.5 * place))
    moved = jnp.where(row_is(0), 1.0, jnp.where(row_is(7), flux, pltpu.roll(centred, 1, 0)))
    sums_a = mass * moved
    sums_b = jnp.where(row_is(0, 1, 2, 3), mp * moved, 0.0)
    near_x = jnp.where(row_is(0), -0.5, jnp.where(row_is(4), 0.5 * centred[0:1], 0.0))
    near_z = jnp.where(row_is(2), -0.5, jnp.where(row_is(4), 0.5 * centred[2:3], 0.0))
    sums_ax = mass * jnp.where(row_is(1), 1.0, jnp.where(row_is(7), centred[3:4], 0.0))
    sums_az = mass * jnp.where(row_is(3), 1.0, jnp.where(row_is(7), centred[5:6], 0.0))
    sums_bx = jnp.where(row_is(1), mp, 0.0)
    sums_bz = jnp.where(row_is(3), mp, 0.0)
    return own, rows(near, sums_a, sums_b), rows(near_x, sums_ax, sums_bx), rows(near_z, sums_az, sums_bz), pressure[0:1]

def prep_kernel(particles_ref, flags_ref, codes_ref, state_ref, lo_ref, hi_ref, flat):
    count = flags_ref.shape[0]
    fields = particles_ref.shape[0] // count
    for i in range(fields):
        flat[pl.ds(i, count, stride=8), :] = particles_ref[pl.ds(i, count, stride=fields), :]
    flat[pl.ds(fields, count, stride=8), :] = 1.0 + SEDIMENT_EXTRA * flags_ref[...].astype(F32)
    for b in range(count):
        state_ref[b] = flat[8 * b:8 * b + 8]
    for ref, first, edge in ((lo_ref, 0, 0), (hi_ref, count - 2, count - 1)):
        for i in range(2):
            ref[i] = flat[8 * (first + i):8 * (first + i) + 8]
        ref[2] = jnp.zeros_like(ref[2])
        ref[2, 0:codes_ref.shape[0], 0:1] = codes_ref[:, edge:edge + 1].astype(F32)


def prepare(particles, flags, codes):
    count, fields, part = particles.shape
    v = pl.BlockSpec(memory_space=pltpu.VMEM)
    rim = jax.ShapeDtypeStruct((3, 8, part), F32)
    return pl.pallas_call(
        prep_kernel,
        out_shape=(jax.ShapeDtypeStruct((count, 8, part), F32), rim, rim),
        in_specs=[v, v, v], out_specs=(v, v, v),
        scratch_shapes=[pltpu.VMEM((count * 8, part), F32)],
    )(particles.reshape(count * fields, part), flags, codes)


def step_blocks(codes_ref, edge_ref, low_ref, mid_ref, high_ref, out_ref, b0, b1, b2):
    ext = mid_ref.shape[0]
    count = ext - 2
    sel = lax.broadcasted_iota(jnp.int32, (8, 1), 0) == 7
    rim = edge_ref[5]
    for col, ref in ((0, low_ref), (1, mid_ref), (2, high_ref)):
        def prep(i, _):
            st = ref[i]
            rowon = jnp.where(i < rim, edge_ref[3], jnp.where(i >= ext - rim, edge_ref[4], 1))
            keep = (edge_ref[col] * rowon).astype(F32)
            _, a, b, c, _ = features(jnp.where(sel, st * keep, st))
            b0[col * ext + i] = a
            b1[col * ext + i] = b
            b2[col * ext + i] = c
            return 0
        lax.fori_loop(0, ext, prep, 0, unroll=2 if ext % 2 == 0 else 1)
    normrow = (lax.broadcasted_iota(jnp.int32, (24, 1), 0) == 4).astype(F32)
    skip = edge_ref[6]

    def block(b, _):
        st = mid_ref[b + 1]
        own, g_self, _, _, pressure = features(st)
        o1, o2, o3 = pieces(own)
        rhs = rows(o1, o1, o2, o2, o1, o3).astype(BF16)
        ns, fs = [], []
        for n in range(codes_ref.shape[0] + 1):
            if n == 0:
                g = g_self
            else:
                c = codes_ref[n - 1, b + skip]
                o = c + jnp.where(c >= 4, 1, 0)
                ds1 = (o * 11) >> 5
                dv1 = o - 3 * ds1
                idx = dv1 * ext + b + ds1
                tx = 2.0 * (ds1 - 1).astype(F32)
                tz = 2.0 * (dv1 - 1).astype(F32)
                g = b0[idx] + tx * b1[idx] + tz * b2[idx] + normrow * (0.25 * (tx * tx + tz * tz))
            p1, p2, p3 = pieces(g[0:8])
            f1, f2, f3 = pieces(g[8:24])
            ns.append(rows(p1, p2, p1, p2, p3, p1).astype(BF16))
            fs.append(rows(f1, f2, f3).astype(BF16))
        nall = jnp.concatenate(ns, axis=1)
        f = jnp.concatenate(fs + fs, axis=1)
        s = lax.dot_general(nall, rhs, (((0,), (0,)), ((), ())), preferred_element_type=F32)
        s = jnp.maximum(s, 1e-20)
        k = jnp.maximum(1.0 - s * lax.rsqrt(s), 0.0)
        wgt = k * k * k
        wh = wgt.astype(BF16)
        wl = (wgt - wh.astype(F32)).astype(BF16)
        acc = jnp.dot(f, jnp.concatenate([wh, wl], 0), preferred_element_type=F32)
        t = acc[0:16] + acc[16:32] + acc[32:48]
        x, vel = st[0:3] - 1.0, st[3:6]
        coef = -5.0 * ALPHA_KERNEL
        sw, swx, swv, swf = t[0:1], t[1:4], t[4:7], t[7:8]
        swp, swpx = t[8:9], t[9:12]
        dens = coef * (jnp.sum(vel * (x * sw - swx) - x * swv, axis=0, keepdims=True) + swf)
        acc3 = -coef * (pressure * (x * sw - swx) + x * swp - swpx)
        grav = jnp.where(lax.broadcasted_iota(jnp.int32, (3, 1), 0) == 2, -GRAVITY, 0.0)
        vel2 = vel + TIME_STEP * (acc3 + grav)
        pos2 = st[0:3] + TIME_STEP * vel2
        rho = st[7:8]
        r2 = st[6:7] + TIME_STEP * dens / rho
        out_ref[b] = rows(pos2, vel2, r2, rho)
        return 0
    unroll = max(u for u in range(1, 18) if count % u == 0)
    lax.fori_loop(0, count, block, 0, unroll=unroll)


def step_scratch(ext, part):
    return [pltpu.VMEM((3 * ext, 24, part), F32)] * 3


def first_step(codes, edges, low, mid, high, basis):
    ext, _, part = mid.shape
    v = pl.BlockSpec(memory_space=pltpu.VMEM)
    sm = pl.BlockSpec(memory_space=pltpu.SMEM)
    def kernel(codes_ref, edge_ref, low_ref, mid_ref, high_ref, basis_any, out_ref, *scratch):
        step_blocks(codes_ref, edge_ref, low_ref, mid_ref, high_ref, out_ref, *scratch)

    return pl.pallas_call(
        kernel, out_shape=jax.ShapeDtypeStruct((ext - 2, 8, part), F32),
        in_specs=[sm, sm, v, v, v, pl.BlockSpec(memory_space=pl.ANY)], out_specs=v,
        scratch_shapes=step_scratch(ext, part),
        compiler_params=pltpu.CompilerParams(vmem_limit_bytes=48 << 20),
    )(codes, edges, low, mid, high, basis)


def cross_row(hist_ref, new, others, terms):
    comps, hist = hist_ref.shape[0], hist_ref.shape[1]
    groups = new[0].shape[0] // 8

    def fold(x):
        total = x[0:8]
        for g in range(1, groups):
            total = total + x[8 * g:8 * g + 8]
        return total

    def one(s, _):
        total = hist_ref[0, s].astype(F32) * new[0]
        for c in range(1, comps):
            total = total + hist_ref[c, s].astype(F32) * new[c]
        terms[pl.ds(pl.multiple_of(8 * s, 8), 8), :] = fold(total)
        return 0
    lax.fori_loop(0, hist, one, 0, unroll=max(u for u in range(1, 10) if hist % u == 0))
    snaps = terms.shape[0] // 8
    for k in range(snaps - hist):
        if k < len(others):
            total = others[k][0] * new[0]
            for c in range(1, comps):
                total = total + others[k][c] * new[c]
            terms[8 * (hist + k):8 * (hist + k) + 8] = fold(total)
        else:
            terms[8 * (hist + k):8 * (hist + k) + 8] = jnp.zeros_like(terms[0:8])
    by_snap = terms[pl.ds(0, snaps, stride=8), :]
    for i in range(1, 8):
        by_snap = by_snap + terms[pl.ds(i, snaps, stride=8), :]
    ones = jnp.ones((8, by_snap.shape[1]), F32)
    return lax.dot_general(ones, by_snap, (((1,), (1,)), ((), ())), precision=HIGHEST, preferred_element_type=F32)[0:1]


def load_new(ref, skip, count, flat):
    def move(b, _):
        flat[pl.ds(pl.multiple_of(8 * b, 8), 8), :] = ref[b + skip]
        return 0
    lax.fori_loop(0, count, move, 0, unroll=math.gcd(count, 8))
    return [flat[pl.ds(3 + c, count, stride=8), :].astype(BF16).astype(F32) for c in range(3)]


def second_step(codes, edges, low, mid, high, hist, gram):
    ext, _, part = mid.shape
    count = ext - 2
    snaps = gram.shape[0]
    v = pl.BlockSpec(memory_space=pltpu.VMEM)
    sm = pl.BlockSpec(memory_space=pltpu.SMEM)

    def kernel(codes_ref, edge_ref, low_ref, mid_ref, high_ref, hist_any, gram_ref, new_ref, state_ref, gram_out,
               b0, b1, b2, hist_ref, flat, terms, sem):
        copy = pltpu.make_async_copy(hist_any, hist_ref, sem)
        copy.start()
        step_blocks(codes_ref, edge_ref, low_ref, mid_ref, high_ref, state_ref, b0, b1, b2)
        copy.wait()
        first = load_new(mid_ref, 1, count, flat)
        second = load_new(state_ref, 0, count, flat)
        for i in range(7):
            new_ref[pl.ds(i, count, stride=7), :] = flat[pl.ds(i, count, stride=8), :]
        row = cross_row(hist_ref, second, (first, second), terms)
        last = lax.broadcasted_iota(jnp.int32, (snaps, 1), 0) == snaps - 1
        gram_out[...] = jnp.where(last, row, gram_ref[...])

    return pl.pallas_call(
        kernel,
        out_shape=(jax.ShapeDtypeStruct((count * 7, part), F32), jax.ShapeDtypeStruct((count, 8, part), F32),
                   jax.ShapeDtypeStruct((snaps, snaps), F32)),
        in_specs=[sm, sm, v, v, v, pl.BlockSpec(memory_space=pl.ANY), v], out_specs=(v, v, v),
        scratch_shapes=step_scratch(ext, part) + [
            pltpu.VMEM(hist.shape, BF16), pltpu.VMEM((count * 8, part), F32), pltpu.VMEM((snaps * 8, part), F32),
            pltpu.SemaphoreType.DMA],
        compiler_params=pltpu.CompilerParams(vmem_limit_bytes=48 << 20),
    )(codes, edges, low, mid, high, hist, gram)


def early_gram(hist, first):
    comps, snaps_old, count, part = hist.shape
    snaps = snaps_old + 2
    v = pl.BlockSpec(memory_space=pltpu.VMEM)

    def kernel(hist_any, first_ref, out_ref, hist_ref, wide, flat, terms, sems):
        copies = [pltpu.make_async_copy(hist_any.at[c], hist_ref.at[c], sems.at[c]) for c in range(comps)]
        for copy in copies:
            copy.start()
        total = jnp.zeros((snaps_old, snaps_old), F32)
        for c in range(comps):
            copies[c].wait()

            def expand(s, _):
                wide[pl.ds(pl.multiple_of(count * s, 8), count), :] = hist_ref[c, s].astype(F32)
                return 0
            lax.fori_loop(0, snaps_old, expand, 0, unroll=max(u for u in range(1, 10) if snaps_old % u == 0))
            for b in range(0, count, 8):
                x = jnp.concatenate([wide[pl.ds(b + j, snaps_old, stride=count), :].astype(BF16) for j in range(8)], axis=1)
                total = total + lax.dot_general(x, x, (((1,), (1,)), ((), ())), preferred_element_type=F32)
        out_ref[...] = jnp.zeros_like(out_ref)
        out_ref[0:snaps_old, 0:snaps_old] = total
        new = load_new(first_ref, 1, count, flat)
        out_ref[snaps_old:snaps_old + 1] = cross_row(hist_ref, new, (new,), terms)

    return pl.pallas_call(
        kernel, out_shape=jax.ShapeDtypeStruct((snaps, snaps), F32),
        in_specs=[pl.BlockSpec(memory_space=pl.ANY), v], out_specs=v,
        scratch_shapes=[pltpu.VMEM(hist.shape, BF16), pltpu.VMEM((snaps_old * count, part), F32), pltpu.VMEM((count * 8, part), F32),
                        pltpu.VMEM((snaps * 8, part), F32), pltpu.SemaphoreType.DMA((comps,))],
        compiler_params=pltpu.CompilerParams(vmem_limit_bytes=48 << 20),
        cost_estimate=pl.CostEstimate(flops=2 * comps * snaps * snaps * count * part, bytes_accessed=2 * comps * snaps * count * part, transcendentals=0),
    )(hist, first)


HIGHEST = lax.Precision.HIGHEST
REPEAT_BELOW = 1e-5


def gram_of(m):
    return lax.dot_general(m, m, (((1,), (1,)), ((), ())), precision=HIGHEST, preferred_element_type=F32)


def orthonormal(m):
    n, wide = m.shape
    nb = n // 8
    s = gram_of(m)
    s = jnp.concatenate([s, jnp.zeros((n, wide - n), F32)], axis=1)
    sb = [s[8 * k:8 * k + 8] for k in range(nb)]
    mb = [m[8 * k:8 * k + 8] for k in range(nb)]
    sub = lax.broadcasted_iota(jnp.int32, (8, wide), 0)
    full = lambda x: jnp.broadcast_to(x, (8, wide))
    worst = None
    for k in range(nb):
        p = 8 * k
        norm0 = jnp.sum(m[8 * k:8 * k + 8] * m[8 * k:8 * k + 8], axis=1, keepdims=True)
        rs = [full(sb[k][i:i + 1]) for i in range(8)]
        rm = [full(mb[k][i:i + 1]) for i in range(8)]
        e = [[full(rs[i][:, p + j:p + j + 1]) for j in range(i + 1)] for i in range(8)]
        cols = [[full(sb[t][:, p + j:p + j + 1]) for j in range(8)] for t in range(k + 1, nb)]
        inv, low = [], [[None] * 8 for _ in range(8)]
        for j in range(8):
            inv.append(1.0 / e[j][j])
            for i in range(j + 1, 8):
                for t in range(j + 1, i + 1):
                    e[i][t] = e[i][t] - (e[i][j] * e[t][j]) * inv[j]
            for i in range(j + 1, 8):
                low[i][j] = e[i][j] * inv[j]
            for i in range(j + 1, 8):
                rs[i] = rs[i] - low[i][j] * rs[j]
                rm[i] = rm[i] - low[i][j] * rm[j]
        d = e[0][0]
        out = rm[0]
        for i in range(1, 8):
            d = jnp.where(sub == i, e[i][i], d)
            out = jnp.where(sub == i, rm[i], out)
        mb[k] = out * lax.rsqrt(d)
        ratio = d / norm0
        worst = ratio if worst is None else jnp.minimum(worst, ratio)
        if k == nb - 1:
            break
        us = [rs[j] * inv[j] for j in range(8)]
        um = [rm[j] * inv[j] for j in range(8)]
        for t in range(k + 1, nb):
            c = cols[t - k - 1]
            for j in range(8):
                for i in range(j + 1, 8):
                    c[i] = c[i] - low[i][j] * c[j]
                sb[t] = sb[t] - c[j] * us[j]
                mb[t] = mb[t] - c[j] * um[j]
    return jnp.concatenate(mb, 0), jnp.min(worst)


def repeated(m, q_ref):
    q, worst = orthonormal(m)
    q_ref[...] = q

    @pl.when(jnp.logical_not(worst >= REPEAT_BELOW))
    def _():
        q_ref[...] = orthonormal(q_ref[...])[0]


def start_basis(basis_t):
    v = pl.BlockSpec(memory_space=pltpu.VMEM)

    def kernel(b_ref, q_ref):
        repeated(b_ref[...], q_ref)

    return pl.pallas_call(
        kernel, out_shape=jax.ShapeDtypeStruct(basis_t.shape, F32), in_specs=[v], out_specs=v,
        cost_estimate=pl.CostEstimate(flops=1 << 30, bytes_accessed=1 << 20, transcendentals=0),
    )(basis_t)


def weigh(iters, g_ref, b_ref, q_ref):
    snaps = g_ref.shape[0]
    rows_in = lax.broadcasted_iota(jnp.int32, (snaps, snaps), 0)
    cols_in = lax.broadcasted_iota(jnp.int32, (snaps, snaps), 1)
    g = g_ref[...]
    low = (rows_in >= snaps - 2) & (cols_in < rows_in)
    g = jnp.where(low | (rows_in == cols_in) | ((rows_in < snaps - 2) & (cols_in < snaps - 2)), g, 0.0)
    g_ref[...] = g + jnp.where(low, g, 0.0).T
    q_ref[...] = b_ref[...]

    def iterate(i, _):
        repeated(jnp.dot(q_ref[...], g_ref[...], precision=HIGHEST, preferred_element_type=F32), q_ref)
        return 0

    lax.fori_loop(0, iters, iterate, 0)
    q = q_ref[...]
    last = (lax.broadcasted_iota(jnp.int32, (1, snaps), 1) == snaps - 1).astype(F32)
    w = jnp.zeros((1, snaps), F32)
    for _ in range(3):
        y = jnp.sum(q * (last - w), axis=1, keepdims=True)
        w = w + jnp.sum(q * y, axis=0, keepdims=True)
    return w


def filtered_field(gram, basis_t, hist, first, second):
    comps, snaps_old, count, part = hist.shape
    v = pl.BlockSpec(memory_space=pltpu.VMEM)

    def kernel(gram_ref, b_ref, hist_any, first_ref, second_ref, out_ref, g_ref, q_ref, hist_ref, flat, table, sem):
        copy = pltpu.make_async_copy(hist_any, hist_ref, sem)
        copy.start()
        g_ref[...] = gram_ref[...]
        w = weigh(POD_ITERS, g_ref, b_ref, q_ref)
        table[...] = jnp.broadcast_to(w, table.shape).T
        copy.wait()
        start = []
        for k, (ref, skip) in enumerate(((first_ref, 1), (second_ref, 0))):
            wk = table[snaps_old + k:snaps_old + k + 1]
            new = [wk * x for x in load_new(ref, skip, count, flat)]
            start = [x + y for x, y in zip(start, new)] if start else new

        def one(s, total):
            wk = table[pl.ds(s, 1), :]
            return [total[c] + wk * hist_ref[c, s].astype(F32) for c in range(comps)]
        total = lax.fori_loop(0, snaps_old, one, start, unroll=max(u for u in range(1, 10) if snaps_old % u == 0))
        for c in range(comps):
            out_ref[pl.ds(c, count, stride=comps), :] = total[c]

    return pl.pallas_call(
        kernel, out_shape=jax.ShapeDtypeStruct((count * comps, part), F32),
        in_specs=[v, v, pl.BlockSpec(memory_space=pl.ANY), v, v], out_specs=v,
        scratch_shapes=[pltpu.VMEM(gram.shape, F32), pltpu.VMEM(basis_t.shape, F32), pltpu.VMEM(hist.shape, BF16),
                        pltpu.VMEM((count * 8, part), F32), pltpu.VMEM(gram.shape, F32), pltpu.SemaphoreType.DMA],
        compiler_params=pltpu.CompilerParams(vmem_limit_bytes=48 << 20),
    )(gram, basis_t, hist, first, second)


def shift(x, axis, by):
    count = lax.axis_size(axis)
    return lax.ppermute(x, axis, [(i, (i + by) % count) for i in range(count)])


def exchange(x, axis, bits):
    count = lax.axis_size(axis)
    masks = [0]
    for bit in bits:
        masks = masks + [m ^ bit for m in masks]
    total = x
    for m in masks[1:]:
        total = total + lax.ppermute(x, axis, [(i, i ^ m) for i in range(count)])
    return total


def reduce_all(x):
    for axis, together in (("vert", 1), ("stream", 2)):
        count = lax.axis_size(axis)
        if count & (count - 1):
            x = lax.psum(x, axis)
            continue
        bits = [1 << k for k in range(count.bit_length() - 1)]
        for k in range(0, len(bits), together):
            x = exchange(x, axis, bits[k:k + together])
    return x


def body(particles, phase_flags, neighbours, history, basis_start):
    count = particles.shape[0]
    codes = neighbours[:, 0].T
    width = codes.shape[0]
    hist = history[:, 0].transpose(1, 2, 0, 3)
    s, v = lax.axis_index("stream"), lax.axis_index("vert")
    ns, nv = lax.axis_size("stream"), lax.axis_size("vert")
    one = jnp.ones((), jnp.int32)
    common = [v > 0, one, v < nv - 1, s > 0, s < ns - 1]
    edges1 = jnp.stack(common + [2 * one, 0 * one, one]).astype(jnp.int32)
    edges2 = jnp.stack(common + [one, one, one]).astype(jnp.int32)
    state, lo, hi = prepare(particles[:, 0], phase_flags[:, 0], codes)
    from_low = shift(hi, "stream", 1)
    from_high = shift(lo, "stream", -1)
    mid = jnp.concatenate([from_low[0:2], state, from_high[0:2]], axis=0)
    wide_codes = jnp.concatenate(
        [from_low[2, 0:width, 0:1].astype(jnp.int32), codes, from_high[2, 0:width, 0:1].astype(jnp.int32)], axis=1)
    basis = start_basis(basis_start.T)
    first = first_step(wide_codes, edges1, shift(mid, "vert", 1), mid, shift(mid, "vert", -1), basis)
    low, high = shift(first, "vert", 1), shift(first, "vert", -1)
    gram = early_gram(hist, first)
    new_state, second, gram = second_step(wide_codes, edges2, low, first, high, hist, gram)
    gram = reduce_all(gram)
    out = filtered_field(gram, basis, hist, first, second)
    return (new_state.reshape(count, 1, 7, -1), out.reshape(count, 1, 3, -1))


def solution(mesh):
    in_specs = (
        P("stream", "vert", None, None),
        P("stream", "vert", None),
        P("stream", "vert", None),
        P("stream", "vert", None, None, None),
        P(),
    )
    out_specs = (P("stream", "vert", None, None), P("stream", "vert", None, None))
    return jax.shard_map(body, mesh=mesh, in_specs=in_specs, out_specs=out_specs, check_vma=False)
```

time: 96.7 us -> 74.4 us (0.77)
  local copies, waits for them, and re-layouts: 10.4 us -> 0.95 us
  waiting for transfers between devices: 19.9 us -> 14.8 us
  starting transfers between devices: 18.9 us -> 15.6 us
  other arithmetic: 2.3 us -> 0.14 us
  Pallas kernels: 43.8 us -> 41.8 us
    ppermute x8 -> x6, starting transfers between devices: 14.5 us -> 7.32 us  [shift(): return lax.ppermute(x, axis, [(i, (i + by) % count) for i in range(count)])]
    unnamed x7 -> x10, local copies, waits for them, and re-layouts: 7.67 us -> 0.77 us
    ppermute x5 -> x6, waiting for transfers between devices: 14.4 us -> 9.23 us  [exchange(): total = total + lax.ppermute(x, axis, [(i, i ^ m) for i in range(count)])]
    ppermute x5 -> x6, starting transfers between devices: 4.35 us -> 8.24 us  [exchange(): total = total + lax.ppermute(x, axis, [(i, i ^ m) for i in range(count)])]
    add x6 -> x4, other arithmetic: 2.24 us -> 0.05 us  [exchange(): total = total + lax.ppermute(x, axis, [(i, i ^ m) for i in range(count)])]
    pallas_call x5 -> x6, Pallas kernels: 43.8 us -> 41.8 us  [the longest x1 11.6 us: filtered_field(): pl.pallas_call(kernel, out_shape=jax.ShapeDtypeStruct((count * comps, par...]
    squeeze x2 -> x0, local copies, waits for them, and re-layouts: 1.67 us -> none  [the longest x1 0.91 us: body(): state = jnp.concatenate([particles[:, 0], rest_density], axis=1)]
    ppermute x8 -> x6, waiting for transfers between devices: 5.6 us -> 5.57 us  [shift(): return lax.ppermute(x, axis, [(i, (i + by) % count) for i in range(count)])]
  transfers between devices with their start and end apart: 13 -> 12, of which waited for: 9 -> 8; matrix products, arithmetic and copies ran while one was open for 8% -> 0% of each run, Pallas kernels for 0% -> 13%
where the time goes in v2:
time: 74.4 us; the launch traced here: 74.1 us
  Pallas kernels  41.8 us (56%)
  starting transfers between devices  15.6 us (21%)
  waiting for transfers between devices  14.8 us (20%)
  local copies, waits for them, and re-layouts  0.95 us (1%)
  between operations  0.93 us (1%)
    pallas_call x1, Pallas kernels, filtered_field(): pl.pallas_call(kernel, out_shape=jax.ShapeDtypeStruct((count * comps, par...  11.6 us
    pallas_call x1, Pallas kernels, second_step(): pl.pallas_call(kernel, out_shape=(jax.ShapeDtypeStruct((count * 7, part),...  10 us
    ppermute x6, waiting for transfers between devices, exchange(): total = total + lax.ppermute(x, axis, [(i, i ^ m) for i in range(count)])  9.23 us
    pallas_call x1, Pallas kernels, first_step(): pl.pallas_call(kernel, out_shape=jax.ShapeDtypeStruct((ext - 2, 8, part),...  8.63 us
    ppermute x6, starting transfers between devices, exchange(): total = total + lax.ppermute(x, axis, [(i, i ^ m) for i in range(count)])  8.24 us
    ppermute x6, starting transfers between devices, shift(): return lax.ppermute(x, axis, [(i, (i + by) % count) for i in range(count)])  7.32 us
    pallas_call x1, Pallas kernels, early_gram(): pl.pallas_call(kernel, out_shape=jax.ShapeDtypeStruct((snaps, snaps), F32...  6.35 us
    ppermute x6, waiting for transfers between devices, shift(): return lax.ppermute(x, axis, [(i, (i + by) % count) for i in range(count)])  5.57 us
  transfers between devices with their start and end apart: 12, of which 8 were waited for; matrix products, arithmetic and copies ran while one was open for 0% of the time, Pallas kernels for 13%

profile of v2, /device:TPU:0, one launch (start us, length us, event | category | flops | bytes accessed | tf_op | source)
XLA Modules:
  0.0 74.1 jit_solution(2394889478027903390)
XLA Ops:
  0.6 0.0 copy-start.4
  0.6 0.0 copy-start
  0.7 1.8 %shard_map.68 = (f32[32,8,128]{2,1,0:T(8,128)}, f32[3,8,128]{2,1,0:T(8,128)}, f32[3,8,128]{2,1,0:T(8,128)}) custom-call(f32[224,128]{1,0:T(8,128)} %bitcast.22, s32[32,128]{1,0:T(8,128)} %bitcast.24, s32[4,32]{1,0:T(4,128)} %bitcast.25), custom_call_target="tpu_custom_call" | custom-call | tf_op jit(solution)/shard_map/pallas_call | solution.py:85
  2.4 0.0 copy-start.3
  2.4 3.0 %collective-permute-start = (f32[3,8,128]{2,1,0:T(8,128)}, f32[3,8,128]{2,1,0:T(8,128)S(1)}, u32[]{:S(2)}, u32[]{:S(2)}) collective-permute-start(f32[3,8,128]{2,1,0:T(8,128)} %get-tuple-element.8), channel_id=1, source_target_pairs={{0,4},{4,8},{8,12},{12,16},{16,20},{20,24},{24,28},{28,0},{1,5},{5... | collective-permute-start | bytes 36872 | tf_op jit(solution)/shard_map/ppermute | solution.py:427
  5.4 3.1 %collective-permute-start.1 = (f32[3,8,128]{2,1,0:T(8,128)}, f32[3,8,128]{2,1,0:T(8,128)S(1)}, u32[]{:S(2)}, u32[]{:S(2)}) collective-permute-start(f32[3,8,128]{2,1,0:T(8,128)} %get-tuple-element.9), channel_id=1, source_target_pairs={{0,28},{4,0},{8,4},{12,8},{16,12},{20,16},{24,20},{28,24},{1,29},{... | collective-permute-start | bytes 36872 | tf_op jit(solution)/shard_map/ppermute | solution.py:427
  8.5 3.4 %shard_map.69.basis_any.b_ref = f32[64,128]{1,0:T(8,128)} custom-call(f32[64,128]{1,0:T(8,128)} %bitcast.28), custom_call_target="tpu_custom_call" | custom-call | flops 1073741824 | bytes 1048576 | tf_op jit(solution)/shard_map/pallas_call | solution.py:362
  11.9 0.1 stack.43.edge_ref
  12.0 0.0 collective-permute-done
  12.0 0.0 collective-permute-done.1
  12.0 0.0 copy-done.3
  12.1 0.7 collective-permute-start.3
  12.8 0.0 collective-permute-start.2
  12.8 0.0 copy-done.4
  12.8 0.1 pad_add_fusion.codes_ref
  12.9 3.8 %collective-permute-done.3.high_ref = f32[36,8,128]{2,1,0:T(8,128)S(1)} collective-permute-done((f32[36,8,128]{2,1,0:T(8,128)S(1)}, f32[36,8,128]{2,1,0:T(8,128)S(1)}, u32[]{:S(2)}, u32[]{:S(2)}) %collective-permute-start.3) | collective-permute-done | bytes 147488 | tf_op jit(solution)/shard_map/ppermute | solution.py:427
  16.6 1.8 %collective-permute-done.2.low_ref = f32[36,8,128]{2,1,0:T(8,128)S(1)} collective-permute-done((f32[36,8,128]{2,1,0:T(8,128)S(1)}, f32[36,8,128]{2,1,0:T(8,128)S(1)}, u32[]{:S(2)}, u32[]{:S(2)}) %collective-permute-start.2) | collective-permute-done | bytes 147488 | tf_op jit(solution)/shard_map/ppermute | solution.py:427
  18.4 0.0 copy-start.1
  18.4 0.8 %copy-done.1 = f32[64,128]{1,0:T(8,128)S(1)} copy-done((f32[64,128]{1,0:T(8,128)S(1)}, f32[64,128]{1,0:T(8,128)}, u32[]{:S(2)}) %copy-start.1) | copy-done | bytes 32792
  19.2 8.6 %shard_map.70.first_ref.mid_ref = f32[34,8,128]{2,1,0:T(8,128)S(1)} custom-call(s32[4,34]{1,0:T(4,128)S(1)} %pad_add_fusion.codes_ref, s32[8]{0:T(128)S(1)} %stack.43.edge_ref, f32[36,8,128]{2,1,0:T(8,128)S(1)} %collective-permute-done.2.low_ref, f32[36,8,128]{2,1,0:T(8,128)S(1)} %pad_maximum_fusion.mid_ref, ...), custom_call_target="tpu_custom_call" | custom-call | tf_op jit(solution)/shard_map/pallas_call | solution.py:172
  27.8 0.5 collective-permute-start.5
  28.3 0.1 collective-permute-start.4
  28.4 0.1 stack.42.edge_ref
  28.5 0.0 copy-done
  28.5 0.0 copy-start.2
  28.5 6.4 %shard_map.71.gram_ref = f32[128,128]{1,0:T(8,128)S(1)} custom-call(bf16[3,126,32,128]{3,2,1,0:T(8,128)(2,1)S(1)} %bitcast.19, f32[34,8,128]{2,1,0:T(8,128)S(1)} %shard_map.70.first_ref.mid_ref), custom_call_target="tpu_custom_call" | custom-call | flops 402653184 | bytes 3145728 | tf_op jit(solution)/shard_map/pallas_call | solution.py:279
  34.8 0.0 collective-permute-done.5.high_ref
  34.8 0.0 collective-permute-done.4.low_ref
  34.8 10.0 %shard_map.72 = (f32[224,128]{1,0:T(8,128)}, f32[32,8,128]{2,1,0:T(8,128)S(1)}, f32[128,128]{1,0:T(8,128)S(1)}) custom-call(s32[4,34]{1,0:T(4,128)S(1)} %pad_add_fusion.codes_ref, s32[8]{0:T(128)S(1)} %stack.42.edge_ref, f32[34,8,128]{2,1,0:T(8,128)S(1)} %collective-permute-done.4.low_ref, f32[34,8,128]{2,1,0:T(8,128)S(1)} %shard_map.70.first_ref.mid_ref, ...), custom_call_target="tpu_custom_call" | custom-call | tf_op jit(solution)/shard_map/pallas_call | solution.py:242
  44.9 1.0 %collective-permute-start.6 = (f32[128,128]{1,0:T(8,128)S(1)}, f32[128,128]{1,0:T(8,128)S(1)}, u32[]{:S(2)}, u32[]{:S(2)}) collective-permute-start(f32[128,128]{1,0:T(8,128)S(1)} %get-tuple-element.12), channel_id=1, source_target_pairs={{0,1},{1,0},{2,3},{3,2},{4,5},{5,4},{6,7},{7,6},{8,9},{9,8},{10,11... | collective-permute-start | bytes 196616 | tf_op jit(solution)/shard_map/ppermute | solution.py:437
  45.9 0.9 %collective-permute-done.6 = f32[128,128]{1,0:T(8,128)S(1)} collective-permute-done((f32[128,128]{1,0:T(8,128)S(1)}, f32[128,128]{1,0:T(8,128)S(1)}, u32[]{:S(2)}, u32[]{:S(2)}) %collective-permute-start.6) | collective-permute-done | bytes 65568 | tf_op jit(solution)/shard_map/ppermute | solution.py:437
  46.8 1.2 %collective-permute-start.7 = (f32[128,128]{1,0:T(8,128)S(1)}, f32[128,128]{1,0:T(8,128)S(1)}, u32[]{:S(2)}, u32[]{:S(2)}) collective-permute-start(f32[128,128]{1,0:T(8,128)S(1)} %add.18), channel_id=1, source_target_pairs={{0,2},{1,3},{2,0},{3,1},{4,6},{5,7},{6,4},{7,5},{8,10},{9,11},{10,... | collective-permute-start | bytes 196616 | tf_op jit(solution)/shard_map/ppermute | solution.py:437
  48.0 3.2 %collective-permute-done.7 = f32[128,128]{1,0:T(8,128)S(1)} collective-permute-done((f32[128,128]{1,0:T(8,128)S(1)}, f32[128,128]{1,0:T(8,128)S(1)}, u32[]{:S(2)}, u32[]{:S(2)}) %collective-permute-start.7) | collective-permute-done | bytes 65568 | tf_op jit(solution)/shard_map/ppermute | solution.py:437
  51.2 1.1 %collective-permute-start.10 = (f32[128,128]{1,0:T(8,128)S(1)}, f32[128,128]{1,0:T(8,128)S(1)}, u32[]{:S(2)}, u32[]{:S(2)}) collective-permute-start(f32[128,128]{1,0:T(8,128)S(1)} %add.19), channel_id=1, source_target_pairs={{0,12},{4,8},{8,4},{12,0},{16,28},{20,24},{24,20},{28,16},{1,13},{... | collective-permute-start | bytes 196616 | tf_op jit(solution)/shard_map/ppermute | solution.py:437
  52.3 0.5 collective-permute-start.9
  52.7 2.0 %collective-permute-start.8 = (f32[128,128]{1,0:T(8,128)S(1)}, f32[128,128]{1,0:T(8,128)S(1)}, u32[]{:S(2)}, u32[]{:S(2)}) collective-permute-start(f32[128,128]{1,0:T(8,128)S(1)} %add.19), channel_id=1, source_target_pairs={{0,4},{4,0},{8,12},{12,8},{16,20},{20,16},{24,28},{28,24},{1,5},{5... | collective-permute-start | bytes 196616 | tf_op jit(solution)/shard_map/ppermute | solution.py:437
  54.8 1.7 %collective-permute-done.10 = f32[128,128]{1,0:T(8,128)S(1)} collective-permute-done((f32[128,128]{1,0:T(8,128)S(1)}, f32[128,128]{1,0:T(8,128)S(1)}, u32[]{:S(2)}, u32[]{:S(2)}) %collective-permute-start.10) | collective-permute-done | bytes 65568 | tf_op jit(solution)/shard_map/ppermute | solution.py:437
  56.5 0.1 collective-permute-done.9
  56.5 0.6 collective-permute-done.8
  57.2 2.5 %collective-permute-start.11 = (f32[128,128]{1,0:T(8,128)S(1)}, f32[128,128]{1,0:T(8,128)S(1)}, u32[]{:S(2)}, u32[]{:S(2)}) collective-permute-start(f32[128,128]{1,0:T(8,128)S(1)} %add_add_fusion), channel_id=1, source_target_pairs={{0,16},{4,20},{8,24},{12,28},{16,0},{20,4},{24,8},{28,12},{1,17},{... | collective-permute-start | bytes 196616 | tf_op jit(solution)/shard_map/ppermute | solution.py:437
  59.7 2.7 %collective-permute-done.11 = f32[128,128]{1,0:T(8,128)S(1)} collective-permute-done((f32[128,128]{1,0:T(8,128)S(1)}, f32[128,128]{1,0:T(8,128)S(1)}, u32[]{:S(2)}, u32[]{:S(2)}) %collective-permute-start.11) | collective-permute-done | bytes 65568 | tf_op jit(solution)/shard_map/ppermute | solution.py:437
  62.4 0.0 copy-done.2
  62.4 11.6 %shard_map.73 = f32[96,128]{1,0:T(8,128)} custom-call(f32[128,128]{1,0:T(8,128)S(1)} %add.23.gram_ref, f32[64,128]{1,0:T(8,128)S(1)} %copy-done.2, bf16[3,126,32,128]{3,2,1,0:T(8,128)(2,1)S(1)} %bitcast.21, f32[34,8,128]{2,1,0:T(8,128)S(1)} %shard_map.70.first_ref.mid_ref, f32[32,8,128]{2,1,0:T(8,128)S(1)} %get-tuple-element.13.second_ref), custom_call_target="tpu_custom_call" | custom-call | tf_op jit(solution)/shard_map/pallas_call | solution.py:416
  (10 shorter events, 0.1 us)
Async XLA Ops:
  0.6 12.1 %copy-start.4 = (s32[32,1,4]{0,2,1:T(4,128)S(1)}, s32[32,1,4]{0,2,1:T(4,128)}, u32[]{:S(2)}) copy-start(s32[32,1,4]{0,2,1:T(4,128)} %param.7) | copy-start | bytes 1540
  0.6 27.8 %copy-start = (bf16[32,1,3,126,128]{4,0,3,2,1:T(8,128)(2,1)S(1)}, bf16[32,1,3,126,128]{4,0,3,2,1:T(8,128)(2,1)}, u32[]{:S(2)}) copy-start(bf16[32,1,3,126,128]{4,0,3,2,1:T(8,128)(2,1)} %param.8) | copy-start | bytes 9289732
  2.4 9.6 %copy-start.3 = (f32[32,8,128]{2,1,0:T(8,128)S(1)}, f32[32,8,128]{2,1,0:T(8,128)}, u32[]{:S(2)}) copy-start(f32[32,8,128]{2,1,0:T(8,128)} %get-tuple-element.10) | copy-start | bytes 393220
  2.4 9.6 %collective-permute-start = (f32[3,8,128]{2,1,0:T(8,128)}, f32[3,8,128]{2,1,0:T(8,128)S(1)}, u32[]{:S(2)}, u32[]{:S(2)}) collective-permute-start(f32[3,8,128]{2,1,0:T(8,128)} %get-tuple-element.8), channel_id=1, source_target_pairs={{0,4},{4,8},{8,12},{12,16},{16,20},{20,24},{24,28},{28,0},{1,5},{5... | collective-permute-start | bytes 36872 | tf_op jit(solution)/shard_map/ppermute | solution.py:427
  5.4 6.6 %collective-permute-start.1 = (f32[3,8,128]{2,1,0:T(8,128)}, f32[3,8,128]{2,1,0:T(8,128)S(1)}, u32[]{:S(2)}, u32[]{:S(2)}) collective-permute-start(f32[3,8,128]{2,1,0:T(8,128)} %get-tuple-element.9), channel_id=1, source_target_pairs={{0,28},{4,0},{8,4},{12,8},{16,12},{20,16},{24,20},{28,24},{1,29},{... | collective-permute-start | bytes 36872 | tf_op jit(solution)/shard_map/ppermute | solution.py:427
  12.1 4.6 %collective-permute-start.3 = (f32[36,8,128]{2,1,0:T(8,128)S(1)}, f32[36,8,128]{2,1,0:T(8,128)S(1)}, u32[]{:S(2)}, u32[]{:S(2)}) collective-permute-start(f32[36,8,128]{2,1,0:T(8,128)S(1)} %pad_maximum_fusion.mid_ref), channel_id=1, source_target_pairs={{0,3},{1,0},{2,1},{3,2},{4,7},{5,4},{6,5},{7,6},{8,11},{9,8},{10,9... | collective-permute-start | bytes 442376 | tf_op jit(solution)/shard_map/ppermute | solution.py:427
  12.8 5.7 %collective-permute-start.2 = (f32[36,8,128]{2,1,0:T(8,128)S(1)}, f32[36,8,128]{2,1,0:T(8,128)S(1)}, u32[]{:S(2)}, u32[]{:S(2)}) collective-permute-start(f32[36,8,128]{2,1,0:T(8,128)S(1)} %pad_maximum_fusion.mid_ref), channel_id=1, source_target_pairs={{0,1},{1,2},{2,3},{3,0},{4,5},{5,6},{6,7},{7,4},{8,9},{9,10},{10,1... | collective-permute-start | bytes 442376 | tf_op jit(solution)/shard_map/ppermute | solution.py:427
  18.4 0.8 %copy-start.1 = (f32[64,128]{1,0:T(8,128)S(1)}, f32[64,128]{1,0:T(8,128)}, u32[]{:S(2)}) copy-start(f32[64,128]{1,0:T(8,128)} %shard_map.69.basis_any.b_ref) | copy-start | bytes 98308
  27.8 7.0 %collective-permute-start.5 = (f32[34,8,128]{2,1,0:T(8,128)S(1)}, f32[34,8,128]{2,1,0:T(8,128)S(1)}, u32[]{:S(2)}, u32[]{:S(2)}) collective-permute-start(f32[34,8,128]{2,1,0:T(8,128)S(1)} %shard_map.70.first_ref.mid_ref), channel_id=1, source_target_pairs={{0,3},{1,0},{2,1},{3,2},{4,7},{5,4},{6,5},{7,6},{8,11},{9,8},{10,9... | collective-permute-start | bytes 417800 | tf_op jit(solution)/shard_map/ppermute | solution.py:427
  28.3 6.5 %collective-permute-start.4 = (f32[34,8,128]{2,1,0:T(8,128)S(1)}, f32[34,8,128]{2,1,0:T(8,128)S(1)}, u32[]{:S(2)}, u32[]{:S(2)}) collective-permute-start(f32[34,8,128]{2,1,0:T(8,128)S(1)} %shard_map.70.first_ref.mid_ref), channel_id=1, source_target_pairs={{0,1},{1,2},{2,3},{3,0},{4,5},{5,6},{6,7},{7,4},{8,9},{9,10},{10,1... | collective-permute-start | bytes 417800 | tf_op jit(solution)/shard_map/ppermute | solution.py:427
  28.5 34.0 %copy-start.2 = (f32[64,128]{1,0:T(8,128)S(1)}, f32[64,128]{1,0:T(8,128)}, u32[]{:S(2)}) copy-start(f32[64,128]{1,0:T(8,128)} %shard_map.69.basis_any.b_ref) | copy-start | bytes 98308
  44.9 1.9 %collective-permute-start.6 = (f32[128,128]{1,0:T(8,128)S(1)}, f32[128,128]{1,0:T(8,128)S(1)}, u32[]{:S(2)}, u32[]{:S(2)}) collective-permute-start(f32[128,128]{1,0:T(8,128)S(1)} %get-tuple-element.12), channel_id=1, source_target_pairs={{0,1},{1,0},{2,3},{3,2},{4,5},{5,4},{6,7},{7,6},{8,9},{9,8},{10,11... | collective-permute-start | bytes 196616 | tf_op jit(solution)/shard_map/ppermute | solution.py:437
  46.8 4.4 %collective-permute-start.7 = (f32[128,128]{1,0:T(8,128)S(1)}, f32[128,128]{1,0:T(8,128)S(1)}, u32[]{:S(2)}, u32[]{:S(2)}) collective-permute-start(f32[128,128]{1,0:T(8,128)S(1)} %add.18), channel_id=1, source_target_pairs={{0,2},{1,3},{2,0},{3,1},{4,6},{5,7},{6,4},{7,5},{8,10},{9,11},{10,... | collective-permute-start | bytes 196616 | tf_op jit(solution)/shard_map/ppermute | solution.py:437
  51.2 5.2 %collective-permute-start.10 = (f32[128,128]{1,0:T(8,128)S(1)}, f32[128,128]{1,0:T(8,128)S(1)}, u32[]{:S(2)}, u32[]{:S(2)}) collective-permute-start(f32[128,128]{1,0:T(8,128)S(1)} %add.19), channel_id=1, source_target_pairs={{0,12},{4,8},{8,4},{12,0},{16,28},{20,24},{24,20},{28,16},{1,13},{... | collective-permute-start | bytes 196616 | tf_op jit(solution)/shard_map/ppermute | solution.py:437
  52.3 4.3 %collective-permute-start.9 = (f32[128,128]{1,0:T(8,128)S(1)}, f32[128,128]{1,0:T(8,128)S(1)}, u32[]{:S(2)}, u32[]{:S(2)}) collective-permute-start(f32[128,128]{1,0:T(8,128)S(1)} %add.19), channel_id=1, source_target_pairs={{0,8},{4,12},{8,0},{12,4},{16,24},{20,28},{24,16},{28,20},{1,9},{5... | collective-permute-start | bytes 196616 | tf_op jit(solution)/shard_map/ppermute | solution.py:437
  52.7 4.4 %collective-permute-start.8 = (f32[128,128]{1,0:T(8,128)S(1)}, f32[128,128]{1,0:T(8,128)S(1)}, u32[]{:S(2)}, u32[]{:S(2)}) collective-permute-start(f32[128,128]{1,0:T(8,128)S(1)} %add.19), channel_id=1, source_target_pairs={{0,4},{4,0},{8,12},{12,8},{16,20},{20,16},{24,28},{28,24},{1,5},{5... | collective-permute-start | bytes 196616 | tf_op jit(solution)/shard_map/ppermute | solution.py:437
  57.2 5.2 %collective-permute-start.11 = (f32[128,128]{1,0:T(8,128)S(1)}, f32[128,128]{1,0:T(8,128)S(1)}, u32[]{:S(2)}, u32[]{:S(2)}) collective-permute-start(f32[128,128]{1,0:T(8,128)S(1)} %add_add_fusion), channel_id=1, source_target_pairs={{0,16},{4,20},{8,24},{12,28},{16,0},{20,4},{24,8},{28,12},{1,17},{... | collective-permute-start | bytes 196616 | tf_op jit(solution)/shard_map/ppermute | solution.py:437

commit v3 on v2

--- a/solution.py
+++ b/solution.py
@@ -9,6 +9,7 @@
 from jax.sharding import PartitionSpec as P
 
 POD_ITERS = 4
+VMEM_LIMIT = 20 << 20
 SEDIMENT_EXTRA = 1.65
 
 
@@ -162,19 +163,16 @@
     return [pltpu.VMEM((3 * ext, 24, part), F32)] * 3
 
 
-def first_step(codes, edges, low, mid, high, basis):
+def first_step(codes, edges, low, mid, high):
     ext, _, part = mid.shape
     v = pl.BlockSpec(memory_space=pltpu.VMEM)
     sm = pl.BlockSpec(memory_space=pltpu.SMEM)
-    def kernel(codes_ref, edge_ref, low_ref, mid_ref, high_ref, basis_any, out_ref, *scratch):
-        step_blocks(codes_ref, edge_ref, low_ref, mid_ref, high_ref, out_ref, *scratch)
-
-    return pl.pallas_call(
-        kernel, out_shape=jax.ShapeDtypeStruct((ext - 2, 8, part), F32),
-        in_specs=[sm, sm, v, v, v, pl.BlockSpec(memory_space=pl.ANY)], out_specs=v,
+    return pl.pallas_call(
+        step_blocks, out_shape=jax.ShapeDtypeStruct((ext - 2, 8, part), F32),
+        in_specs=[sm, sm, v, v, v], out_specs=v,
         scratch_shapes=step_scratch(ext, part),
-        compiler_params=pltpu.CompilerParams(vmem_limit_bytes=48 << 20),
-    )(codes, edges, low, mid, high, basis)
+        compiler_params=pltpu.CompilerParams(vmem_limit_bytes=VMEM_LIMIT),
+    )(codes, edges, low, mid, high)
 
 
 def cross_row(hist_ref, new, others, terms):
@@ -225,12 +223,9 @@
     v = pl.BlockSpec(memory_space=pltpu.VMEM)
     sm = pl.BlockSpec(memory_space=pltpu.SMEM)
 
-    def kernel(codes_ref, edge_ref, low_ref, mid_ref, high_ref, hist_any, gram_ref, new_ref, state_ref, gram_out,
-               b0, b1, b2, hist_ref, flat, terms, sem):
-        copy = pltpu.make_async_copy(hist_any, hist_ref, sem)
-        copy.start()
+    def kernel(codes_ref, edge_ref, low_ref, mid_ref, high_ref, hist_ref, gram_ref, new_ref, state_ref, gram_out,
+               b0, b1, b2, flat, terms):
         step_blocks(codes_ref, edge_ref, low_ref, mid_ref, high_ref, state_ref, b0, b1, b2)
-        copy.wait()
         first = load_new(mid_ref, 1, count, flat)
         second = load_new(state_ref, 0, count, flat)
         for i in range(7):
@@ -243,33 +238,28 @@
         kernel,
         out_shape=(jax.ShapeDtypeStruct((count * 7, part), F32), jax.ShapeDtypeStruct((count, 8, part), F32),
                    jax.ShapeDtypeStruct((snaps, snaps), F32)),
-        in_specs=[sm, sm, v, v, v, pl.BlockSpec(memory_space=pl.ANY), v], out_specs=(v, v, v),
+        in_specs=[sm, sm, v, v, v, v, v], out_specs=(v, v, v),
         scratch_shapes=step_scratch(ext, part) + [
-            pltpu.VMEM(hist.shape, BF16), pltpu.VMEM((count * 8, part), F32), pltpu.VMEM((snaps * 8, part), F32),
-            pltpu.SemaphoreType.DMA],
-        compiler_params=pltpu.CompilerParams(vmem_limit_bytes=48 << 20),
+            pltpu.VMEM((count * 8, part), F32), pltpu.VMEM((snaps * 8, part), F32)],
+        compiler_params=pltpu.CompilerParams(vmem_limit_bytes=VMEM_LIMIT),
     )(codes, edges, low, mid, high, hist, gram)
 
 
 def early_gram(hist, first):
     comps, snaps_old, count, part = hist.shape
     snaps = snaps_old + 2
-    v = pl.BlockSpec(memory_space=pltpu.VMEM)
-
-    def kernel(hist_any, first_ref, out_ref, hist_ref, wide, flat, terms, sems):
-        copies = [pltpu.make_async_copy(hist_any.at[c], hist_ref.at[c], sems.at[c]) for c in range(comps)]
-        for copy in copies:
-            copy.start()
+    pitch = count + 8
+    v = pl.BlockSpec(memory_space=pltpu.VMEM)
+
+    def kernel(hist_ref, first_ref, out_ref, wide, flat, terms):
         total = jnp.zeros((snaps_old, snaps_old), F32)
         for c in range(comps):
-            copies[c].wait()
-
             def expand(s, _):
-                wide[pl.ds(pl.multiple_of(count * s, 8), count), :] = hist_ref[c, s].astype(F32)
+                wide[pl.ds(pl.multiple_of(pitch * s, 8), count), :] = hist_ref[c, s].astype(F32)
                 return 0
             lax.fori_loop(0, snaps_old, expand, 0, unroll=max(u for u in range(1, 10) if snaps_old % u == 0))
             for b in range(0, count, 8):
-                x = jnp.concatenate([wide[pl.ds(b + j, snaps_old, stride=count), :].astype(BF16) for j in range(8)], axis=1)
+                x = jnp.concatenate([wide[pl.ds(b + j, snaps_old, stride=pitch), :].astype(BF16) for j in range(8)], axis=1)
                 total = total + lax.dot_general(x, x, (((1,), (1,)), ((), ())), preferred_element_type=F32)
         out_ref[...] = jnp.zeros_like(out_ref)
         out_ref[0:snaps_old, 0:snaps_old] = total
@@ -278,10 +268,10 @@
 
     return pl.pallas_call(
         kernel, out_shape=jax.ShapeDtypeStruct((snaps, snaps), F32),
-        in_specs=[pl.BlockSpec(memory_space=pl.ANY), v], out_specs=v,
-        scratch_shapes=[pltpu.VMEM(hist.shape, BF16), pltpu.VMEM((snaps_old * count, part), F32), pltpu.VMEM((count * 8, part), F32),
-                        pltpu.VMEM((snaps * 8, part), F32), pltpu.SemaphoreType.DMA((comps,))],
-        compiler_params=pltpu.CompilerParams(vmem_limit_bytes=48 << 20),
+        in_specs=[v, v], out_specs=v,
+        scratch_shapes=[pltpu.VMEM((snaps_old * pitch, part), F32), pltpu.VMEM((count * 8, part), F32),
+                        pltpu.VMEM((snaps * 8, part), F32)],
+        compiler_params=pltpu.CompilerParams(vmem_limit_bytes=VMEM_LIMIT),
         cost_estimate=pl.CostEstimate(flops=2 * comps * snaps * snaps * count * part, bytes_accessed=2 * comps * snaps * count * part, transcendentals=0),
     )(hist, first)
 
@@ -393,13 +383,10 @@
     comps, snaps_old, count, part = hist.shape
     v = pl.BlockSpec(memory_space=pltpu.VMEM)
 
-    def kernel(gram_ref, b_ref, hist_any, first_ref, second_ref, out_ref, g_ref, q_ref, hist_ref, flat, table, sem):
-        copy = pltpu.make_async_copy(hist_any, hist_ref, sem)
-        copy.start()
+    def kernel(gram_ref, b_ref, hist_ref, first_ref, second_ref, out_ref, g_ref, q_ref, flat, table):
         g_ref[...] = gram_ref[...]
         w = weigh(POD_ITERS, g_ref, b_ref, q_ref)
         table[...] = jnp.broadcast_to(w, table.shape).T
-        copy.wait()
         start = []
         for k, (ref, skip) in enumerate(((first_ref, 1), (second_ref, 0))):
             wk = table[snaps_old + k:snaps_old + k + 1]
@@ -415,10 +402,10 @@
 
     return pl.pallas_call(
         kernel, out_shape=jax.ShapeDtypeStruct((count * comps, part), F32),
-        in_specs=[v, v, pl.BlockSpec(memory_space=pl.ANY), v, v], out_specs=v,
-        scratch_shapes=[pltpu.VMEM(gram.shape, F32), pltpu.VMEM(basis_t.shape, F32), pltpu.VMEM(hist.shape, BF16),
-                        pltpu.VMEM((count * 8, part), F32), pltpu.VMEM(gram.shape, F32), pltpu.SemaphoreType.DMA],
-        compiler_params=pltpu.CompilerParams(vmem_limit_bytes=48 << 20),
+        in_specs=[v, v, v, v, v], out_specs=v,
+        scratch_shapes=[pltpu.VMEM(gram.shape, F32), pltpu.VMEM(basis_t.shape, F32),
+                        pltpu.VMEM((count * 8, part), F32), pltpu.VMEM(gram.shape, F32)],
+        compiler_params=pltpu.CompilerParams(vmem_limit_bytes=VMEM_LIMIT),
     )(gram, basis_t, hist, first, second)
 
 
@@ -467,8 +454,10 @@
     mid = jnp.concatenate([from_low[0:2], state, from_high[0:2]], axis=0)
     wide_codes = jnp.concatenate(
         [from_low[2, 0:width, 0:1].astype(jnp.int32), codes, from_high[2, 0:width, 0:1].astype(jnp.int32)], axis=1)
+    low_mid, high_mid = shift(mid, "vert", 1), shift(mid, "vert", -1)
     basis = start_basis(basis_start.T)
-    first = first_step(wide_codes, edges1, shift(mid, "vert", 1), mid, shift(mid, "vert", -1), basis)
+    wide_codes, basis = lax.optimization_barrier((wide_codes, basis))
+    first = first_step(wide_codes, edges1, low_mid, mid, high_mid)
     low, high = shift(first, "vert", 1), shift(first, "vert", -1)
     gram = early_gram(hist, first)
     new_state, second, gram = second_step(wide_codes, edges2, low, first, high, hist, gram)

time: 74.4 us -> 70.6 us (0.949)
  Pallas kernels: 41.8 us -> 37.7 us
  waiting for transfers between devices: 14.8 us -> 17.2 us
  starting transfers between devices: 15.6 us -> 14.4 us
  local copies, waits for them, and re-layouts: 0.95 us -> 0.19 us
    pallas_call x1, Pallas kernels: 6.35 us -> 3.24 us  [early_gram(): pl.pallas_call(kernel, out_shape=jax.ShapeDtypeStruct((snaps, snaps), F32...]
    ppermute x6, waiting for transfers between devices: 5.57 us -> 7.58 us  [shift(): return lax.ppermute(x, axis, [(i, (i + by) % count) for i in range(count)])]
    ppermute x6, starting transfers between devices: 8.24 us -> 7.13 us  [exchange(): total = total + lax.ppermute(x, axis, [(i, i ^ m) for i in range(count)])]
    unnamed x10 -> x8, local copies, waits for them, and re-layouts: 0.77 us -> 0.02 us
  transfers between devices with their start and end apart: 12 -> 12, of which waited for: 8 -> 9; matrix products, arithmetic and copies ran while one was open for 0% -> 0% of each run, Pallas kernels for 13% -> 9%
where the time goes in v3:
time: 70.6 us; the launch traced here: 70.4 us
  Pallas kernels  37.7 us (53%)
  waiting for transfers between devices  17.2 us (24%)
  starting transfers between devices  14.4 us (20%)
  between operations  0.74 us (1%)
    pallas_call x1, Pallas kernels, filtered_field(): pl.pallas_call(kernel, out_shape=jax.ShapeDtypeStruct((count * comps, par...  11.1 us
    ppermute x6, waiting for transfers between devices, exchange(): total = total + lax.ppermute(x, axis, [(i, i ^ m) for i in range(count)])  9.62 us
    pallas_call x1, Pallas kernels, second_step(): pl.pallas_call(kernel, out_shape=(jax.ShapeDtypeStruct((count * 7, part),...  9.59 us
    pallas_call x1, Pallas kernels, first_step(): pl.pallas_call(step_blocks, out_shape=jax.ShapeDtypeStruct((ext - 2, 8, p...  8.64 us
    ppermute x6, waiting for transfers between devices, shift(): return lax.ppermute(x, axis, [(i, (i + by) % count) for i in range(count)])  7.58 us
    ppermute x6, starting transfers between devices, shift(): return lax.ppermute(x, axis, [(i, (i + by) % count) for i in range(count)])  7.32 us
    ppermute x6, starting transfers between devices, exchange(): total = total + lax.ppermute(x, axis, [(i, i ^ m) for i in range(count)])  7.13 us
    pallas_call x1, Pallas kernels, start_basis(): pl.pallas_call(kernel, out_shape=jax.ShapeDtypeStruct(basis_t.shape, F32)...  3.42 us
  transfers between devices with their start and end apart: 12, of which 9 were waited for; matrix products, arithmetic and copies ran while one was open for 0% of the time, Pallas kernels for 9%

profile of v3, /device:TPU:0, one launch (start us, length us, event | category | flops | bytes accessed | tf_op | source)
XLA Modules:
  0.0 70.4 jit_solution(1777852634483330908)
XLA Ops:
  0.6 0.0 copy-start.3
  0.6 0.0 copy-start
  0.7 1.8 %shard_map.68 = (f32[32,8,128]{2,1,0:T(8,128)}, f32[3,8,128]{2,1,0:T(8,128)}, f32[3,8,128]{2,1,0:T(8,128)}) custom-call(f32[224,128]{1,0:T(8,128)} %bitcast.22, s32[32,128]{1,0:T(8,128)} %bitcast.24, s32[4,32]{1,0:T(4,128)} %bitcast.25), custom_call_target="tpu_custom_call" | custom-call | tf_op jit(solution)/shard_map/pallas_call | solution.py:86
  2.4 0.0 copy-start.2
  2.4 3.0 %collective-permute-start = (f32[3,8,128]{2,1,0:T(8,128)}, f32[3,8,128]{2,1,0:T(8,128)S(1)}, u32[]{:S(2)}, u32[]{:S(2)}) collective-permute-start(f32[3,8,128]{2,1,0:T(8,128)} %get-tuple-element.10), channel_id=1, source_target_pairs={{0,4},{4,8},{8,12},{12,16},{16,20},{20,24},{24,28},{28,0},{1,5},{5... | collective-permute-start | bytes 36872 | tf_op jit(solution)/shard_map/ppermute | solution.py:414
  5.4 3.1 %collective-permute-start.1 = (f32[3,8,128]{2,1,0:T(8,128)}, f32[3,8,128]{2,1,0:T(8,128)S(1)}, u32[]{:S(2)}, u32[]{:S(2)}) collective-permute-start(f32[3,8,128]{2,1,0:T(8,128)} %get-tuple-element.11), channel_id=1, source_target_pairs={{0,28},{4,0},{8,4},{12,8},{16,12},{20,16},{24,20},{28,24},{1,29},{... | collective-permute-start | bytes 36872 | tf_op jit(solution)/shard_map/ppermute | solution.py:414
  8.5 3.4 %shard_map.69.b_ref = f32[64,128]{1,0:T(8,128)} custom-call(f32[64,128]{1,0:T(8,128)} %bitcast.28), custom_call_target="tpu_custom_call" | custom-call | flops 1073741824 | bytes 1048576 | tf_op jit(solution)/shard_map/pallas_call | solution.py:352
  11.9 0.1 stack.43.edge_ref
  12.0 0.0 collective-permute-done
  12.0 0.0 collective-permute-done.1
  12.0 0.0 copy-done.2
  12.0 0.7 collective-permute-start.3
  12.7 0.0 collective-permute-start.2
  12.8 0.0 copy-done.3
  12.8 0.1 pad_add_fusion.codes_ref
  12.8 3.8 %collective-permute-done.3.high_ref = f32[36,8,128]{2,1,0:T(8,128)S(1)} collective-permute-done((f32[36,8,128]{2,1,0:T(8,128)S(1)}, f32[36,8,128]{2,1,0:T(8,128)S(1)}, u32[]{:S(2)}, u32[]{:S(2)}) %collective-permute-start.3) | collective-permute-done | bytes 147488 | tf_op jit(solution)/shard_map/ppermute | solution.py:414
  16.6 1.8 %collective-permute-done.2.low_ref = f32[36,8,128]{2,1,0:T(8,128)S(1)} collective-permute-done((f32[36,8,128]{2,1,0:T(8,128)S(1)}, f32[36,8,128]{2,1,0:T(8,128)S(1)}, u32[]{:S(2)}, u32[]{:S(2)}) %collective-permute-start.2) | collective-permute-done | bytes 147488 | tf_op jit(solution)/shard_map/ppermute | solution.py:414
  18.4 8.6 %shard_map.70.first_ref.mid_ref = f32[34,8,128]{2,1,0:T(8,128)S(1)} custom-call(s32[4,34]{1,0:T(4,128)S(1)} %pad_add_fusion.codes_ref, s32[8]{0:T(128)S(1)} %stack.43.edge_ref, f32[36,8,128]{2,1,0:T(8,128)S(1)} %collective-permute-done.2.low_ref, f32[36,8,128]{2,1,0:T(8,128)S(1)} %pad_maximum_fusion.mid_ref, f32[36,8,128]{2,1,0:T(8,128)S(1)} %collective-permute-done.3.high_ref), custom_call_target="tpu_custom_call" | custom-call | tf_op jit(solution)/shard_map/pallas_call | solution.py:170
  27.0 0.5 collective-permute-start.5
  27.5 0.1 collective-permute-start.4
  27.6 0.1 stack.42.edge_ref
  27.7 0.0 copy-done
  27.7 0.0 copy-start.1
  27.7 3.2 %shard_map.71.gram_ref = f32[128,128]{1,0:T(8,128)S(1)} custom-call(bf16[3,126,32,128]{3,2,1,0:T(8,128)(2,1)S(1)} %bitcast.19, f32[34,8,128]{2,1,0:T(8,128)S(1)} %shard_map.70.first_ref.mid_ref), custom_call_target="tpu_custom_call" | custom-call | flops 402653184 | bytes 3145728 | tf_op jit(solution)/shard_map/pallas_call | solution.py:269
  30.9 0.4 collective-permute-done.5.high_ref
  31.3 1.6 %collective-permute-done.4.low_ref = f32[34,8,128]{2,1,0:T(8,128)S(1)} collective-permute-done((f32[34,8,128]{2,1,0:T(8,128)S(1)}, f32[34,8,128]{2,1,0:T(8,128)S(1)}, u32[]{:S(2)}, u32[]{:S(2)}) %collective-permute-start.4) | collective-permute-done | bytes 139296 | tf_op jit(solution)/shard_map/ppermute | solution.py:414
  33.0 9.6 %shard_map.72 = (f32[224,128]{1,0:T(8,128)}, f32[32,8,128]{2,1,0:T(8,128)S(1)}, f32[128,128]{1,0:T(8,128)S(1)}) custom-call(s32[4,34]{1,0:T(4,128)S(1)} %pad_add_fusion.codes_ref, s32[8]{0:T(128)S(1)} %stack.42.edge_ref, f32[34,8,128]{2,1,0:T(8,128)S(1)} %collective-permute-done.4.low_ref, f32[34,8,128]{2,1,0:T(8,128)S(1)} %shard_map.70.first_ref.mid_ref, ...), custom_call_target="tpu_custom_call" | custom-call | tf_op jit(solution)/shard_map/pallas_call | solution.py:237
  42.5 0.0 collective-permute-start.6
  42.6 1.3 %collective-permute-done.6 = f32[128,128]{1,0:T(8,128)S(1)} collective-permute-done((f32[128,128]{1,0:T(8,128)S(1)}, f32[128,128]{1,0:T(8,128)S(1)}, u32[]{:S(2)}, u32[]{:S(2)}) %collective-permute-start.6) | collective-permute-done | bytes 65568 | tf_op jit(solution)/shard_map/ppermute | solution.py:424
  43.8 1.2 %collective-permute-start.7 = (f32[128,128]{1,0:T(8,128)S(1)}, f32[128,128]{1,0:T(8,128)S(1)}, u32[]{:S(2)}, u32[]{:S(2)}) collective-permute-start(f32[128,128]{1,0:T(8,128)S(1)} %add.18), channel_id=1, source_target_pairs={{0,2},{1,3},{2,0},{3,1},{4,6},{5,7},{6,4},{7,5},{8,10},{9,11},{10,... | collective-permute-start | bytes 196616 | tf_op jit(solution)/shard_map/ppermute | solution.py:424
  45.0 3.2 %collective-permute-done.7 = f32[128,128]{1,0:T(8,128)S(1)} collective-permute-done((f32[128,128]{1,0:T(8,128)S(1)}, f32[128,128]{1,0:T(8,128)S(1)}, u32[]{:S(2)}, u32[]{:S(2)}) %collective-permute-start.7) | collective-permute-done | bytes 65568 | tf_op jit(solution)/shard_map/ppermute | solution.py:424
  48.2 1.0 %collective-permute-start.10 = (f32[128,128]{1,0:T(8,128)S(1)}, f32[128,128]{1,0:T(8,128)S(1)}, u32[]{:S(2)}, u32[]{:S(2)}) collective-permute-start(f32[128,128]{1,0:T(8,128)S(1)} %add.19), channel_id=1, source_target_pairs={{0,12},{4,8},{8,4},{12,0},{16,28},{20,24},{24,20},{28,16},{1,13},{... | collective-permute-start | bytes 196616 | tf_op jit(solution)/shard_map/ppermute | solution.py:424
  49.1 0.5 collective-permute-start.9
  49.6 2.1 %collective-permute-start.8 = (f32[128,128]{1,0:T(8,128)S(1)}, f32[128,128]{1,0:T(8,128)S(1)}, u32[]{:S(2)}, u32[]{:S(2)}) collective-permute-start(f32[128,128]{1,0:T(8,128)S(1)} %add.19), channel_id=1, source_target_pairs={{0,4},{4,0},{8,12},{12,8},{16,20},{20,16},{24,28},{28,24},{1,5},{5... | collective-permute-start | bytes 196616 | tf_op jit(solution)/shard_map/ppermute | solution.py:424
  51.7 1.7 %collective-permute-done.10 = f32[128,128]{1,0:T(8,128)S(1)} collective-permute-done((f32[128,128]{1,0:T(8,128)S(1)}, f32[128,128]{1,0:T(8,128)S(1)}, u32[]{:S(2)}, u32[]{:S(2)}) %collective-permute-start.10) | collective-permute-done | bytes 65568 | tf_op jit(solution)/shard_map/ppermute | solution.py:424
  53.4 0.0 collective-permute-done.9
  53.4 0.7 collective-permute-done.8
  54.1 2.4 %collective-permute-start.11 = (f32[128,128]{1,0:T(8,128)S(1)}, f32[128,128]{1,0:T(8,128)S(1)}, u32[]{:S(2)}, u32[]{:S(2)}) collective-permute-start(f32[128,128]{1,0:T(8,128)S(1)} %add_add_fusion), channel_id=1, source_target_pairs={{0,16},{4,20},{8,24},{12,28},{16,0},{20,4},{24,8},{28,12},{1,17},{... | collective-permute-start | bytes 196616 | tf_op jit(solution)/shard_map/ppermute | solution.py:424
  56.5 2.8 %collective-permute-done.11 = f32[128,128]{1,0:T(8,128)S(1)} collective-permute-done((f32[128,128]{1,0:T(8,128)S(1)}, f32[128,128]{1,0:T(8,128)S(1)}, u32[]{:S(2)}, u32[]{:S(2)}) %collective-permute-start.11) | collective-permute-done | bytes 65568 | tf_op jit(solution)/shard_map/ppermute | solution.py:424
  59.4 0.0 copy-done.1
  59.4 11.1 %shard_map.73 = f32[96,128]{1,0:T(8,128)} custom-call(f32[128,128]{1,0:T(8,128)S(1)} %add.23.gram_ref, f32[64,128]{1,0:T(8,128)S(1)} %copy-done.1, bf16[3,126,32,128]{3,2,1,0:T(8,128)(2,1)S(1)} %bitcast.21, f32[34,8,128]{2,1,0:T(8,128)S(1)} %shard_map.70.first_ref.mid_ref, f32[32,8,128]{2,1,0:T(8,128)S(1)} %get-tuple-element.17.second_ref), custom_call_target="tpu_custom_call" | custom-call | tf_op jit(solution)/shard_map/pallas_call | solution.py:403
  (10 shorter events, 0.1 us)
Async XLA Ops:
  0.6 12.1 %copy-start.3 = (s32[32,1,4]{0,2,1:T(4,128)S(1)}, s32[32,1,4]{0,2,1:T(4,128)}, u32[]{:S(2)}) copy-start(s32[32,1,4]{0,2,1:T(4,128)} %param.7) | copy-start | bytes 1540
  0.6 27.1 %copy-start = (bf16[32,1,3,126,128]{4,0,3,2,1:T(8,128)(2,1)S(1)}, bf16[32,1,3,126,128]{4,0,3,2,1:T(8,128)(2,1)}, u32[]{:S(2)}) copy-start(bf16[32,1,3,126,128]{4,0,3,2,1:T(8,128)(2,1)} %param.8) | copy-start | bytes 9289732
  2.4 9.6 %copy-start.2 = (f32[32,8,128]{2,1,0:T(8,128)S(1)}, f32[32,8,128]{2,1,0:T(8,128)}, u32[]{:S(2)}) copy-start(f32[32,8,128]{2,1,0:T(8,128)} %get-tuple-element.13) | copy-start | bytes 393220
  2.4 9.6 %collective-permute-start = (f32[3,8,128]{2,1,0:T(8,128)}, f32[3,8,128]{2,1,0:T(8,128)S(1)}, u32[]{:S(2)}, u32[]{:S(2)}) collective-permute-start(f32[3,8,128]{2,1,0:T(8,128)} %get-tuple-element.10), channel_id=1, source_target_pairs={{0,4},{4,8},{8,12},{12,16},{16,20},{20,24},{24,28},{28,0},{1,5},{5... | collective-permute-start | bytes 36872 | tf_op jit(solution)/shard_map/ppermute | solution.py:414
  5.4 6.6 %collective-permute-start.1 = (f32[3,8,128]{2,1,0:T(8,128)}, f32[3,8,128]{2,1,0:T(8,128)S(1)}, u32[]{:S(2)}, u32[]{:S(2)}) collective-permute-start(f32[3,8,128]{2,1,0:T(8,128)} %get-tuple-element.11), channel_id=1, source_target_pairs={{0,28},{4,0},{8,4},{12,8},{16,12},{20,16},{24,20},{28,24},{1,29},{... | collective-permute-start | bytes 36872 | tf_op jit(solution)/shard_map/ppermute | solution.py:414
  12.0 4.6 %collective-permute-start.3 = (f32[36,8,128]{2,1,0:T(8,128)S(1)}, f32[36,8,128]{2,1,0:T(8,128)S(1)}, u32[]{:S(2)}, u32[]{:S(2)}) collective-permute-start(f32[36,8,128]{2,1,0:T(8,128)S(1)} %pad_maximum_fusion.mid_ref), channel_id=1, source_target_pairs={{0,3},{1,0},{2,1},{3,2},{4,7},{5,4},{6,5},{7,6},{8,11},{9,8},{10,9... | collective-permute-start | bytes 442376 | tf_op jit(solution)/shard_map/ppermute | solution.py:414
  12.7 5.7 %collective-permute-start.2 = (f32[36,8,128]{2,1,0:T(8,128)S(1)}, f32[36,8,128]{2,1,0:T(8,128)S(1)}, u32[]{:S(2)}, u32[]{:S(2)}) collective-permute-start(f32[36,8,128]{2,1,0:T(8,128)S(1)} %pad_maximum_fusion.mid_ref), channel_id=1, source_target_pairs={{0,1},{1,2},{2,3},{3,0},{4,5},{5,6},{6,7},{7,4},{8,9},{9,10},{10,1... | collective-permute-start | bytes 442376 | tf_op jit(solution)/shard_map/ppermute | solution.py:414
  27.0 4.3 %collective-permute-start.5 = (f32[34,8,128]{2,1,0:T(8,128)S(1)}, f32[34,8,128]{2,1,0:T(8,128)S(1)}, u32[]{:S(2)}, u32[]{:S(2)}) collective-permute-start(f32[34,8,128]{2,1,0:T(8,128)S(1)} %shard_map.70.first_ref.mid_ref), channel_id=1, source_target_pairs={{0,3},{1,0},{2,1},{3,2},{4,7},{5,4},{6,5},{7,6},{8,11},{9,8},{10,9... | collective-permute-start | bytes 417800 | tf_op jit(solution)/shard_map/ppermute | solution.py:414
  27.5 5.4 %collective-permute-start.4 = (f32[34,8,128]{2,1,0:T(8,128)S(1)}, f32[34,8,128]{2,1,0:T(8,128)S(1)}, u32[]{:S(2)}, u32[]{:S(2)}) collective-permute-start(f32[34,8,128]{2,1,0:T(8,128)S(1)} %shard_map.70.first_ref.mid_ref), channel_id=1, source_target_pairs={{0,1},{1,2},{2,3},{3,0},{4,5},{5,6},{6,7},{7,4},{8,9},{9,10},{10,1... | collective-permute-start | bytes 417800 | tf_op jit(solution)/shard_map/ppermute | solution.py:414
  27.7 31.7 %copy-start.1 = (f32[64,128]{1,0:T(8,128)S(1)}, f32[64,128]{1,0:T(8,128)}, u32[]{:S(2)}) copy-start(f32[64,128]{1,0:T(8,128)} %shard_map.69.b_ref) | copy-start | bytes 98308
  42.5 1.3 %collective-permute-start.6 = (f32[128,128]{1,0:T(8,128)S(1)}, f32[128,128]{1,0:T(8,128)S(1)}, u32[]{:S(2)}, u32[]{:S(2)}) collective-permute-start(f32[128,128]{1,0:T(8,128)S(1)} %get-tuple-element.15), channel_id=1, source_target_pairs={{0,1},{1,0},{2,3},{3,2},{4,5},{5,4},{6,7},{7,6},{8,9},{9,8},{10,11... | collective-permute-start | bytes 196616 | tf_op jit(solution)/shard_map/ppermute | solution.py:424
  43.8 4.3 %collective-permute-start.7 = (f32[128,128]{1,0:T(8,128)S(1)}, f32[128,128]{1,0:T(8,128)S(1)}, u32[]{:S(2)}, u32[]{:S(2)}) collective-permute-start(f32[128,128]{1,0:T(8,128)S(1)} %add.18), channel_id=1, source_target_pairs={{0,2},{1,3},{2,0},{3,1},{4,6},{5,7},{6,4},{7,5},{8,10},{9,11},{10,... | collective-permute-start | bytes 196616 | tf_op jit(solution)/shard_map/ppermute | solution.py:424
  48.2 5.2 %collective-permute-start.10 = (f32[128,128]{1,0:T(8,128)S(1)}, f32[128,128]{1,0:T(8,128)S(1)}, u32[]{:S(2)}, u32[]{:S(2)}) collective-permute-start(f32[128,128]{1,0:T(8,128)S(1)} %add.19), channel_id=1, source_target_pairs={{0,12},{4,8},{8,4},{12,0},{16,28},{20,24},{24,20},{28,16},{1,13},{... | collective-permute-start | bytes 196616 | tf_op jit(solution)/shard_map/ppermute | solution.py:424
  49.1 4.3 %collective-permute-start.9 = (f32[128,128]{1,0:T(8,128)S(1)}, f32[128,128]{1,0:T(8,128)S(1)}, u32[]{:S(2)}, u32[]{:S(2)}) collective-permute-start(f32[128,128]{1,0:T(8,128)S(1)} %add.19), channel_id=1, source_target_pairs={{0,8},{4,12},{8,0},{12,4},{16,24},{20,28},{24,16},{28,20},{1,9},{5... | collective-permute-start | bytes 196616 | tf_op jit(solution)/shard_map/ppermute | solution.py:424
  49.6 4.5 %collective-permute-start.8 = (f32[128,128]{1,0:T(8,128)S(1)}, f32[128,128]{1,0:T(8,128)S(1)}, u32[]{:S(2)}, u32[]{:S(2)}) collective-permute-start(f32[128,128]{1,0:T(8,128)S(1)} %add.19), channel_id=1, source_target_pairs={{0,4},{4,0},{8,12},{12,8},{16,20},{20,16},{24,28},{28,24},{1,5},{5... | collective-permute-start | bytes 196616 | tf_op jit(solution)/shard_map/ppermute | solution.py:424
  54.1 5.2 %collective-permute-start.11 = (f32[128,128]{1,0:T(8,128)S(1)}, f32[128,128]{1,0:T(8,128)S(1)}, u32[]{:S(2)}, u32[]{:S(2)}) collective-permute-start(f32[128,128]{1,0:T(8,128)S(1)} %add_add_fusion), channel_id=1, source_target_pairs={{0,16},{4,20},{8,24},{12,28},{16,0},{20,4},{24,8},{28,12},{1,17},{... | collective-permute-start | bytes 196616 | tf_op jit(solution)/shard_map/ppermute | solution.py:424

commit v4 on v3

--- a/solution.py
+++ b/solution.py
@@ -96,52 +96,49 @@
     count = ext - 2
     sel = lax.broadcasted_iota(jnp.int32, (8, 1), 0) == 7
     rim = edge_ref[5]
-    for col, ref in ((0, low_ref), (1, mid_ref), (2, high_ref)):
-        def prep(i, _):
+
+    def prep(i):
+        rowon = jnp.where(i < rim, edge_ref[3], jnp.where(i >= ext - rim, edge_ref[4], 1))
+        for col, ref in ((0, low_ref), (1, mid_ref), (2, high_ref)):
             st = ref[i]
-            rowon = jnp.where(i < rim, edge_ref[3], jnp.where(i >= ext - rim, edge_ref[4], 1))
             keep = (edge_ref[col] * rowon).astype(F32)
             _, a, b, c, _ = features(jnp.where(sel, st * keep, st))
             b0[col * ext + i] = a
             b1[col * ext + i] = b
             b2[col * ext + i] = c
-            return 0
-        lax.fori_loop(0, ext, prep, 0, unroll=2 if ext % 2 == 0 else 1)
+
+    for i in range(3):
+        prep(i)
     normrow = (lax.broadcasted_iota(jnp.int32, (24, 1), 0) == 4).astype(F32)
     skip = edge_ref[6]
 
-    def block(b, _):
+    def operands(b):
         st = mid_ref[b + 1]
         own, g_self, _, _, pressure = features(st)
         o1, o2, o3 = pieces(own)
         rhs = rows(o1, o1, o2, o2, o1, o3).astype(BF16)
+        gs = [g_self]
+        for n in range(codes_ref.shape[0]):
+            c = codes_ref[n, b + skip]
+            o = c + jnp.where(c >= 4, 1, 0)
+            ds1 = (o * 11) >> 5
+            dv1 = o - 3 * ds1
+            idx = dv1 * ext + b + ds1
+            tx = 2.0 * (ds1 - 1).astype(F32)
+            tz = 2.0 * (dv1 - 1).astype(F32)
+            gs.append(b0[idx] + tx * b1[idx] + tz * b2[idx] + normrow * (0.25 * (tx * tx + tz * tz)))
+        prep(jnp.minimum(b + 3, ext - 1))
         ns, fs = [], []
-        for n in range(codes_ref.shape[0] + 1):
-            if n == 0:
-                g = g_self
-            else:
-                c = codes_ref[n - 1, b + skip]
-                o = c + jnp.where(c >= 4, 1, 0)
-                ds1 = (o * 11) >> 5
-                dv1 = o - 3 * ds1
-                idx = dv1 * ext + b + ds1
-                tx = 2.0 * (ds1 - 1).astype(F32)
-                tz = 2.0 * (dv1 - 1).astype(F32)
-                g = b0[idx] + tx * b1[idx] + tz * b2[idx] + normrow * (0.25 * (tx * tx + tz * tz))
+        for g in gs:
             p1, p2, p3 = pieces(g[0:8])
-            f1, f2, f3 = pieces(g[8:24])
+            f1 = g[8:24].astype(BF16)
+            f2 = (g[8:24] - f1.astype(F32)).astype(BF16)
             ns.append(rows(p1, p2, p1, p2, p3, p1).astype(BF16))
-            fs.append(rows(f1, f2, f3).astype(BF16))
-        nall = jnp.concatenate(ns, axis=1)
-        f = jnp.concatenate(fs + fs, axis=1)
-        s = lax.dot_general(nall, rhs, (((0,), (0,)), ((), ())), preferred_element_type=F32)
-        s = jnp.maximum(s, 1e-20)
-        k = jnp.maximum(1.0 - s * lax.rsqrt(s), 0.0)
-        wgt = k * k * k
-        wh = wgt.astype(BF16)
-        wl = (wgt - wh.astype(F32)).astype(BF16)
-        acc = jnp.dot(f, jnp.concatenate([wh, wl], 0), preferred_element_type=F32)
-        t = acc[0:16] + acc[16:32] + acc[32:48]
+            fs.append(rows(f1, f2))
+        return st, pressure, rhs, jnp.concatenate(ns, axis=1), jnp.concatenate(fs + fs, axis=1)
+
+    def finish(b, st, pressure, acc):
+        t = acc[0:16] + acc[16:32]
         x, vel = st[0:3] - 1.0, st[3:6]
         coef = -5.0 * ALPHA_KERNEL
         sw, swx, swv, swf = t[0:1], t[1:4], t[4:7], t[7:8]
@@ -154,9 +151,26 @@
         rho = st[7:8]
         r2 = st[6:7] + TIME_STEP * dens / rho
         out_ref[b] = rows(pos2, vel2, r2, rho)
+
+    def blocks(i, _):
+        group = [operands(width * i + k) for k in range(width)]
+        zero = jnp.zeros_like(group[0][2])
+        rhs = rows(*[jnp.concatenate([g[2] if m == k else zero for m in range(width)], axis=1) for k, g in enumerate(group)])
+        nall = rows(*[g[3] for g in group])
+        s = lax.dot_general(nall, rhs, (((0,), (0,)), ((), ())), preferred_element_type=F32)
+        s = jnp.maximum(s, 1e-20)
+        k = jnp.maximum(1.0 - s * lax.rsqrt(s), 0.0)
+        wgt = k * k * k
+        wh = wgt.astype(BF16)
+        wl = (wgt - wh.astype(F32)).astype(BF16)
+        acc = jnp.dot(rows(*[g[4] for g in group]), rows(wh, wl), preferred_element_type=F32)
+        high, part = acc.shape[0] // width, zero.shape[1]
+        for k, g in enumerate(group):
+            finish(width * i + k, g[0], g[1], acc[high * k:high * (k + 1), part * k:part * (k + 1)])
         return 0
-    unroll = max(u for u in range(1, 18) if count % u == 0)
-    lax.fori_loop(0, count, block, 0, unroll=unroll)
+    width = 2 if count % 2 == 0 else 1
+    trips = count // width
+    lax.fori_loop(0, trips, blocks, 0, unroll=max(u for u in range(1, 18) if trips % u == 0))
 
 
 def step_scratch(ext, part):
@@ -278,6 +292,7 @@
 
 HIGHEST = lax.Precision.HIGHEST
 REPEAT_BELOW = 1e-5
+JOIN_ABOVE = 1e-4
 
 
 def gram_of(m):
@@ -362,14 +377,29 @@
     g = g_ref[...]
     low = (rows_in >= snaps - 2) & (cols_in < rows_in)
     g = jnp.where(low | (rows_in == cols_in) | ((rows_in < snaps - 2) & (cols_in < snaps - 2)), g, 0.0)
-    g_ref[...] = g + jnp.where(low, g, 0.0).T
+    trace = jnp.sum(jnp.where(rows_in == cols_in, g, 0.0), axis=(0, 1), keepdims=True)
+    g_ref[...] = (g + jnp.where(low, g, 0.0).T) * (1.0 / trace)
     q_ref[...] = b_ref[...]
 
+    def product(q):
+        return jnp.dot(q, g_ref[...], precision=HIGHEST, preferred_element_type=F32)
+
     def iterate(i, _):
-        repeated(jnp.dot(q_ref[...], g_ref[...], precision=HIGHEST, preferred_element_type=F32), q_ref)
+        repeated(product(q_ref[...]), q_ref)
         return 0
 
-    lax.fori_loop(0, iters, iterate, 0)
+    lax.fori_loop(0, iters - 2, iterate, 0)
+    q, worst = orthonormal(product(product(q_ref[...])))
+    good = worst >= JOIN_ABOVE
+
+    @pl.when(jnp.logical_not(good))
+    def _():
+        lax.fori_loop(iters - 2, iters, iterate, 0)
+
+    @pl.when(good)
+    def _():
+        q_ref[...] = q
+
     q = q_ref[...]
     last = (lax.broadcasted_iota(jnp.int32, (1, snaps), 1) == snaps - 1).astype(F32)
     w = jnp.zeros((1, snaps), F32)

time: 70.6 us -> 66 us (0.935)
  Pallas kernels: 37.7 us -> 33.2 us
    pallas_call x1, Pallas kernels: 11.1 us -> 9.19 us  [filtered_field(): pl.pallas_call(kernel, out_shape=jax.ShapeDtypeStruct((count * comps, par...]
    pallas_call x1, Pallas kernels: 8.64 us -> 7.26 us  [first_step(): pl.pallas_call(step_blocks, out_shape=jax.ShapeDtypeStruct((ext - 2, 8, p...]
    pallas_call x1, Pallas kernels: 9.59 us -> 8.29 us  [second_step(): pl.pallas_call(kernel, out_shape=(jax.ShapeDtypeStruct((count * 7, part),...]
  transfers between devices with their start and end apart: 12 -> 12, of which waited for: 9 -> 9; matrix products, arithmetic and copies ran while one was open for 0% -> 0% of each run, Pallas kernels for 9% -> 10%
where the time goes in v4:
time: 66 us; the launch traced here: 65.9 us
  Pallas kernels  33.2 us (50%)
  waiting for transfers between devices  17.1 us (26%)
  starting transfers between devices  14.5 us (22%)
  between operations  0.74 us (1%)
    ppermute x6, waiting for transfers between devices, exchange(): total = total + lax.ppermute(x, axis, [(i, i ^ m) for i in range(count)])  9.58 us
    pallas_call x1, Pallas kernels, filtered_field(): pl.pallas_call(kernel, out_shape=jax.ShapeDtypeStruct((count * comps, par...  9.19 us
    pallas_call x1, Pallas kernels, second_step(): pl.pallas_call(kernel, out_shape=(jax.ShapeDtypeStruct((count * 7, part),...  8.29 us
    ppermute x6, waiting for transfers between devices, shift(): return lax.ppermute(x, axis, [(i, (i + by) % count) for i in range(count)])  7.57 us
    ppermute x6, starting transfers between devices, shift(): return lax.ppermute(x, axis, [(i, (i + by) % count) for i in range(count)])  7.32 us
    pallas_call x1, Pallas kernels, first_step(): pl.pallas_call(step_blocks, out_shape=jax.ShapeDtypeStruct((ext - 2, 8, p...  7.26 us
    ppermute x6, starting transfers between devices, exchange(): total = total + lax.ppermute(x, axis, [(i, i ^ m) for i in range(count)])  7.16 us
    pallas_call x1, Pallas kernels, start_basis(): pl.pallas_call(kernel, out_shape=jax.ShapeDtypeStruct(basis_t.shape, F32)...  3.42 us
  transfers between devices with their start and end apart: 12, of which 9 were waited for; matrix products, arithmetic and copies ran while one was open for 0% of the time, Pallas kernels for 10%

profile of v4, /device:TPU:0, one launch (start us, length us, event | category | flops | bytes accessed | tf_op | source)
XLA Modules:
  0.0 65.9 jit_solution(11117589166241607812)
XLA Ops:
  0.6 0.0 copy-start.3
  0.6 0.0 copy-start
  0.7 1.8 %shard_map.68 = (f32[32,8,128]{2,1,0:T(8,128)}, f32[3,8,128]{2,1,0:T(8,128)}, f32[3,8,128]{2,1,0:T(8,128)}) custom-call(f32[224,128]{1,0:T(8,128)} %bitcast.22, s32[32,128]{1,0:T(8,128)} %bitcast.24, s32[4,32]{1,0:T(4,128)} %bitcast.25), custom_call_target="tpu_custom_call" | custom-call | tf_op jit(solution)/shard_map/pallas_call | solution.py:86
  2.4 0.0 copy-start.2
  2.4 3.0 %collective-permute-start = (f32[3,8,128]{2,1,0:T(8,128)}, f32[3,8,128]{2,1,0:T(8,128)S(1)}, u32[]{:S(2)}, u32[]{:S(2)}) collective-permute-start(f32[3,8,128]{2,1,0:T(8,128)} %get-tuple-element.10), channel_id=1, source_target_pairs={{0,4},{4,8},{8,12},{12,16},{16,20},{20,24},{24,28},{28,0},{1,5},{5... | collective-permute-start | bytes 36872 | tf_op jit(solution)/shard_map/ppermute | solution.py:444
  5.4 3.1 %collective-permute-start.1 = (f32[3,8,128]{2,1,0:T(8,128)}, f32[3,8,128]{2,1,0:T(8,128)S(1)}, u32[]{:S(2)}, u32[]{:S(2)}) collective-permute-start(f32[3,8,128]{2,1,0:T(8,128)} %get-tuple-element.11), channel_id=1, source_target_pairs={{0,28},{4,0},{8,4},{12,8},{16,12},{20,16},{24,20},{28,24},{1,29},{... | collective-permute-start | bytes 36872 | tf_op jit(solution)/shard_map/ppermute | solution.py:444
  8.5 3.4 %shard_map.69.b_ref = f32[64,128]{1,0:T(8,128)} custom-call(f32[64,128]{1,0:T(8,128)} %bitcast.28), custom_call_target="tpu_custom_call" | custom-call | flops 1073741824 | bytes 1048576 | tf_op jit(solution)/shard_map/pallas_call | solution.py:367
  11.9 0.1 stack.43.edge_ref
  12.0 0.0 collective-permute-done
  12.0 0.0 collective-permute-done.1
  12.0 0.0 copy-done.2
  12.0 0.7 %collective-permute-start.3 = (f32[36,8,128]{2,1,0:T(8,128)S(1)}, f32[36,8,128]{2,1,0:T(8,128)S(1)}, u32[]{:S(2)}, u32[]{:S(2)}) collective-permute-start(f32[36,8,128]{2,1,0:T(8,128)S(1)} %pad_maximum_fusion.mid_ref), channel_id=1, source_target_pairs={{0,3},{1,0},{2,1},{3,2},{4,7},{5,4},{6,5},{7,6},{8,11},{9,8},{10,9... | collective-permute-start | bytes 442376 | tf_op jit(solution)/shard_map/ppermute | solution.py:444
  12.7 0.0 collective-permute-start.2
  12.8 0.0 copy-done.3
  12.8 0.1 pad_add_fusion.codes_ref
  12.8 3.8 %collective-permute-done.3.high_ref = f32[36,8,128]{2,1,0:T(8,128)S(1)} collective-permute-done((f32[36,8,128]{2,1,0:T(8,128)S(1)}, f32[36,8,128]{2,1,0:T(8,128)S(1)}, u32[]{:S(2)}, u32[]{:S(2)}) %collective-permute-start.3) | collective-permute-done | bytes 147488 | tf_op jit(solution)/shard_map/ppermute | solution.py:444
  16.6 1.8 %collective-permute-done.2.low_ref = f32[36,8,128]{2,1,0:T(8,128)S(1)} collective-permute-done((f32[36,8,128]{2,1,0:T(8,128)S(1)}, f32[36,8,128]{2,1,0:T(8,128)S(1)}, u32[]{:S(2)}, u32[]{:S(2)}) %collective-permute-start.2) | collective-permute-done | bytes 147488 | tf_op jit(solution)/shard_map/ppermute | solution.py:444
  18.4 7.3 %shard_map.70.first_ref.mid_ref = f32[34,8,128]{2,1,0:T(8,128)S(1)} custom-call(s32[4,34]{1,0:T(4,128)S(1)} %pad_add_fusion.codes_ref, s32[8]{0:T(128)S(1)} %stack.43.edge_ref, f32[36,8,128]{2,1,0:T(8,128)S(1)} %collective-permute-done.2.low_ref, f32[36,8,128]{2,1,0:T(8,128)S(1)} %pad_maximum_fusion.mid_ref, f32[36,8,128]{2,1,0:T(8,128)S(1)} %collective-permute-done.3.high_ref), custom_call_target="tpu_custom_call" | custom-call | tf_op jit(solution)/shard_map/pallas_call | solution.py:184
  25.7 0.5 collective-permute-start.5
  26.1 0.1 collective-permute-start.4
  26.2 0.1 stack.42.edge_ref
  26.3 0.0 copy-done
  26.3 0.0 copy-start.1
  26.3 3.2 %shard_map.71.gram_ref = f32[128,128]{1,0:T(8,128)S(1)} custom-call(bf16[3,126,32,128]{3,2,1,0:T(8,128)(2,1)S(1)} %bitcast.19, f32[34,8,128]{2,1,0:T(8,128)S(1)} %shard_map.70.first_ref.mid_ref), custom_call_target="tpu_custom_call" | custom-call | flops 402653184 | bytes 3145728 | tf_op jit(solution)/shard_map/pallas_call | solution.py:283
  29.6 0.3 collective-permute-done.5.high_ref
  29.9 1.7 %collective-permute-done.4.low_ref = f32[34,8,128]{2,1,0:T(8,128)S(1)} collective-permute-done((f32[34,8,128]{2,1,0:T(8,128)S(1)}, f32[34,8,128]{2,1,0:T(8,128)S(1)}, u32[]{:S(2)}, u32[]{:S(2)}) %collective-permute-start.4) | collective-permute-done | bytes 139296 | tf_op jit(solution)/shard_map/ppermute | solution.py:444
  31.6 8.3 %shard_map.72 = (f32[224,128]{1,0:T(8,128)}, f32[32,8,128]{2,1,0:T(8,128)S(1)}, f32[128,128]{1,0:T(8,128)S(1)}) custom-call(s32[4,34]{1,0:T(4,128)S(1)} %pad_add_fusion.codes_ref, s32[8]{0:T(128)S(1)} %stack.42.edge_ref, f32[34,8,128]{2,1,0:T(8,128)S(1)} %collective-permute-done.4.low_ref, f32[34,8,128]{2,1,0:T(8,128)S(1)} %shard_map.70.first_ref.mid_ref, ...), custom_call_target="tpu_custom_call" | custom-call | tf_op jit(solution)/shard_map/pallas_call | solution.py:251
  39.9 0.0 collective-permute-start.6
  39.9 1.3 %collective-permute-done.6 = f32[128,128]{1,0:T(8,128)S(1)} collective-permute-done((f32[128,128]{1,0:T(8,128)S(1)}, f32[128,128]{1,0:T(8,128)S(1)}, u32[]{:S(2)}, u32[]{:S(2)}) %collective-permute-start.6) | collective-permute-done | bytes 65568 | tf_op jit(solution)/shard_map/ppermute | solution.py:454
  41.1 1.2 %collective-permute-start.7 = (f32[128,128]{1,0:T(8,128)S(1)}, f32[128,128]{1,0:T(8,128)S(1)}, u32[]{:S(2)}, u32[]{:S(2)}) collective-permute-start(f32[128,128]{1,0:T(8,128)S(1)} %add.18), channel_id=1, source_target_pairs={{0,2},{1,3},{2,0},{3,1},{4,6},{5,7},{6,4},{7,5},{8,10},{9,11},{10,... | collective-permute-start | bytes 196616 | tf_op jit(solution)/shard_map/ppermute | solution.py:454
  42.3 3.1 %collective-permute-done.7 = f32[128,128]{1,0:T(8,128)S(1)} collective-permute-done((f32[128,128]{1,0:T(8,128)S(1)}, f32[128,128]{1,0:T(8,128)S(1)}, u32[]{:S(2)}, u32[]{:S(2)}) %collective-permute-start.7) | collective-permute-done | bytes 65568 | tf_op jit(solution)/shard_map/ppermute | solution.py:454
  45.5 1.0 %collective-permute-start.10 = (f32[128,128]{1,0:T(8,128)S(1)}, f32[128,128]{1,0:T(8,128)S(1)}, u32[]{:S(2)}, u32[]{:S(2)}) collective-permute-start(f32[128,128]{1,0:T(8,128)S(1)} %add.19), channel_id=1, source_target_pairs={{0,12},{4,8},{8,4},{12,0},{16,28},{20,24},{24,20},{28,16},{1,13},{... | collective-permute-start | bytes 196616 | tf_op jit(solution)/shard_map/ppermute | solution.py:454
  46.5 0.4 collective-permute-start.9
  46.9 2.1 %collective-permute-start.8 = (f32[128,128]{1,0:T(8,128)S(1)}, f32[128,128]{1,0:T(8,128)S(1)}, u32[]{:S(2)}, u32[]{:S(2)}) collective-permute-start(f32[128,128]{1,0:T(8,128)S(1)} %add.19), channel_id=1, source_target_pairs={{0,4},{4,0},{8,12},{12,8},{16,20},{20,16},{24,28},{28,24},{1,5},{5... | collective-permute-start | bytes 196616 | tf_op jit(solution)/shard_map/ppermute | solution.py:454
  49.0 1.7 %collective-permute-done.10 = f32[128,128]{1,0:T(8,128)S(1)} collective-permute-done((f32[128,128]{1,0:T(8,128)S(1)}, f32[128,128]{1,0:T(8,128)S(1)}, u32[]{:S(2)}, u32[]{:S(2)}) %collective-permute-start.10) | collective-permute-done | bytes 65568 | tf_op jit(solution)/shard_map/ppermute | solution.py:454
  50.7 0.0 collective-permute-done.9
  50.7 0.7 %collective-permute-done.8 = f32[128,128]{1,0:T(8,128)S(1)} collective-permute-done((f32[128,128]{1,0:T(8,128)S(1)}, f32[128,128]{1,0:T(8,128)S(1)}, u32[]{:S(2)}, u32[]{:S(2)}) %collective-permute-start.8) | collective-permute-done | bytes 65568 | tf_op jit(solution)/shard_map/ppermute | solution.py:454
  51.4 2.4 %collective-permute-start.11 = (f32[128,128]{1,0:T(8,128)S(1)}, f32[128,128]{1,0:T(8,128)S(1)}, u32[]{:S(2)}, u32[]{:S(2)}) collective-permute-start(f32[128,128]{1,0:T(8,128)S(1)} %add_add_fusion), channel_id=1, source_target_pairs={{0,16},{4,20},{8,24},{12,28},{16,0},{20,4},{24,8},{28,12},{1,17},{... | collective-permute-start | bytes 196616 | tf_op jit(solution)/shard_map/ppermute | solution.py:454
  53.8 2.8 %collective-permute-done.11 = f32[128,128]{1,0:T(8,128)S(1)} collective-permute-done((f32[128,128]{1,0:T(8,128)S(1)}, f32[128,128]{1,0:T(8,128)S(1)}, u32[]{:S(2)}, u32[]{:S(2)}) %collective-permute-start.11) | collective-permute-done | bytes 65568 | tf_op jit(solution)/shard_map/ppermute | solution.py:454
  56.7 0.0 copy-done.1
  56.7 9.2 %shard_map.73 = f32[96,128]{1,0:T(8,128)} custom-call(f32[128,128]{1,0:T(8,128)S(1)} %add.23.gram_ref, f32[64,128]{1,0:T(8,128)S(1)} %copy-done.1, bf16[3,126,32,128]{3,2,1,0:T(8,128)(2,1)S(1)} %bitcast.21, f32[34,8,128]{2,1,0:T(8,128)S(1)} %shard_map.70.first_ref.mid_ref, f32[32,8,128]{2,1,0:T(8,128)S(1)} %get-tuple-element.17.second_ref), custom_call_target="tpu_custom_call" | custom-call | tf_op jit(solution)/shard_map/pallas_call | solution.py:433
  (10 shorter events, 0.1 us)
Async XLA Ops:
  0.6 12.1 %copy-start.3 = (s32[32,1,4]{0,2,1:T(4,128)S(1)}, s32[32,1,4]{0,2,1:T(4,128)}, u32[]{:S(2)}) copy-start(s32[32,1,4]{0,2,1:T(4,128)} %param.7) | copy-start | bytes 1540
  0.6 25.7 %copy-start = (bf16[32,1,3,126,128]{4,0,3,2,1:T(8,128)(2,1)S(1)}, bf16[32,1,3,126,128]{4,0,3,2,1:T(8,128)(2,1)}, u32[]{:S(2)}) copy-start(bf16[32,1,3,126,128]{4,0,3,2,1:T(8,128)(2,1)} %param.8) | copy-start | bytes 9289732
  2.4 9.6 %copy-start.2 = (f32[32,8,128]{2,1,0:T(8,128)S(1)}, f32[32,8,128]{2,1,0:T(8,128)}, u32[]{:S(2)}) copy-start(f32[32,8,128]{2,1,0:T(8,128)} %get-tuple-element.13) | copy-start | bytes 393220
  2.4 9.6 %collective-permute-start = (f32[3,8,128]{2,1,0:T(8,128)}, f32[3,8,128]{2,1,0:T(8,128)S(1)}, u32[]{:S(2)}, u32[]{:S(2)}) collective-permute-start(f32[3,8,128]{2,1,0:T(8,128)} %get-tuple-element.10), channel_id=1, source_target_pairs={{0,4},{4,8},{8,12},{12,16},{16,20},{20,24},{24,28},{28,0},{1,5},{5... | collective-permute-start | bytes 36872 | tf_op jit(solution)/shard_map/ppermute | solution.py:444
  5.4 6.6 %collective-permute-start.1 = (f32[3,8,128]{2,1,0:T(8,128)}, f32[3,8,128]{2,1,0:T(8,128)S(1)}, u32[]{:S(2)}, u32[]{:S(2)}) collective-permute-start(f32[3,8,128]{2,1,0:T(8,128)} %get-tuple-element.11), channel_id=1, source_target_pairs={{0,28},{4,0},{8,4},{12,8},{16,12},{20,16},{24,20},{28,24},{1,29},{... | collective-permute-start | bytes 36872 | tf_op jit(solution)/shard_map/ppermute | solution.py:444
  12.0 4.6 %collective-permute-start.3 = (f32[36,8,128]{2,1,0:T(8,128)S(1)}, f32[36,8,128]{2,1,0:T(8,128)S(1)}, u32[]{:S(2)}, u32[]{:S(2)}) collective-permute-start(f32[36,8,128]{2,1,0:T(8,128)S(1)} %pad_maximum_fusion.mid_ref), channel_id=1, source_target_pairs={{0,3},{1,0},{2,1},{3,2},{4,7},{5,4},{6,5},{7,6},{8,11},{9,8},{10,9... | collective-permute-start | bytes 442376 | tf_op jit(solution)/shard_map/ppermute | solution.py:444
  12.7 5.7 %collective-permute-start.2 = (f32[36,8,128]{2,1,0:T(8,128)S(1)}, f32[36,8,128]{2,1,0:T(8,128)S(1)}, u32[]{:S(2)}, u32[]{:S(2)}) collective-permute-start(f32[36,8,128]{2,1,0:T(8,128)S(1)} %pad_maximum_fusion.mid_ref), channel_id=1, source_target_pairs={{0,1},{1,2},{2,3},{3,0},{4,5},{5,6},{6,7},{7,4},{8,9},{9,10},{10,1... | collective-permute-start | bytes 442376 | tf_op jit(solution)/shard_map/ppermute | solution.py:444
  25.7 4.2 %collective-permute-start.5 = (f32[34,8,128]{2,1,0:T(8,128)S(1)}, f32[34,8,128]{2,1,0:T(8,128)S(1)}, u32[]{:S(2)}, u32[]{:S(2)}) collective-permute-start(f32[34,8,128]{2,1,0:T(8,128)S(1)} %shard_map.70.first_ref.mid_ref), channel_id=1, source_target_pairs={{0,3},{1,0},{2,1},{3,2},{4,7},{5,4},{6,5},{7,6},{8,11},{9,8},{10,9... | collective-permute-start | bytes 417800 | tf_op jit(solution)/shard_map/ppermute | solution.py:444
  26.1 5.4 %collective-permute-start.4 = (f32[34,8,128]{2,1,0:T(8,128)S(1)}, f32[34,8,128]{2,1,0:T(8,128)S(1)}, u32[]{:S(2)}, u32[]{:S(2)}) collective-permute-start(f32[34,8,128]{2,1,0:T(8,128)S(1)} %shard_map.70.first_ref.mid_ref), channel_id=1, source_target_pairs={{0,1},{1,2},{2,3},{3,0},{4,5},{5,6},{6,7},{7,4},{8,9},{9,10},{10,1... | collective-permute-start | bytes 417800 | tf_op jit(solution)/shard_map/ppermute | solution.py:444
  26.3 30.3 %copy-start.1 = (f32[64,128]{1,0:T(8,128)S(1)}, f32[64,128]{1,0:T(8,128)}, u32[]{:S(2)}) copy-start(f32[64,128]{1,0:T(8,128)} %shard_map.69.b_ref) | copy-start | bytes 98308
  39.9 1.3 %collective-permute-start.6 = (f32[128,128]{1,0:T(8,128)S(1)}, f32[128,128]{1,0:T(8,128)S(1)}, u32[]{:S(2)}, u32[]{:S(2)}) collective-permute-start(f32[128,128]{1,0:T(8,128)S(1)} %get-tuple-element.15), channel_id=1, source_target_pairs={{0,1},{1,0},{2,3},{3,2},{4,5},{5,4},{6,7},{7,6},{8,9},{9,8},{10,11... | collective-permute-start | bytes 196616 | tf_op jit(solution)/shard_map/ppermute | solution.py:454
  41.1 4.3 %collective-permute-start.7 = (f32[128,128]{1,0:T(8,128)S(1)}, f32[128,128]{1,0:T(8,128)S(1)}, u32[]{:S(2)}, u32[]{:S(2)}) collective-permute-start(f32[128,128]{1,0:T(8,128)S(1)} %add.18), channel_id=1, source_target_pairs={{0,2},{1,3},{2,0},{3,1},{4,6},{5,7},{6,4},{7,5},{8,10},{9,11},{10,... | collective-permute-start | bytes 196616 | tf_op jit(solution)/shard_map/ppermute | solution.py:454
  45.5 5.2 %collective-permute-start.10 = (f32[128,128]{1,0:T(8,128)S(1)}, f32[128,128]{1,0:T(8,128)S(1)}, u32[]{:S(2)}, u32[]{:S(2)}) collective-permute-start(f32[128,128]{1,0:T(8,128)S(1)} %add.19), channel_id=1, source_target_pairs={{0,12},{4,8},{8,4},{12,0},{16,28},{20,24},{24,20},{28,16},{1,13},{... | collective-permute-start | bytes 196616 | tf_op jit(solution)/shard_map/ppermute | solution.py:454
  46.5 4.3 %collective-permute-start.9 = (f32[128,128]{1,0:T(8,128)S(1)}, f32[128,128]{1,0:T(8,128)S(1)}, u32[]{:S(2)}, u32[]{:S(2)}) collective-permute-start(f32[128,128]{1,0:T(8,128)S(1)} %add.19), channel_id=1, source_target_pairs={{0,8},{4,12},{8,0},{12,4},{16,24},{20,28},{24,16},{28,20},{1,9},{5... | collective-permute-start | bytes 196616 | tf_op jit(solution)/shard_map/ppermute | solution.py:454
  46.9 4.5 %collective-permute-start.8 = (f32[128,128]{1,0:T(8,128)S(1)}, f32[128,128]{1,0:T(8,128)S(1)}, u32[]{:S(2)}, u32[]{:S(2)}) collective-permute-start(f32[128,128]{1,0:T(8,128)S(1)} %add.19), channel_id=1, source_target_pairs={{0,4},{4,0},{8,12},{12,8},{16,20},{20,16},{24,28},{28,24},{1,5},{5... | collective-permute-start | bytes 196616 | tf_op jit(solution)/shard_map/ppermute | solution.py:454
  51.4 5.2 %collective-permute-start.11 = (f32[128,128]{1,0:T(8,128)S(1)}, f32[128,128]{1,0:T(8,128)S(1)}, u32[]{:S(2)}, u32[]{:S(2)}) collective-permute-start(f32[128,128]{1,0:T(8,128)S(1)} %add_add_fusion), channel_id=1, source_target_pairs={{0,16},{4,20},{8,24},{12,28},{16,0},{20,4},{24,8},{28,12},{1,17},{... | collective-permute-start | bytes 196616 | tf_op jit(solution)/shard_map/ppermute | solution.py:454

commit v5 on v4

--- a/solution.py
+++ b/solution.py
@@ -91,7 +91,64 @@
     )(particles.reshape(count * fields, part), flags, codes)
 
 
-def step_blocks(codes_ref, edge_ref, low_ref, mid_ref, high_ref, out_ref, b0, b1, b2):
+def own_side(own):
+    o1, o2, o3 = pieces(own)
+    return rows(o1, o1, o2, o2, o1, o3).astype(BF16)
+
+
+def near_side(g):
+    p1, p2, p3 = pieces(g[0:8])
+    f1 = g[8:24].astype(BF16)
+    f2 = (g[8:24] - f1.astype(F32)).astype(BF16)
+    return rows(p1, p2, p1, p2, p3, p1).astype(BF16), rows(f1, f2)
+
+
+def weighted_sums(group):
+    width = len(group)
+    zero = jnp.zeros_like(group[0][0])
+    rhs = rows(*[jnp.concatenate([g[0] if m == k else zero for m in range(width)], axis=1) for k, g in enumerate(group)])
+    s = lax.dot_general(rows(*[g[1] for g in group]), rhs, (((0,), (0,)), ((), ())), preferred_element_type=F32)
+    s = jnp.maximum(s, 1e-20)
+    k = jnp.maximum(1.0 - s * lax.rsqrt(s), 0.0)
+    wgt = k * k * k
+    wh = wgt.astype(BF16)
+    wl = (wgt - wh.astype(F32)).astype(BF16)
+    f = rows(*[jnp.concatenate([g[2], g[2]], axis=1) for g in group])
+    acc = jnp.dot(f, rows(wh, wl), preferred_element_type=F32)
+    part = zero.shape[1]
+    cut = [acc[32 * k:32 * (k + 1), part * k:part * (k + 1)] for k in range(width)]
+    return [t[0:16] + t[16:32] for t in cut]
+
+
+def in_groups(count, run):
+    width = 2 if count % 2 == 0 else 1
+    trips = count // width
+
+    def trip(i, _):
+        run([width * i + k for k in range(width)])
+        return 0
+    lax.fori_loop(0, trips, trip, 0, unroll=max(u for u in range(1, 18) if trips % u == 0))
+
+
+def inner_part(state_ref, skip, self_ref, side_ref):
+    def run(blocks):
+        group = []
+        for b in blocks:
+            own, g_self, _, _, pressure = features(state_ref[b + skip])
+            side = own_side(own)
+            side_ref[b] = side
+            self_ref[b, 16:24] = spread(pressure)
+            group.append((side,) + near_side(g_self))
+        for b, t in zip(blocks, weighted_sums(group)):
+            self_ref[b, 0:16] = t
+    in_groups(self_ref.shape[0], run)
+
+
+def inner_shapes(count, part):
+    return (jax.ShapeDtypeStruct((count, 24, part), F32), jax.ShapeDtypeStruct((count, 48, part), BF16))
+
+
+def step_blocks(codes_ref, edge_ref, low_ref, mid_ref, high_ref, self_ref, side_ref, out_ref, b0, b1, b2):
     ext = mid_ref.shape[0]
     count = ext - 2
     sel = lax.broadcasted_iota(jnp.int32, (8, 1), 0) == 7
@@ -114,10 +171,7 @@
 
     def operands(b):
         st = mid_ref[b + 1]
-        own, g_self, _, _, pressure = features(st)
-        o1, o2, o3 = pieces(own)
-        rhs = rows(o1, o1, o2, o2, o1, o3).astype(BF16)
-        gs = [g_self]
+        gs = []
         for n in range(codes_ref.shape[0]):
             c = codes_ref[n, b + skip]
             o = c + jnp.where(c >= 4, 1, 0)
@@ -128,17 +182,10 @@
             tz = 2.0 * (dv1 - 1).astype(F32)
             gs.append(b0[idx] + tx * b1[idx] + tz * b2[idx] + normrow * (0.25 * (tx * tx + tz * tz)))
         prep(jnp.minimum(b + 3, ext - 1))
-        ns, fs = [], []
-        for g in gs:
-            p1, p2, p3 = pieces(g[0:8])
-            f1 = g[8:24].astype(BF16)
-            f2 = (g[8:24] - f1.astype(F32)).astype(BF16)
-            ns.append(rows(p1, p2, p1, p2, p3, p1).astype(BF16))
-            fs.append(rows(f1, f2))
-        return st, pressure, rhs, jnp.concatenate(ns, axis=1), jnp.concatenate(fs + fs, axis=1)
-
-    def finish(b, st, pressure, acc):
-        t = acc[0:16] + acc[16:32]
+        near = [near_side(g) for g in gs]
+        return st, (side_ref[b],) + tuple(jnp.concatenate(x, axis=1) for x in zip(*near))
+
+    def finish(b, st, pressure, t):
         x, vel = st[0:3] - 1.0, st[3:6]
         coef = -5.0 * ALPHA_KERNEL
         sw, swx, swv, swf = t[0:1], t[1:4], t[4:7], t[7:8]
@@ -152,41 +199,27 @@
         r2 = st[6:7] + TIME_STEP * dens / rho
         out_ref[b] = rows(pos2, vel2, r2, rho)
 
-    def blocks(i, _):
-        group = [operands(width * i + k) for k in range(width)]
-        zero = jnp.zeros_like(group[0][2])
-        rhs = rows(*[jnp.concatenate([g[2] if m == k else zero for m in range(width)], axis=1) for k, g in enumerate(group)])
-        nall = rows(*[g[3] for g in group])
-        s = lax.dot_general(nall, rhs, (((0,), (0,)), ((), ())), preferred_element_type=F32)
-        s = jnp.maximum(s, 1e-20)
-        k = jnp.maximum(1.0 - s * lax.rsqrt(s), 0.0)
-        wgt = k * k * k
-        wh = wgt.astype(BF16)
-        wl = (wgt - wh.astype(F32)).astype(BF16)
-        acc = jnp.dot(rows(*[g[4] for g in group]), rows(wh, wl), preferred_element_type=F32)
-        high, part = acc.shape[0] // width, zero.shape[1]
-        for k, g in enumerate(group):
-            finish(width * i + k, g[0], g[1], acc[high * k:high * (k + 1), part * k:part * (k + 1)])
-        return 0
-    width = 2 if count % 2 == 0 else 1
-    trips = count // width
-    lax.fori_loop(0, trips, blocks, 0, unroll=max(u for u in range(1, 18) if trips % u == 0))
+    def run(blocks):
+        group = [operands(b) for b in blocks]
+        for b, (st, _), t in zip(blocks, group, weighted_sums([g[1] for g in group])):
+            finish(b, st, self_ref[b, 16:17], t + self_ref[b, 0:16])
+    in_groups(count, run)
 
 
 def step_scratch(ext, part):
     return [pltpu.VMEM((3 * ext, 24, part), F32)] * 3
 
 
-def first_step(codes, edges, low, mid, high):
+def first_step(codes, edges, low, mid, high, inner):
     ext, _, part = mid.shape
     v = pl.BlockSpec(memory_space=pltpu.VMEM)
     sm = pl.BlockSpec(memory_space=pltpu.SMEM)
     return pl.pallas_call(
         step_blocks, out_shape=jax.ShapeDtypeStruct((ext - 2, 8, part), F32),
-        in_specs=[sm, sm, v, v, v], out_specs=v,
+        in_specs=[sm, sm, v, v, v, v, v], out_specs=v,
         scratch_shapes=step_scratch(ext, part),
         compiler_params=pltpu.CompilerParams(vmem_limit_bytes=VMEM_LIMIT),
-    )(codes, edges, low, mid, high)
+    )(codes, edges, low, mid, high, *inner)
 
 
 def cross_row(hist_ref, new, others, terms):
@@ -230,16 +263,16 @@
     return [flat[pl.ds(3 + c, count, stride=8), :].astype(BF16).astype(F32) for c in range(3)]
 
 
-def second_step(codes, edges, low, mid, high, hist, gram):
+def second_step(codes, edges, low, mid, high, inner, hist, gram):
     ext, _, part = mid.shape
     count = ext - 2
     snaps = gram.shape[0]
     v = pl.BlockSpec(memory_space=pltpu.VMEM)
     sm = pl.BlockSpec(memory_space=pltpu.SMEM)
 
-    def kernel(codes_ref, edge_ref, low_ref, mid_ref, high_ref, hist_ref, gram_ref, new_ref, state_ref, gram_out,
+    def kernel(codes_ref, edge_ref, low_ref, mid_ref, high_ref, self_ref, side_ref, hist_ref, gram_ref, new_ref, state_ref, gram_out,
                b0, b1, b2, flat, terms):
-        step_blocks(codes_ref, edge_ref, low_ref, mid_ref, high_ref, state_ref, b0, b1, b2)
+        step_blocks(codes_ref, edge_ref, low_ref, mid_ref, high_ref, self_ref, side_ref, state_ref, b0, b1, b2)
         first = load_new(mid_ref, 1, count, flat)
         second = load_new(state_ref, 0, count, flat)
         for i in range(7):
@@ -252,11 +285,25 @@
         kernel,
         out_shape=(jax.ShapeDtypeStruct((count * 7, part), F32), jax.ShapeDtypeStruct((count, 8, part), F32),
                    jax.ShapeDtypeStruct((snaps, snaps), F32)),
-        in_specs=[sm, sm, v, v, v, v, v], out_specs=(v, v, v),
+        in_specs=[sm, sm] + [v] * 7, out_specs=(v, v, v),
         scratch_shapes=step_scratch(ext, part) + [
             pltpu.VMEM((count * 8, part), F32), pltpu.VMEM((snaps * 8, part), F32)],
         compiler_params=pltpu.CompilerParams(vmem_limit_bytes=VMEM_LIMIT),
-    )(codes, edges, low, mid, high, hist, gram)
+    )(codes, edges, low, mid, high, *inner, hist, gram)
+
+
+def inner_sums(mid):
+    count, _, part = mid.shape
+    v = pl.BlockSpec(memory_space=pltpu.VMEM)
+
+    def kernel(mid_ref, self_ref, side_ref):
+        inner_part(mid_ref, 1, self_ref, side_ref)
+
+    return pl.pallas_call(
+        kernel, out_shape=inner_shapes(count - 2, part), in_specs=[v], out_specs=(v, v),
+        compiler_params=pltpu.CompilerParams(vmem_limit_bytes=VMEM_LIMIT),
+        cost_estimate=pl.CostEstimate(flops=1 << 30, bytes_accessed=1 << 20, transcendentals=0),
+    )(mid)
 
 
 def early_gram(hist, first):
@@ -444,26 +491,22 @@
     return lax.ppermute(x, axis, [(i, (i + by) % count) for i in range(count)])
 
 
-def exchange(x, axis, bits):
-    count = lax.axis_size(axis)
-    masks = [0]
-    for bit in bits:
-        masks = masks + [m ^ bit for m in masks]
-    total = x
-    for m in masks[1:]:
-        total = total + lax.ppermute(x, axis, [(i, i ^ m) for i in range(count)])
-    return total
-
-
 def reduce_all(x):
-    for axis, together in (("vert", 1), ("stream", 2)):
-        count = lax.axis_size(axis)
-        if count & (count - 1):
-            x = lax.psum(x, axis)
-            continue
-        bits = [1 << k for k in range(count.bit_length() - 1)]
-        for k in range(0, len(bits), together):
-            x = exchange(x, axis, bits[k:k + together])
+    axes = ("stream", "vert")
+    sizes = [lax.axis_size(a) for a in axes]
+    if any(n & (n - 1) for n in sizes):
+        return lax.psum(x, axes)
+    bits = [(0, 1 << k) for k in range(sizes[1].bit_length() - 1)] + [(1 << k, 0) for k in range(sizes[0].bit_length() - 1)]
+    start = len(bits) % 2
+    for group in [bits[0:start]] * start + [bits[k:k + 2] for k in range(start, len(bits), 2)]:
+        masks = [(0, 0)]
+        for s, v in group:
+            masks = masks + [(a ^ s, b ^ v) for a, b in masks]
+        total = x
+        for s, v in masks[1:]:
+            total = total + lax.ppermute(x, axes, [
+                (i * sizes[1] + j, (i ^ s) * sizes[1] + (j ^ v)) for i in range(sizes[0]) for j in range(sizes[1])])
+        x = total
     return x
 
 
@@ -487,10 +530,11 @@
     low_mid, high_mid = shift(mid, "vert", 1), shift(mid, "vert", -1)
     basis = start_basis(basis_start.T)
     wide_codes, basis = lax.optimization_barrier((wide_codes, basis))
-    first = first_step(wide_codes, edges1, low_mid, mid, high_mid)
+    first = first_step(wide_codes, edges1, low_mid, mid, high_mid, inner_sums(mid))
     low, high = shift(first, "vert", 1), shift(first, "vert", -1)
+    inner = inner_sums(first)
     gram = early_gram(hist, first)
-    new_state, second, gram = second_step(wide_codes, edges2, low, first, high, hist, gram)
+    new_state, second, gram = second_step(wide_codes, edges2, low, first, high, inner, hist, gram)
     gram = reduce_all(gram)
     out = filtered_field(gram, basis, hist, first, second)
     return (new_state.reshape(count, 1, 7, -1), out.reshape(count, 1, 3, -1))

time: 66 us -> 63.5 us (0.962)
  waiting for transfers between devices: 17.1 us -> 12.3 us
  starting transfers between devices: 14.5 us -> 15.8 us
  Pallas kernels: 33.2 us -> 34.1 us
    ppermute x6, waiting for transfers between devices: 7.57 us -> 4.63 us  [shift(): return lax.ppermute(x, axis, [(i, (i + by) % count) for i in range(count)])]
    pallas_call x0 -> x2, Pallas kernels: none -> 2.74 us  [inner_sums(): pl.pallas_call(kernel, out_shape=inner_shapes(count - 2, part), in_specs=...]
    ppermute x6 -> x7, waiting for transfers between devices: 9.58 us -> 7.68 us  [reduce_all(): lax.ppermute(x, axes, [(i * sizes[1] + j, (i ^ s) * sizes[1] + (j ^ v)) f...]
    ppermute x6 -> x7, starting transfers between devices: 7.16 us -> 8.5 us  [reduce_all(): lax.ppermute(x, axes, [(i * sizes[1] + j, (i ^ s) * sizes[1] + (j ^ v)) f...]
    pallas_call x1, Pallas kernels: 7.26 us -> 6.26 us  [first_step(): pl.pallas_call(step_blocks, out_shape=jax.ShapeDtypeStruct((ext - 2, 8, p...]
    pallas_call x1, Pallas kernels: 8.29 us -> 7.45 us  [second_step(): pl.pallas_call(kernel, out_shape=(jax.ShapeDtypeStruct((count * 7, part),...]
  transfers between devices with their start and end apart: 12 -> 13, of which waited for: 9 -> 9; matrix products, arithmetic and copies ran while one was open for 0% -> 0% of each run, Pallas kernels for 10% -> 15%
where the time goes in v5:
time: 63.5 us; the launch traced here: 63.3 us
  Pallas kernels  34.1 us (54%)
  starting transfers between devices  15.8 us (25%)
  waiting for transfers between devices  12.3 us (19%)
  between operations  0.79 us (1%)
    pallas_call x1, Pallas kernels, filtered_field(): pl.pallas_call(kernel, out_shape=jax.ShapeDtypeStruct((count * comps, par...  9.19 us
    ppermute x7, starting transfers between devices, reduce_all(): lax.ppermute(x, axes, [(i * sizes[1] + j, (i ^ s) * sizes[1] + (j ^ v)) f...  8.5 us
    ppermute x7, waiting for transfers between devices, reduce_all(): lax.ppermute(x, axes, [(i * sizes[1] + j, (i ^ s) * sizes[1] + (j ^ v)) f...  7.68 us
    pallas_call x1, Pallas kernels, second_step(): pl.pallas_call(kernel, out_shape=(jax.ShapeDtypeStruct((count * 7, part),...  7.45 us
    ppermute x6, starting transfers between devices, shift(): return lax.ppermute(x, axis, [(i, (i + by) % count) for i in range(count)])  7.32 us
    pallas_call x1, Pallas kernels, first_step(): pl.pallas_call(step_blocks, out_shape=jax.ShapeDtypeStruct((ext - 2, 8, p...  6.26 us
    ppermute x6, waiting for transfers between devices, shift(): return lax.ppermute(x, axis, [(i, (i + by) % count) for i in range(count)])  4.63 us
    pallas_call x1, Pallas kernels, start_basis(): pl.pallas_call(kernel, out_shape=jax.ShapeDtypeStruct(basis_t.shape, F32)...  3.42 us
  transfers between devices with their start and end apart: 13, of which 9 were waited for; matrix products, arithmetic and copies ran while one was open for 0% of the time, Pallas kernels for 15%

profile of v5, /device:TPU:0, one launch (start us, length us, event | category | flops | bytes accessed | tf_op | source)
XLA Modules:
  0.0 63.3 jit_solution(1026548267949478369)
XLA Ops:
  0.6 0.0 copy-start.3
  0.6 1.6 %shard_map.68 = (f32[32,8,128]{2,1,0:T(8,128)}, f32[3,8,128]{2,1,0:T(8,128)}, f32[3,8,128]{2,1,0:T(8,128)}) custom-call(f32[224,128]{1,0:T(8,128)} %bitcast.22, s32[32,128]{1,0:T(8,128)} %bitcast.24, s32[4,32]{1,0:T(4,128)} %bitcast.25), custom_call_target="tpu_custom_call" | custom-call | tf_op jit(solution)/shard_map/pallas_call | solution.py:86
  2.2 0.0 copy-start.2
  2.3 3.0 %collective-permute-start = (f32[3,8,128]{2,1,0:T(8,128)}, f32[3,8,128]{2,1,0:T(8,128)S(1)}, u32[]{:S(2)}, u32[]{:S(2)}) collective-permute-start(f32[3,8,128]{2,1,0:T(8,128)} %get-tuple-element.14), channel_id=1, source_target_pairs={{0,4},{4,8},{8,12},{12,16},{16,20},{20,24},{24,28},{28,0},{1,5},{5... | collective-permute-start | bytes 36872 | tf_op jit(solution)/shard_map/ppermute | solution.py:491
  5.2 3.1 %collective-permute-start.1 = (f32[3,8,128]{2,1,0:T(8,128)}, f32[3,8,128]{2,1,0:T(8,128)S(1)}, u32[]{:S(2)}, u32[]{:S(2)}) collective-permute-start(f32[3,8,128]{2,1,0:T(8,128)} %get-tuple-element.15), channel_id=1, source_target_pairs={{0,28},{4,0},{8,4},{12,8},{16,12},{20,16},{24,20},{28,24},{1,29},{... | collective-permute-start | bytes 36872 | tf_op jit(solution)/shard_map/ppermute | solution.py:491
  8.3 3.4 %shard_map.69.b_ref = f32[64,128]{1,0:T(8,128)} custom-call(f32[64,128]{1,0:T(8,128)} %bitcast.28), custom_call_target="tpu_custom_call" | custom-call | flops 1073741824 | bytes 1048576 | tf_op jit(solution)/shard_map/pallas_call | solution.py:414
  11.7 0.0 copy-start
  11.7 0.1 stack.43.edge_ref
  11.8 0.0 collective-permute-done
  11.8 0.0 collective-permute-done.1
  11.8 0.0 copy-done.2
  11.9 0.7 %collective-permute-start.3 = (f32[36,8,128]{2,1,0:T(8,128)S(1)}, f32[36,8,128]{2,1,0:T(8,128)S(1)}, u32[]{:S(2)}, u32[]{:S(2)}) collective-permute-start(f32[36,8,128]{2,1,0:T(8,128)S(1)} %pad_maximum_fusion.mid_ref), channel_id=1, source_target_pairs={{0,3},{1,0},{2,1},{3,2},{4,7},{5,4},{6,5},{7,6},{8,11},{9,8},{10,9... | collective-permute-start | bytes 442376 | tf_op jit(solution)/shard_map/ppermute | solution.py:491
  12.6 0.0 collective-permute-start.2
  12.6 0.0 copy-done.3
  12.6 0.1 pad_add_fusion.codes_ref
  12.7 1.4 %shard_map.70 = (f32[34,24,128]{2,1,0:T(8,128)S(1)}, bf16[34,48,128]{2,1,0:T(8,128)(2,1)S(1)}) custom-call(f32[36,8,128]{2,1,0:T(8,128)S(1)} %pad_maximum_fusion.mid_ref), custom_call_target="tpu_custom_call" | custom-call | flops 1073741824 | bytes 1048576 | tf_op jit(solution)/shard_map/pallas_call | solution.py:302
  14.1 2.4 %collective-permute-done.3.high_ref = f32[36,8,128]{2,1,0:T(8,128)S(1)} collective-permute-done((f32[36,8,128]{2,1,0:T(8,128)S(1)}, f32[36,8,128]{2,1,0:T(8,128)S(1)}, u32[]{:S(2)}, u32[]{:S(2)}) %collective-permute-start.3) | collective-permute-done | bytes 147488 | tf_op jit(solution)/shard_map/ppermute | solution.py:491
  16.5 1.8 %collective-permute-done.2.low_ref = f32[36,8,128]{2,1,0:T(8,128)S(1)} collective-permute-done((f32[36,8,128]{2,1,0:T(8,128)S(1)}, f32[36,8,128]{2,1,0:T(8,128)S(1)}, u32[]{:S(2)}, u32[]{:S(2)}) %collective-permute-start.2) | collective-permute-done | bytes 147488 | tf_op jit(solution)/shard_map/ppermute | solution.py:491
  18.2 6.3 %shard_map.71.mid_ref.first_ref = f32[34,8,128]{2,1,0:T(8,128)S(1)} custom-call(s32[4,34]{1,0:T(4,128)S(1)} %pad_add_fusion.codes_ref, s32[8]{0:T(128)S(1)} %stack.43.edge_ref, f32[36,8,128]{2,1,0:T(8,128)S(1)} %collective-permute-done.2.low_ref, f32[36,8,128]{2,1,0:T(8,128)S(1)} %pad_maximum_fusion.mid_ref, ...), custom_call_target="tpu_custom_call" | custom-call | tf_op jit(solution)/shard_map/pallas_call | solution.py:217
  24.5 0.5 collective-permute-start.5
  25.0 0.1 collective-permute-start.4
  25.1 0.1 stack.42.edge_ref
  25.2 0.0 copy-done
  25.2 3.4 %shard_map.73.gram_ref = f32[128,128]{1,0:T(8,128)S(1)} custom-call(bf16[3,126,32,128]{3,2,1,0:T(8,128)(2,1)S(1)} %bitcast.19, f32[34,8,128]{2,1,0:T(8,128)S(1)} %shard_map.71.mid_ref.first_ref), custom_call_target="tpu_custom_call" | custom-call | flops 402653184 | bytes 3145728 | tf_op jit(solution)/shard_map/pallas_call | solution.py:330
  28.5 1.3 %shard_map.72 = (f32[32,24,128]{2,1,0:T(8,128)S(1)}, bf16[32,48,128]{2,1,0:T(8,128)(2,1)S(1)}) custom-call(f32[34,8,128]{2,1,0:T(8,128)S(1)} %shard_map.71.mid_ref.first_ref), custom_call_target="tpu_custom_call" | custom-call | flops 1073741824 | bytes 1048576 | tf_op jit(solution)/shard_map/pallas_call | solution.py:302
  29.9 0.0 copy-start.1
  29.9 0.0 collective-permute-done.5.high_ref
  29.9 0.5 collective-permute-done.4.low_ref
  30.4 7.5 %shard_map.74 = (f32[224,128]{1,0:T(8,128)}, f32[32,8,128]{2,1,0:T(8,128)S(1)}, f32[128,128]{1,0:T(8,128)S(1)}) custom-call(s32[4,34]{1,0:T(4,128)S(1)} %pad_add_fusion.codes_ref, s32[8]{0:T(128)S(1)} %stack.42.edge_ref, f32[34,8,128]{2,1,0:T(8,128)S(1)} %collective-permute-done.4.low_ref, f32[34,8,128]{2,1,0:T(8,128)S(1)} %shard_map.71.mid_ref.first_ref, ...), custom_call_target="tpu_custom_call" | custom-call | tf_op jit(solution)/shard_map/pallas_call | solution.py:284
  37.9 0.5 collective-permute-start.6
  38.4 0.9 %collective-permute-done.6 = f32[128,128]{1,0:T(8,128)S(1)} collective-permute-done((f32[128,128]{1,0:T(8,128)S(1)}, f32[128,128]{1,0:T(8,128)S(1)}, u32[]{:S(2)}, u32[]{:S(2)}) %collective-permute-start.6) | collective-permute-done | bytes 65568 | tf_op jit(solution)/shard_map/ppermute | solution.py:507
  39.3 0.1 collective-permute-start.9
  39.4 2.5 %collective-permute-start.8 = (f32[128,128]{1,0:T(8,128)S(1)}, f32[128,128]{1,0:T(8,128)S(1)}, u32[]{:S(2)}, u32[]{:S(2)}) collective-permute-start(f32[128,128]{1,0:T(8,128)S(1)} %add.21), channel_id=1, source_target_pairs={{0,4},{1,5},{2,6},{3,7},{4,0},{5,1},{6,2},{7,3},{8,12},{9,13},{10,... | collective-permute-start | bytes 196616 | tf_op jit(solution)/shard_map/ppermute | solution.py:507
  41.9 0.9 %collective-permute-start.7 = (f32[128,128]{1,0:T(8,128)S(1)}, f32[128,128]{1,0:T(8,128)S(1)}, u32[]{:S(2)}, u32[]{:S(2)}) collective-permute-start(f32[128,128]{1,0:T(8,128)S(1)} %add.21), channel_id=1, source_target_pairs={{0,2},{1,3},{2,0},{3,1},{4,6},{5,7},{6,4},{7,5},{8,10},{9,11},{10,... | collective-permute-start | bytes 196616 | tf_op jit(solution)/shard_map/ppermute | solution.py:507
  42.8 2.3 %collective-permute-done.9 = f32[128,128]{1,0:T(8,128)S(1)} collective-permute-done((f32[128,128]{1,0:T(8,128)S(1)}, f32[128,128]{1,0:T(8,128)S(1)}, u32[]{:S(2)}, u32[]{:S(2)}) %collective-permute-start.9) | collective-permute-done | bytes 65568 | tf_op jit(solution)/shard_map/ppermute | solution.py:507
  45.2 0.5 collective-permute-done.8
  45.6 0.5 collective-permute-done.7
  46.2 2.3 %collective-permute-start.12 = (f32[128,128]{1,0:T(8,128)S(1)}, f32[128,128]{1,0:T(8,128)S(1)}, u32[]{:S(2)}, u32[]{:S(2)}) collective-permute-start(f32[128,128]{1,0:T(8,128)S(1)} %add_add_fusion.1), channel_id=1, source_target_pairs={{0,24},{1,25},{2,26},{3,27},{4,28},{5,29},{6,30},{7,31},{8,16},{9,... | collective-permute-start | bytes 196616 | tf_op jit(solution)/shard_map/ppermute | solution.py:507
  48.5 0.0 collective-permute-start.11
  48.5 2.2 %collective-permute-start.10 = (f32[128,128]{1,0:T(8,128)S(1)}, f32[128,128]{1,0:T(8,128)S(1)}, u32[]{:S(2)}, u32[]{:S(2)}) collective-permute-start(f32[128,128]{1,0:T(8,128)S(1)} %add_add_fusion.1), channel_id=1, source_target_pairs={{0,8},{1,9},{2,10},{3,11},{4,12},{5,13},{6,14},{7,15},{8,0},{9,1},... | collective-permute-start | bytes 196616 | tf_op jit(solution)/shard_map/ppermute | solution.py:507
  50.6 1.7 %collective-permute-done.12 = f32[128,128]{1,0:T(8,128)S(1)} collective-permute-done((f32[128,128]{1,0:T(8,128)S(1)}, f32[128,128]{1,0:T(8,128)S(1)}, u32[]{:S(2)}, u32[]{:S(2)}) %collective-permute-start.12) | collective-permute-done | bytes 65568 | tf_op jit(solution)/shard_map/ppermute | solution.py:507
  52.3 1.7 %collective-permute-done.11 = f32[128,128]{1,0:T(8,128)S(1)} collective-permute-done((f32[128,128]{1,0:T(8,128)S(1)}, f32[128,128]{1,0:T(8,128)S(1)}, u32[]{:S(2)}, u32[]{:S(2)}) %collective-permute-start.11) | collective-permute-done | bytes 65568 | tf_op jit(solution)/shard_map/ppermute | solution.py:507
  54.1 0.0 collective-permute-done.10
  54.1 0.0 copy-done.1
  54.1 9.2 %shard_map.75 = f32[96,128]{1,0:T(8,128)} custom-call(f32[128,128]{1,0:T(8,128)S(1)} %add_add_fusion.gram_ref, f32[64,128]{1,0:T(8,128)S(1)} %copy-done.1, bf16[3,126,32,128]{3,2,1,0:T(8,128)(2,1)S(1)} %bitcast.21, f32[34,8,128]{2,1,0:T(8,128)S(1)} %shard_map.71.mid_ref.first_ref, f32[32,8,128]{2,1,0:T(8,128)S(1)} %get-tuple-element.25.second_ref), custom_call_target="tpu_custom_call" | custom-call | tf_op jit(solution)/shard_map/pallas_call | solution.py:480
  (9 shorter events, 0.1 us)
Async XLA Ops:
  0.6 12.0 %copy-start.3 = (s32[32,1,4]{0,2,1:T(4,128)S(1)}, s32[32,1,4]{0,2,1:T(4,128)}, u32[]{:S(2)}) copy-start(s32[32,1,4]{0,2,1:T(4,128)} %param.7) | copy-start | bytes 1540
  2.2 9.6 %copy-start.2 = (f32[32,8,128]{2,1,0:T(8,128)S(1)}, f32[32,8,128]{2,1,0:T(8,128)}, u32[]{:S(2)}) copy-start(f32[32,8,128]{2,1,0:T(8,128)} %get-tuple-element.17) | copy-start | bytes 393220
  2.3 9.6 %collective-permute-start = (f32[3,8,128]{2,1,0:T(8,128)}, f32[3,8,128]{2,1,0:T(8,128)S(1)}, u32[]{:S(2)}, u32[]{:S(2)}) collective-permute-start(f32[3,8,128]{2,1,0:T(8,128)} %get-tuple-element.14), channel_id=1, source_target_pairs={{0,4},{4,8},{8,12},{12,16},{16,20},{20,24},{24,28},{28,0},{1,5},{5... | collective-permute-start | bytes 36872 | tf_op jit(solution)/shard_map/ppermute | solution.py:491
  5.2 6.6 %collective-permute-start.1 = (f32[3,8,128]{2,1,0:T(8,128)}, f32[3,8,128]{2,1,0:T(8,128)S(1)}, u32[]{:S(2)}, u32[]{:S(2)}) collective-permute-start(f32[3,8,128]{2,1,0:T(8,128)} %get-tuple-element.15), channel_id=1, source_target_pairs={{0,28},{4,0},{8,4},{12,8},{16,12},{20,16},{24,20},{28,24},{1,29},{... | collective-permute-start | bytes 36872 | tf_op jit(solution)/shard_map/ppermute | solution.py:491
  11.7 13.4 %copy-start = (bf16[32,1,3,126,128]{4,0,3,2,1:T(8,128)(2,1)S(1)}, bf16[32,1,3,126,128]{4,0,3,2,1:T(8,128)(2,1)}, u32[]{:S(2)}) copy-start(bf16[32,1,3,126,128]{4,0,3,2,1:T(8,128)(2,1)} %param.8) | copy-start | bytes 9289732
  11.9 4.6 %collective-permute-start.3 = (f32[36,8,128]{2,1,0:T(8,128)S(1)}, f32[36,8,128]{2,1,0:T(8,128)S(1)}, u32[]{:S(2)}, u32[]{:S(2)}) collective-permute-start(f32[36,8,128]{2,1,0:T(8,128)S(1)} %pad_maximum_fusion.mid_ref), channel_id=1, source_target_pairs={{0,3},{1,0},{2,1},{3,2},{4,7},{5,4},{6,5},{7,6},{8,11},{9,8},{10,9... | collective-permute-start | bytes 442376 | tf_op jit(solution)/shard_map/ppermute | solution.py:491
  12.6 5.7 %collective-permute-start.2 = (f32[36,8,128]{2,1,0:T(8,128)S(1)}, f32[36,8,128]{2,1,0:T(8,128)S(1)}, u32[]{:S(2)}, u32[]{:S(2)}) collective-permute-start(f32[36,8,128]{2,1,0:T(8,128)S(1)} %pad_maximum_fusion.mid_ref), channel_id=1, source_target_pairs={{0,1},{1,2},{2,3},{3,0},{4,5},{5,6},{6,7},{7,4},{8,9},{9,10},{10,1... | collective-permute-start | bytes 442376 | tf_op jit(solution)/shard_map/ppermute | solution.py:491
  24.5 5.4 %collective-permute-start.5 = (f32[34,8,128]{2,1,0:T(8,128)S(1)}, f32[34,8,128]{2,1,0:T(8,128)S(1)}, u32[]{:S(2)}, u32[]{:S(2)}) collective-permute-start(f32[34,8,128]{2,1,0:T(8,128)S(1)} %shard_map.71.mid_ref.first_ref), channel_id=1, source_target_pairs={{0,3},{1,0},{2,1},{3,2},{4,7},{5,4},{6,5},{7,6},{8,11},{9,8},{10,9... | collective-permute-start | bytes 417800 | tf_op jit(solution)/shard_map/ppermute | solution.py:491
  25.0 5.4 %collective-permute-start.4 = (f32[34,8,128]{2,1,0:T(8,128)S(1)}, f32[34,8,128]{2,1,0:T(8,128)S(1)}, u32[]{:S(2)}, u32[]{:S(2)}) collective-permute-start(f32[34,8,128]{2,1,0:T(8,128)S(1)} %shard_map.71.mid_ref.first_ref), channel_id=1, source_target_pairs={{0,1},{1,2},{2,3},{3,0},{4,5},{5,6},{6,7},{7,4},{8,9},{9,10},{10,1... | collective-permute-start | bytes 417800 | tf_op jit(solution)/shard_map/ppermute | solution.py:491
  29.9 24.2 %copy-start.1 = (f32[64,128]{1,0:T(8,128)S(1)}, f32[64,128]{1,0:T(8,128)}, u32[]{:S(2)}) copy-start(f32[64,128]{1,0:T(8,128)} %shard_map.69.b_ref) | copy-start | bytes 98308
  37.9 1.4 %collective-permute-start.6 = (f32[128,128]{1,0:T(8,128)S(1)}, f32[128,128]{1,0:T(8,128)S(1)}, u32[]{:S(2)}, u32[]{:S(2)}) collective-permute-start(f32[128,128]{1,0:T(8,128)S(1)} %get-tuple-element.23), channel_id=1, source_target_pairs={{0,1},{1,0},{2,3},{3,2},{4,5},{5,4},{6,7},{7,6},{8,9},{9,8},{10,11... | collective-permute-start | bytes 196616 | tf_op jit(solution)/shard_map/ppermute | solution.py:507
  39.3 5.9 %collective-permute-start.9 = (f32[128,128]{1,0:T(8,128)S(1)}, f32[128,128]{1,0:T(8,128)S(1)}, u32[]{:S(2)}, u32[]{:S(2)}) collective-permute-start(f32[128,128]{1,0:T(8,128)S(1)} %add.21), channel_id=1, source_target_pairs={{0,6},{1,7},{2,4},{3,5},{4,2},{5,3},{6,0},{7,1},{8,14},{9,15},{10,... | collective-permute-start | bytes 196616 | tf_op jit(solution)/shard_map/ppermute | solution.py:507
  39.4 6.3 %collective-permute-start.8 = (f32[128,128]{1,0:T(8,128)S(1)}, f32[128,128]{1,0:T(8,128)S(1)}, u32[]{:S(2)}, u32[]{:S(2)}) collective-permute-start(f32[128,128]{1,0:T(8,128)S(1)} %add.21), channel_id=1, source_target_pairs={{0,4},{1,5},{2,6},{3,7},{4,0},{5,1},{6,2},{7,3},{8,12},{9,13},{10,... | collective-permute-start | bytes 196616 | tf_op jit(solution)/shard_map/ppermute | solution.py:507
  41.9 4.3 %collective-permute-start.7 = (f32[128,128]{1,0:T(8,128)S(1)}, f32[128,128]{1,0:T(8,128)S(1)}, u32[]{:S(2)}, u32[]{:S(2)}) collective-permute-start(f32[128,128]{1,0:T(8,128)S(1)} %add.21), channel_id=1, source_target_pairs={{0,2},{1,3},{2,0},{3,1},{4,6},{5,7},{6,4},{7,5},{8,10},{9,11},{10,... | collective-permute-start | bytes 196616 | tf_op jit(solution)/shard_map/ppermute | solution.py:507
  46.2 6.1 %collective-permute-start.12 = (f32[128,128]{1,0:T(8,128)S(1)}, f32[128,128]{1,0:T(8,128)S(1)}, u32[]{:S(2)}, u32[]{:S(2)}) collective-permute-start(f32[128,128]{1,0:T(8,128)S(1)} %add_add_fusion.1), channel_id=1, source_target_pairs={{0,24},{1,25},{2,26},{3,27},{4,28},{5,29},{6,30},{7,31},{8,16},{9,... | collective-permute-start | bytes 196616 | tf_op jit(solution)/shard_map/ppermute | solution.py:507
  48.5 5.6 %collective-permute-start.11 = (f32[128,128]{1,0:T(8,128)S(1)}, f32[128,128]{1,0:T(8,128)S(1)}, u32[]{:S(2)}, u32[]{:S(2)}) collective-permute-start(f32[128,128]{1,0:T(8,128)S(1)} %add_add_fusion.1), channel_id=1, source_target_pairs={{0,16},{1,17},{2,18},{3,19},{4,20},{5,21},{6,22},{7,23},{8,24},{9,... | collective-permute-start | bytes 196616 | tf_op jit(solution)/shard_map/ppermute | solution.py:507
  48.5 5.6 %collective-permute-start.10 = (f32[128,128]{1,0:T(8,128)S(1)}, f32[128,128]{1,0:T(8,128)S(1)}, u32[]{:S(2)}, u32[]{:S(2)}) collective-permute-start(f32[128,128]{1,0:T(8,128)S(1)} %add_add_fusion.1), channel_id=1, source_target_pairs={{0,8},{1,9},{2,10},{3,11},{4,12},{5,13},{6,14},{7,15},{8,0},{9,1},... | collective-permute-start | bytes 196616 | tf_op jit(solution)/shard_map/ppermute | solution.py:507

commit v6 on v5

--- a/solution.py
+++ b/solution.py
@@ -263,6 +263,34 @@
     return [flat[pl.ds(3 + c, count, stride=8), :].astype(BF16).astype(F32) for c in range(3)]
 
 
+def corner(n):
+    rows_in = lax.broadcasted_iota(jnp.int32, (n, n), 0)
+    cols_in = lax.broadcasted_iota(jnp.int32, (n, n), 1)
+    return rows_in, cols_in
+
+
+def pack(g, out_ref):
+    n = g.shape[0] // 2
+    rows_in, cols_in = corner(n)
+    right = g[n:, n:]
+    out_ref[0:n, 0:n] = jnp.where(rows_in >= cols_in, g[0:n, 0:n], right.T)
+    out_ref[0:n, n:] = g[n:, 0:n]
+    diagonal = jnp.sum(jnp.where(rows_in == cols_in, right, 0.0), axis=0, keepdims=True)
+    out_ref[n:] = jnp.broadcast_to(jnp.concatenate([diagonal, diagonal], axis=1), (8, 2 * n))
+
+
+def unpack(p_ref):
+    n = p_ref.shape[1] // 2
+    rows_in, cols_in = corner(n)
+    both = p_ref[0:n, 0:n]
+    turned = both.T
+    left = jnp.where(rows_in >= cols_in, both, turned)
+    right = jnp.where(rows_in < cols_in, both, turned)
+    right = jnp.where(rows_in == cols_in, p_ref[n:n + 1, 0:n], right)
+    below = p_ref[0:n, n:]
+    return rows(jnp.concatenate([left, below.T], axis=1), jnp.concatenate([below, right], axis=1))
+
+
 def second_step(codes, edges, low, mid, high, inner, hist, gram):
     ext, _, part = mid.shape
     count = ext - 2
@@ -279,12 +307,12 @@
             new_ref[pl.ds(i, count, stride=7), :] = flat[pl.ds(i, count, stride=8), :]
         row = cross_row(hist_ref, second, (first, second), terms)
         last = lax.broadcasted_iota(jnp.int32, (snaps, 1), 0) == snaps - 1
-        gram_out[...] = jnp.where(last, row, gram_ref[...])
+        pack(jnp.where(last, row, gram_ref[...]), gram_out)
 
     return pl.pallas_call(
         kernel,
         out_shape=(jax.ShapeDtypeStruct((count * 7, part), F32), jax.ShapeDtypeStruct((count, 8, part), F32),
-                   jax.ShapeDtypeStruct((snaps, snaps), F32)),
+                   jax.ShapeDtypeStruct((snaps // 2 + 8, snaps), F32)),
         in_specs=[sm, sm] + [v] * 7, out_specs=(v, v, v),
         scratch_shapes=step_scratch(ext, part) + [
             pltpu.VMEM((count * 8, part), F32), pltpu.VMEM((snaps * 8, part), F32)],
@@ -306,13 +334,13 @@
     )(mid)
 
 
-def early_gram(hist, first):
+def history_gram(hist):
     comps, snaps_old, count, part = hist.shape
     snaps = snaps_old + 2
     pitch = count + 8
     v = pl.BlockSpec(memory_space=pltpu.VMEM)
 
-    def kernel(hist_ref, first_ref, out_ref, wide, flat, terms):
+    def kernel(hist_ref, out_ref, wide):
         total = jnp.zeros((snaps_old, snaps_old), F32)
         for c in range(comps):
             def expand(s, _):
@@ -324,17 +352,33 @@
                 total = total + lax.dot_general(x, x, (((1,), (1,)), ((), ())), preferred_element_type=F32)
         out_ref[...] = jnp.zeros_like(out_ref)
         out_ref[0:snaps_old, 0:snaps_old] = total
+
+    return pl.pallas_call(
+        kernel, out_shape=jax.ShapeDtypeStruct((snaps, snaps), F32),
+        in_specs=[v], out_specs=v,
+        scratch_shapes=[pltpu.VMEM((snaps_old * pitch, part), F32)],
+        compiler_params=pltpu.CompilerParams(vmem_limit_bytes=VMEM_LIMIT),
+        cost_estimate=pl.CostEstimate(flops=2 * comps * snaps * snaps * count * part, bytes_accessed=2 * comps * snaps * count * part, transcendentals=0),
+    )(hist)
+
+
+def early_row(hist, first, gram):
+    comps, snaps_old, count, part = hist.shape
+    snaps = snaps_old + 2
+    v = pl.BlockSpec(memory_space=pltpu.VMEM)
+
+    def kernel(hist_ref, first_ref, gram_ref, out_ref, flat, terms):
+        out_ref[...] = gram_ref[...]
         new = load_new(first_ref, 1, count, flat)
         out_ref[snaps_old:snaps_old + 1] = cross_row(hist_ref, new, (new,), terms)
 
     return pl.pallas_call(
         kernel, out_shape=jax.ShapeDtypeStruct((snaps, snaps), F32),
-        in_specs=[v, v], out_specs=v,
-        scratch_shapes=[pltpu.VMEM((snaps_old * pitch, part), F32), pltpu.VMEM((count * 8, part), F32),
-                        pltpu.VMEM((snaps * 8, part), F32)],
+        in_specs=[v, v, v], out_specs=v,
+        scratch_shapes=[pltpu.VMEM((count * 8, part), F32), pltpu.VMEM((snaps * 8, part), F32)],
         compiler_params=pltpu.CompilerParams(vmem_limit_bytes=VMEM_LIMIT),
-        cost_estimate=pl.CostEstimate(flops=2 * comps * snaps * snaps * count * part, bytes_accessed=2 * comps * snaps * count * part, transcendentals=0),
-    )(hist, first)
+        cost_estimate=pl.CostEstimate(flops=1 << 30, bytes_accessed=2 * comps * snaps * count * part, transcendentals=0),
+    )(hist, first, gram)
 
 
 HIGHEST = lax.Precision.HIGHEST
@@ -393,14 +437,14 @@
                     c[i] = c[i] - low[i][j] * c[j]
                 sb[t] = sb[t] - c[j] * us[j]
                 mb[t] = mb[t] - c[j] * um[j]
-    return jnp.concatenate(mb, 0), jnp.min(worst)
+    return jnp.concatenate(mb, 0), worst
 
 
 def repeated(m, q_ref):
     q, worst = orthonormal(m)
     q_ref[...] = q
 
-    @pl.when(jnp.logical_not(worst >= REPEAT_BELOW))
+    @pl.when(jnp.logical_not(jnp.min(worst) >= REPEAT_BELOW))
     def _():
         q_ref[...] = orthonormal(q_ref[...])[0]
 
@@ -417,35 +461,34 @@
     )(basis_t)
 
 
-def weigh(iters, g_ref, b_ref, q_ref):
+def weigh(iters, packed_ref, g_ref, b_ref, q_ref):
     snaps = g_ref.shape[0]
-    rows_in = lax.broadcasted_iota(jnp.int32, (snaps, snaps), 0)
-    cols_in = lax.broadcasted_iota(jnp.int32, (snaps, snaps), 1)
-    g = g_ref[...]
-    low = (rows_in >= snaps - 2) & (cols_in < rows_in)
-    g = jnp.where(low | (rows_in == cols_in) | ((rows_in < snaps - 2) & (cols_in < snaps - 2)), g, 0.0)
+    rows_in, cols_in = corner(snaps)
+    g = unpack(packed_ref)
     trace = jnp.sum(jnp.where(rows_in == cols_in, g, 0.0), axis=(0, 1), keepdims=True)
-    g_ref[...] = (g + jnp.where(low, g, 0.0).T) * (1.0 / trace)
+    g_ref[...] = g * (1.0 / trace)
     q_ref[...] = b_ref[...]
 
     def product(q):
         return jnp.dot(q, g_ref[...], precision=HIGHEST, preferred_element_type=F32)
 
-    def iterate(i, _):
-        repeated(product(q_ref[...]), q_ref)
-        return 0
-
-    lax.fori_loop(0, iters - 2, iterate, 0)
-    q, worst = orthonormal(product(product(q_ref[...])))
-    good = worst >= JOIN_ABOVE
+    q, checks = b_ref[...], []
+    for k in range(iters - 1):
+        q = product(q) if k < iters - 2 else product(product(q))
+        q, worst = orthonormal(q)
+        checks.append(worst * (1.0 / (REPEAT_BELOW if k < iters - 2 else JOIN_ABOVE)))
+    good = jnp.min(functools.reduce(jnp.minimum, checks)) >= 1.0
+    q_ref[...] = q
 
     @pl.when(jnp.logical_not(good))
     def _():
-        lax.fori_loop(iters - 2, iters, iterate, 0)
-
-    @pl.when(good)
-    def _():
-        q_ref[...] = q
+        q_ref[...] = b_ref[...]
+
+        def iterate(i, _):
+            repeated(product(q_ref[...]), q_ref)
+            return 0
+
+        lax.fori_loop(0, iters, iterate, 0)
 
     q = q_ref[...]
     last = (lax.broadcasted_iota(jnp.int32, (1, snaps), 1) == snaps - 1).astype(F32)
@@ -461,8 +504,7 @@
     v = pl.BlockSpec(memory_space=pltpu.VMEM)
 
     def kernel(gram_ref, b_ref, hist_ref, first_ref, second_ref, out_ref, g_ref, q_ref, flat, table):
-        g_ref[...] = gram_ref[...]
-        w = weigh(POD_ITERS, g_ref, b_ref, q_ref)
+        w = weigh(POD_ITERS, gram_ref, g_ref, b_ref, q_ref)
         table[...] = jnp.broadcast_to(w, table.shape).T
         start = []
         for k, (ref, skip) in enumerate(((first_ref, 1), (second_ref, 0))):
@@ -480,8 +522,8 @@
     return pl.pallas_call(
         kernel, out_shape=jax.ShapeDtypeStruct((count * comps, part), F32),
         in_specs=[v, v, v, v, v], out_specs=v,
-        scratch_shapes=[pltpu.VMEM(gram.shape, F32), pltpu.VMEM(basis_t.shape, F32),
-                        pltpu.VMEM((count * 8, part), F32), pltpu.VMEM(gram.shape, F32)],
+        scratch_shapes=[pltpu.VMEM((snaps_old + 2, snaps_old + 2), F32), pltpu.VMEM(basis_t.shape, F32),
+                        pltpu.VMEM((count * 8, part), F32), pltpu.VMEM((snaps_old + 2, snaps_old + 2), F32)],
         compiler_params=pltpu.CompilerParams(vmem_limit_bytes=VMEM_LIMIT),
     )(gram, basis_t, hist, first, second)
 
@@ -529,11 +571,13 @@
         [from_low[2, 0:width, 0:1].astype(jnp.int32), codes, from_high[2, 0:width, 0:1].astype(jnp.int32)], axis=1)
     low_mid, high_mid = shift(mid, "vert", 1), shift(mid, "vert", -1)
     basis = start_basis(basis_start.T)
-    wide_codes, basis = lax.optimization_barrier((wide_codes, basis))
-    first = first_step(wide_codes, edges1, low_mid, mid, high_mid, inner_sums(mid))
+    inner, hist = lax.optimization_barrier((inner_sums(mid), hist))
+    hist_gram = history_gram(hist)
+    wide_codes, basis, hist_gram = lax.optimization_barrier((wide_codes, basis, hist_gram))
+    first = first_step(wide_codes, edges1, low_mid, mid, high_mid, inner)
     low, high = shift(first, "vert", 1), shift(first, "vert", -1)
     inner = inner_sums(first)
-    gram = early_gram(hist, first)
+    gram = early_row(hist, first, hist_gram)
     new_state, second, gram = second_step(wide_codes, edges2, low, first, high, inner, hist, gram)
     gram = reduce_all(gram)
     out = filtered_field(gram, basis, hist, first, second)

time: 63.5 us -> 61.6 us (0.970)
  waiting for transfers between devices: 12.3 us -> 11.5 us
    ppermute x7, waiting for transfers between devices: 7.68 us -> 6.58 us  [reduce_all(): lax.ppermute(x, axes, [(i * sizes[1] + j, (i ^ s) * sizes[1] + (j ^ v)) f...]
    pallas_call x1 -> x2, Pallas kernels: 3.39 us -> 3.17 us  [the longest x1 2.2 us: history_gram(): pl.pallas_call(kernel, out_shape=jax.ShapeDtypeStruct((snaps, snaps), F32...]
  transfers between devices with their start and end apart: 13 -> 13, of which waited for: 9 -> 10; matrix products, arithmetic and copies ran while one was open for 0% -> 0% of each run, Pallas kernels for 15% -> 15%
where the time goes in v6:
time: 61.6 us; the launch traced here: 61.4 us
  Pallas kernels  33.5 us (54%)
  starting transfers between devices  15.3 us (25%)
  waiting for transfers between devices  11.5 us (19%)
  between operations  0.79 us (1%)
    pallas_call x1, Pallas kernels, filtered_field(): pl.pallas_call(kernel, out_shape=jax.ShapeDtypeStruct((count * comps, par...  8.88 us
    ppermute x7, starting transfers between devices, reduce_all(): lax.ppermute(x, axes, [(i * sizes[1] + j, (i ^ s) * sizes[1] + (j ^ v)) f...  7.94 us
    pallas_call x1, Pallas kernels, second_step(): pl.pallas_call(kernel, out_shape=(jax.ShapeDtypeStruct((count * 7, part),...  7.46 us
    ppermute x6, starting transfers between devices, shift(): return lax.ppermute(x, axis, [(i, (i + by) % count) for i in range(count)])  7.32 us
    ppermute x7, waiting for transfers between devices, reduce_all(): lax.ppermute(x, axes, [(i * sizes[1] + j, (i ^ s) * sizes[1] + (j ^ v)) f...  6.58 us
    pallas_call x1, Pallas kernels, first_step(): pl.pallas_call(step_blocks, out_shape=jax.ShapeDtypeStruct((ext - 2, 8, p...  6.24 us
    ppermute x6, waiting for transfers between devices, shift(): return lax.ppermute(x, axis, [(i, (i + by) % count) for i in range(count)])  4.95 us
    pallas_call x1, Pallas kernels, start_basis(): pl.pallas_call(kernel, out_shape=jax.ShapeDtypeStruct(basis_t.shape, F32)...  3.42 us
  transfers between devices with their start and end apart: 13, of which 10 were waited for; matrix products, arithmetic and copies ran while one was open for 0% of the time, Pallas kernels for 15%

profile of v6, /device:TPU:0, one launch (start us, length us, event | category | flops | bytes accessed | tf_op | source)
XLA Modules:
  0.0 61.4 jit_solution(9332097252019559829)
XLA Ops:
  0.6 1.6 %shard_map.68 = (f32[32,8,128]{2,1,0:T(8,128)}, f32[3,8,128]{2,1,0:T(8,128)}, f32[3,8,128]{2,1,0:T(8,128)}) custom-call(f32[224,128]{1,0:T(8,128)} %bitcast.23, s32[32,128]{1,0:T(8,128)} %bitcast.25, s32[4,32]{1,0:T(4,128)} %bitcast.26), custom_call_target="tpu_custom_call" | custom-call | tf_op jit(solution)/shard_map/pallas_call | solution.py:86
  2.2 0.0 copy-start.2
  2.2 3.0 %collective-permute-start = (f32[3,8,128]{2,1,0:T(8,128)}, f32[3,8,128]{2,1,0:T(8,128)S(1)}, u32[]{:S(2)}, u32[]{:S(2)}) collective-permute-start(f32[3,8,128]{2,1,0:T(8,128)} %get-tuple-element.18), channel_id=1, source_target_pairs={{0,4},{4,8},{8,12},{12,16},{16,20},{20,24},{24,28},{28,0},{1,5},{5... | collective-permute-start | bytes 36872 | tf_op jit(solution)/shard_map/ppermute | solution.py:533
  5.2 3.1 %collective-permute-start.1 = (f32[3,8,128]{2,1,0:T(8,128)}, f32[3,8,128]{2,1,0:T(8,128)S(1)}, u32[]{:S(2)}, u32[]{:S(2)}) collective-permute-start(f32[3,8,128]{2,1,0:T(8,128)} %get-tuple-element.19), channel_id=1, source_target_pairs={{0,28},{4,0},{8,4},{12,8},{16,12},{20,16},{24,20},{28,24},{1,29},{... | collective-permute-start | bytes 36872 | tf_op jit(solution)/shard_map/ppermute | solution.py:533
  8.3 3.4 %shard_map.69.b_ref = f32[64,128]{1,0:T(8,128)} custom-call(f32[64,128]{1,0:T(8,128)} %bitcast.29), custom_call_target="tpu_custom_call" | custom-call | flops 1073741824 | bytes 1048576 | tf_op jit(solution)/shard_map/pallas_call | solution.py:458
  11.7 0.0 copy-start
  11.7 0.1 stack.42.edge_ref
  11.8 0.1 stack.43.edge_ref
  11.9 0.0 collective-permute-done
  11.9 0.0 collective-permute-done.1
  11.9 0.0 copy-done.2
  12.0 0.0 copy-start.3
  12.0 0.7 %collective-permute-start.3 = (f32[36,8,128]{2,1,0:T(8,128)S(1)}, f32[36,8,128]{2,1,0:T(8,128)S(1)}, u32[]{:S(2)}, u32[]{:S(2)}) collective-permute-start(f32[36,8,128]{2,1,0:T(8,128)S(1)} %pad_maximum_fusion.mid_ref), channel_id=1, source_target_pairs={{0,3},{1,0},{2,1},{3,2},{4,7},{5,4},{6,5},{7,6},{8,11},{9,8},{10,9... | collective-permute-start | bytes 442376 | tf_op jit(solution)/shard_map/ppermute | solution.py:533
  12.7 0.0 collective-permute-start.2
  12.7 1.4 %shard_map.70 = (f32[34,24,128]{2,1,0:T(8,128)S(1)}, bf16[34,48,128]{2,1,0:T(8,128)(2,1)S(1)}) custom-call(f32[36,8,128]{2,1,0:T(8,128)S(1)} %pad_maximum_fusion.mid_ref), custom_call_target="tpu_custom_call" | custom-call | flops 1073741824 | bytes 1048576 | tf_op jit(solution)/shard_map/pallas_call | solution.py:330
  14.1 0.0 copy-done
  14.1 2.2 %shard_map.71.gram_ref = f32[128,128]{1,0:T(8,128)S(1)} custom-call(bf16[3,126,32,128]{3,2,1,0:T(8,128)(2,1)S(1)} %bitcast.19), custom_call_target="tpu_custom_call" | custom-call | flops 402653184 | bytes 3145728 | tf_op jit(solution)/shard_map/pallas_call | solution.py:356
  16.3 0.0 copy-done.3
  16.4 0.1 pad_add_fusion.codes_ref
  16.4 0.1 collective-permute-done.3.high_ref
  16.5 1.8 %collective-permute-done.2.low_ref = f32[36,8,128]{2,1,0:T(8,128)S(1)} collective-permute-done((f32[36,8,128]{2,1,0:T(8,128)S(1)}, f32[36,8,128]{2,1,0:T(8,128)S(1)}, u32[]{:S(2)}, u32[]{:S(2)}) %collective-permute-start.2) | collective-permute-done | bytes 147488 | tf_op jit(solution)/shard_map/ppermute | solution.py:533
  18.3 6.2 %shard_map.72.mid_ref.first_ref = f32[34,8,128]{2,1,0:T(8,128)S(1)} custom-call(s32[4,34]{1,0:T(4,128)S(1)} %pad_add_fusion.codes_ref, s32[8]{0:T(128)S(1)} %stack.43.edge_ref, f32[36,8,128]{2,1,0:T(8,128)S(1)} %collective-permute-done.2.low_ref, f32[36,8,128]{2,1,0:T(8,128)S(1)} %pad_maximum_fusion.mid_ref, ...), custom_call_target="tpu_custom_call" | custom-call | tf_op jit(solution)/shard_map/pallas_call | solution.py:217
  24.6 0.5 collective-permute-start.5
  25.1 0.1 collective-permute-start.4
  25.1 1.3 %shard_map.73 = (f32[32,24,128]{2,1,0:T(8,128)S(1)}, bf16[32,48,128]{2,1,0:T(8,128)(2,1)S(1)}) custom-call(f32[34,8,128]{2,1,0:T(8,128)S(1)} %shard_map.72.mid_ref.first_ref), custom_call_target="tpu_custom_call" | custom-call | flops 1073741824 | bytes 1048576 | tf_op jit(solution)/shard_map/pallas_call | solution.py:330
  26.5 1.0 %shard_map.74.gram_ref = f32[128,128]{1,0:T(8,128)S(1)} custom-call(bf16[3,126,32,128]{3,2,1,0:T(8,128)(2,1)S(1)} %bitcast.20, f32[34,8,128]{2,1,0:T(8,128)S(1)} %shard_map.72.mid_ref.first_ref, f32[128,128]{1,0:T(8,128)S(1)} %shard_map.71.gram_ref), custom_call_target="tpu_custom_call" | custom-call | flops 1073741824 | bytes 3145728 | tf_op jit(solution)/shard_map/pallas_call | solution.py:375
  27.4 0.0 copy-start.1
  27.4 1.3 %collective-permute-done.5.high_ref = f32[34,8,128]{2,1,0:T(8,128)S(1)} collective-permute-done((f32[34,8,128]{2,1,0:T(8,128)S(1)}, f32[34,8,128]{2,1,0:T(8,128)S(1)}, u32[]{:S(2)}, u32[]{:S(2)}) %collective-permute-start.5) | collective-permute-done | bytes 139296 | tf_op jit(solution)/shard_map/ppermute | solution.py:533
  28.8 1.7 %collective-permute-done.4.low_ref = f32[34,8,128]{2,1,0:T(8,128)S(1)} collective-permute-done((f32[34,8,128]{2,1,0:T(8,128)S(1)}, f32[34,8,128]{2,1,0:T(8,128)S(1)}, u32[]{:S(2)}, u32[]{:S(2)}) %collective-permute-start.4) | collective-permute-done | bytes 139296 | tf_op jit(solution)/shard_map/ppermute | solution.py:533
  30.5 7.5 %shard_map.75 = (f32[224,128]{1,0:T(8,128)}, f32[32,8,128]{2,1,0:T(8,128)S(1)}, f32[72,128]{1,0:T(8,128)S(1)}) custom-call(s32[4,34]{1,0:T(4,128)S(1)} %pad_add_fusion.codes_ref, s32[8]{0:T(128)S(1)} %stack.42.edge_ref, f32[34,8,128]{2,1,0:T(8,128)S(1)} %collective-permute-done.4.low_ref, f32[34,8,128]{2,1,0:T(8,128)S(1)} %shard_map.72.mid_ref.first_ref, ...), custom_call_target="tpu_custom_call" | custom-call | tf_op jit(solution)/shard_map/pallas_call | solution.py:312
  38.0 0.0 collective-permute-start.6
  38.0 1.2 %collective-permute-done.6 = f32[72,128]{1,0:T(8,128)S(1)} collective-permute-done((f32[72,128]{1,0:T(8,128)S(1)}, f32[72,128]{1,0:T(8,128)S(1)}, u32[]{:S(2)}, u32[]{:S(2)}) %collective-permute-start.6) | collective-permute-done | bytes 36896 | tf_op jit(solution)/shard_map/ppermute | solution.py:549
  39.2 0.0 collective-permute-start.9
  39.2 2.6 %collective-permute-start.8 = (f32[72,128]{1,0:T(8,128)S(1)}, f32[72,128]{1,0:T(8,128)S(1)}, u32[]{:S(2)}, u32[]{:S(2)}) collective-permute-start(f32[72,128]{1,0:T(8,128)S(1)} %add.21), channel_id=1, source_target_pairs={{0,4},{1,5},{2,6},{3,7},{4,0},{5,1},{6,2},{7,3},{8,12},{9,13},{10,... | collective-permute-start | bytes 110600 | tf_op jit(solution)/shard_map/ppermute | solution.py:549
  41.7 0.9 %collective-permute-start.7 = (f32[72,128]{1,0:T(8,128)S(1)}, f32[72,128]{1,0:T(8,128)S(1)}, u32[]{:S(2)}, u32[]{:S(2)}) collective-permute-start(f32[72,128]{1,0:T(8,128)S(1)} %add.21), channel_id=1, source_target_pairs={{0,2},{1,3},{2,0},{3,1},{4,6},{5,7},{6,4},{7,5},{8,10},{9,11},{10,... | collective-permute-start | bytes 110600 | tf_op jit(solution)/shard_map/ppermute | solution.py:549
  42.7 1.7 %collective-permute-done.9 = f32[72,128]{1,0:T(8,128)S(1)} collective-permute-done((f32[72,128]{1,0:T(8,128)S(1)}, f32[72,128]{1,0:T(8,128)S(1)}, u32[]{:S(2)}, u32[]{:S(2)}) %collective-permute-start.9) | collective-permute-done | bytes 36896 | tf_op jit(solution)/shard_map/ppermute | solution.py:549
  44.4 0.0 collective-permute-done.8
  44.4 1.3 %collective-permute-done.7 = f32[72,128]{1,0:T(8,128)S(1)} collective-permute-done((f32[72,128]{1,0:T(8,128)S(1)}, f32[72,128]{1,0:T(8,128)S(1)}, u32[]{:S(2)}, u32[]{:S(2)}) %collective-permute-start.7) | collective-permute-done | bytes 36896 | tf_op jit(solution)/shard_map/ppermute | solution.py:549
  45.7 1.5 %collective-permute-start.12 = (f32[72,128]{1,0:T(8,128)S(1)}, f32[72,128]{1,0:T(8,128)S(1)}, u32[]{:S(2)}, u32[]{:S(2)}) collective-permute-start(f32[72,128]{1,0:T(8,128)S(1)} %add_add_fusion.1), channel_id=1, source_target_pairs={{0,24},{1,25},{2,26},{3,27},{4,28},{5,29},{6,30},{7,31},{8,16},{9,... | collective-permute-start | bytes 110600 | tf_op jit(solution)/shard_map/ppermute | solution.py:549
  47.2 0.0 collective-permute-start.11
  47.2 2.9 %collective-permute-start.10 = (f32[72,128]{1,0:T(8,128)S(1)}, f32[72,128]{1,0:T(8,128)S(1)}, u32[]{:S(2)}, u32[]{:S(2)}) collective-permute-start(f32[72,128]{1,0:T(8,128)S(1)} %add_add_fusion.1), channel_id=1, source_target_pairs={{0,8},{1,9},{2,10},{3,11},{4,12},{5,13},{6,14},{7,15},{8,0},{9,1},... | collective-permute-start | bytes 110600 | tf_op jit(solution)/shard_map/ppermute | solution.py:549
  50.2 1.4 %collective-permute-done.12 = f32[72,128]{1,0:T(8,128)S(1)} collective-permute-done((f32[72,128]{1,0:T(8,128)S(1)}, f32[72,128]{1,0:T(8,128)S(1)}, u32[]{:S(2)}, u32[]{:S(2)}) %collective-permute-start.12) | collective-permute-done | bytes 36896 | tf_op jit(solution)/shard_map/ppermute | solution.py:549
  51.5 0.9 %collective-permute-done.11 = f32[72,128]{1,0:T(8,128)S(1)} collective-permute-done((f32[72,128]{1,0:T(8,128)S(1)}, f32[72,128]{1,0:T(8,128)S(1)}, u32[]{:S(2)}, u32[]{:S(2)}) %collective-permute-start.11) | collective-permute-done | bytes 36896 | tf_op jit(solution)/shard_map/ppermute | solution.py:549
  52.4 0.1 collective-permute-done.10
  52.5 0.0 copy-done.1
  52.5 8.9 %shard_map.76 = f32[96,128]{1,0:T(8,128)} custom-call(f32[72,128]{1,0:T(8,128)S(1)} %add_add_fusion.gram_ref, f32[64,128]{1,0:T(8,128)S(1)} %copy-done.1, bf16[3,126,32,128]{3,2,1,0:T(8,128)(2,1)S(1)} %bitcast.22, f32[34,8,128]{2,1,0:T(8,128)S(1)} %shard_map.72.mid_ref.first_ref, f32[32,8,128]{2,1,0:T(8,128)S(1)} %get-tuple-element.33.second_ref), custom_call_target="tpu_custom_call" | custom-call | tf_op jit(solution)/shard_map/pallas_call | solution.py:522
  (9 shorter events, 0.1 us)
Async XLA Ops:
  2.2 9.7 %copy-start.2 = (f32[32,8,128]{2,1,0:T(8,128)S(1)}, f32[32,8,128]{2,1,0:T(8,128)}, u32[]{:S(2)}) copy-start(f32[32,8,128]{2,1,0:T(8,128)} %get-tuple-element.20) | copy-start | bytes 393220
  2.2 9.7 %collective-permute-start = (f32[3,8,128]{2,1,0:T(8,128)}, f32[3,8,128]{2,1,0:T(8,128)S(1)}, u32[]{:S(2)}, u32[]{:S(2)}) collective-permute-start(f32[3,8,128]{2,1,0:T(8,128)} %get-tuple-element.18), channel_id=1, source_target_pairs={{0,4},{4,8},{8,12},{12,16},{16,20},{20,24},{24,28},{28,0},{1,5},{5... | collective-permute-start | bytes 36872 | tf_op jit(solution)/shard_map/ppermute | solution.py:533
  5.2 6.7 %collective-permute-start.1 = (f32[3,8,128]{2,1,0:T(8,128)}, f32[3,8,128]{2,1,0:T(8,128)S(1)}, u32[]{:S(2)}, u32[]{:S(2)}) collective-permute-start(f32[3,8,128]{2,1,0:T(8,128)} %get-tuple-element.19), channel_id=1, source_target_pairs={{0,28},{4,0},{8,4},{12,8},{16,12},{20,16},{24,20},{28,24},{1,29},{... | collective-permute-start | bytes 36872 | tf_op jit(solution)/shard_map/ppermute | solution.py:533
  11.7 2.4 %copy-start = (bf16[32,1,3,126,128]{4,0,3,2,1:T(8,128)(2,1)S(1)}, bf16[32,1,3,126,128]{4,0,3,2,1:T(8,128)(2,1)}, u32[]{:S(2)}) copy-start(bf16[32,1,3,126,128]{4,0,3,2,1:T(8,128)(2,1)} %param.8) | copy-start | bytes 9289732
  12.0 4.4 %copy-start.3 = (s32[32,1,4]{0,2,1:T(4,128)S(1)}, s32[32,1,4]{0,2,1:T(4,128)}, u32[]{:S(2)}) copy-start(s32[32,1,4]{0,2,1:T(4,128)} %param.7) | copy-start | bytes 1540
  12.0 4.6 %collective-permute-start.3 = (f32[36,8,128]{2,1,0:T(8,128)S(1)}, f32[36,8,128]{2,1,0:T(8,128)S(1)}, u32[]{:S(2)}, u32[]{:S(2)}) collective-permute-start(f32[36,8,128]{2,1,0:T(8,128)S(1)} %pad_maximum_fusion.mid_ref), channel_id=1, source_target_pairs={{0,3},{1,0},{2,1},{3,2},{4,7},{5,4},{6,5},{7,6},{8,11},{9,8},{10,9... | collective-permute-start | bytes 442376 | tf_op jit(solution)/shard_map/ppermute | solution.py:533
  12.7 5.7 %collective-permute-start.2 = (f32[36,8,128]{2,1,0:T(8,128)S(1)}, f32[36,8,128]{2,1,0:T(8,128)S(1)}, u32[]{:S(2)}, u32[]{:S(2)}) collective-permute-start(f32[36,8,128]{2,1,0:T(8,128)S(1)} %pad_maximum_fusion.mid_ref), channel_id=1, source_target_pairs={{0,1},{1,2},{2,3},{3,0},{4,5},{5,6},{6,7},{7,4},{8,9},{9,10},{10,1... | collective-permute-start | bytes 442376 | tf_op jit(solution)/shard_map/ppermute | solution.py:533
  24.6 4.2 %collective-permute-start.5 = (f32[34,8,128]{2,1,0:T(8,128)S(1)}, f32[34,8,128]{2,1,0:T(8,128)S(1)}, u32[]{:S(2)}, u32[]{:S(2)}) collective-permute-start(f32[34,8,128]{2,1,0:T(8,128)S(1)} %shard_map.72.mid_ref.first_ref), channel_id=1, source_target_pairs={{0,3},{1,0},{2,1},{3,2},{4,7},{5,4},{6,5},{7,6},{8,11},{9,8},{10,9... | collective-permute-start | bytes 417800 | tf_op jit(solution)/shard_map/ppermute | solution.py:533
  25.1 5.4 %collective-permute-start.4 = (f32[34,8,128]{2,1,0:T(8,128)S(1)}, f32[34,8,128]{2,1,0:T(8,128)S(1)}, u32[]{:S(2)}, u32[]{:S(2)}) collective-permute-start(f32[34,8,128]{2,1,0:T(8,128)S(1)} %shard_map.72.mid_ref.first_ref), channel_id=1, source_target_pairs={{0,1},{1,2},{2,3},{3,0},{4,5},{5,6},{6,7},{7,4},{8,9},{9,10},{10,1... | collective-permute-start | bytes 417800 | tf_op jit(solution)/shard_map/ppermute | solution.py:533
  27.4 25.1 %copy-start.1 = (f32[64,128]{1,0:T(8,128)S(1)}, f32[64,128]{1,0:T(8,128)}, u32[]{:S(2)}) copy-start(f32[64,128]{1,0:T(8,128)} %shard_map.69.b_ref) | copy-start | bytes 98308
  38.0 1.2 %collective-permute-start.6 = (f32[72,128]{1,0:T(8,128)S(1)}, f32[72,128]{1,0:T(8,128)S(1)}, u32[]{:S(2)}, u32[]{:S(2)}) collective-permute-start(f32[72,128]{1,0:T(8,128)S(1)} %get-tuple-element.31), channel_id=1, source_target_pairs={{0,1},{1,0},{2,3},{3,2},{4,5},{5,4},{6,7},{7,6},{8,9},{9,8},{10,11... | collective-permute-start | bytes 110600 | tf_op jit(solution)/shard_map/ppermute | solution.py:549
  39.2 5.2 %collective-permute-start.9 = (f32[72,128]{1,0:T(8,128)S(1)}, f32[72,128]{1,0:T(8,128)S(1)}, u32[]{:S(2)}, u32[]{:S(2)}) collective-permute-start(f32[72,128]{1,0:T(8,128)S(1)} %add.21), channel_id=1, source_target_pairs={{0,6},{1,7},{2,4},{3,5},{4,2},{5,3},{6,0},{7,1},{8,14},{9,15},{10,... | collective-permute-start | bytes 110600 | tf_op jit(solution)/shard_map/ppermute | solution.py:549
  39.2 5.2 %collective-permute-start.8 = (f32[72,128]{1,0:T(8,128)S(1)}, f32[72,128]{1,0:T(8,128)S(1)}, u32[]{:S(2)}, u32[]{:S(2)}) collective-permute-start(f32[72,128]{1,0:T(8,128)S(1)} %add.21), channel_id=1, source_target_pairs={{0,4},{1,5},{2,6},{3,7},{4,0},{5,1},{6,2},{7,3},{8,12},{9,13},{10,... | collective-permute-start | bytes 110600 | tf_op jit(solution)/shard_map/ppermute | solution.py:549
  41.7 4.0 %collective-permute-start.7 = (f32[72,128]{1,0:T(8,128)S(1)}, f32[72,128]{1,0:T(8,128)S(1)}, u32[]{:S(2)}, u32[]{:S(2)}) collective-permute-start(f32[72,128]{1,0:T(8,128)S(1)} %add.21), channel_id=1, source_target_pairs={{0,2},{1,3},{2,0},{3,1},{4,6},{5,7},{6,4},{7,5},{8,10},{9,11},{10,... | collective-permute-start | bytes 110600 | tf_op jit(solution)/shard_map/ppermute | solution.py:549
  45.7 5.8 %collective-permute-start.12 = (f32[72,128]{1,0:T(8,128)S(1)}, f32[72,128]{1,0:T(8,128)S(1)}, u32[]{:S(2)}, u32[]{:S(2)}) collective-permute-start(f32[72,128]{1,0:T(8,128)S(1)} %add_add_fusion.1), channel_id=1, source_target_pairs={{0,24},{1,25},{2,26},{3,27},{4,28},{5,29},{6,30},{7,31},{8,16},{9,... | collective-permute-start | bytes 110600 | tf_op jit(solution)/shard_map/ppermute | solution.py:549
  47.2 5.2 %collective-permute-start.11 = (f32[72,128]{1,0:T(8,128)S(1)}, f32[72,128]{1,0:T(8,128)S(1)}, u32[]{:S(2)}, u32[]{:S(2)}) collective-permute-start(f32[72,128]{1,0:T(8,128)S(1)} %add_add_fusion.1), channel_id=1, source_target_pairs={{0,16},{1,17},{2,18},{3,19},{4,20},{5,21},{6,22},{7,23},{8,24},{9,... | collective-permute-start | bytes 110600 | tf_op jit(solution)/shard_map/ppermute | solution.py:549
  47.2 5.3 %collective-permute-start.10 = (f32[72,128]{1,0:T(8,128)S(1)}, f32[72,128]{1,0:T(8,128)S(1)}, u32[]{:S(2)}, u32[]{:S(2)}) collective-permute-start(f32[72,128]{1,0:T(8,128)S(1)} %add_add_fusion.1), channel_id=1, source_target_pairs={{0,8},{1,9},{2,10},{3,11},{4,12},{5,13},{6,14},{7,15},{8,0},{9,1},... | collective-permute-start | bytes 110600 | tf_op jit(solution)/shard_map/ppermute | solution.py:549

commit v7 on v6

--- a/solution.py
+++ b/solution.py
@@ -39,30 +39,28 @@
 def spread(row):
     return jnp.broadcast_to(row, (8, row.shape[1]))
 
-def features(state):
+def base_rows(state, keep):
     centred = jnp.where(row_is(0, 1, 2), state - 1.0, state)
-    r, rho = spread(state[6:7]), spread(state[7:8])
+    r, rho = spread(state[6:7]), spread(state[7:8] * keep)
     live = rho > 0.0
     mass = rho * VOLUME
     r2 = r * r
     pressure = jnp.where(live, STIFFNESS * (r2 * r2 * r2 * r - 1.0) / (jnp.where(live, rho, 1.0) * r2), 0.0)
-    mp = mass * pressure
-    place = jnp.where(row_is(0, 1, 2), centred, 0.0)
+    return jnp.where(row_is(6), mass, jnp.where(row_is(7), mass * pressure, centred)), pressure
+
+
+def features(base):
+    place = jnp.where(row_is(0, 1, 2), base, 0.0)
     norm = 0.25 * jnp.sum(place * place, axis=0, keepdims=True)
-    speed = jnp.where(row_is(0, 1, 2), pltpu.roll(centred, 5, 0), 0.0)
+    speed = jnp.where(row_is(0, 1, 2), pltpu.roll(base, 5, 0), 0.0)
     flux = jnp.sum(place * speed, axis=0, keepdims=True)
     own = jnp.where(row_is(3), norm, jnp.where(row_is(4), 1.0, place))
     near = jnp.where(row_is(3), 1.0, jnp.where(row_is(4), norm, -0.5 * place))
-    moved = jnp.where(row_is(0), 1.0, jnp.where(row_is(7), flux, pltpu.roll(centred, 1, 0)))
-    sums_a = mass * moved
-    sums_b = jnp.where(row_is(0, 1, 2, 3), mp * moved, 0.0)
-    near_x = jnp.where(row_is(0), -0.5, jnp.where(row_is(4), 0.5 * centred[0:1], 0.0))
-    near_z = jnp.where(row_is(2), -0.5, jnp.where(row_is(4), 0.5 * centred[2:3], 0.0))
-    sums_ax = mass * jnp.where(row_is(1), 1.0, jnp.where(row_is(7), centred[3:4], 0.0))
-    sums_az = mass * jnp.where(row_is(3), 1.0, jnp.where(row_is(7), centred[5:6], 0.0))
-    sums_bx = jnp.where(row_is(1), mp, 0.0)
-    sums_bz = jnp.where(row_is(3), mp, 0.0)
-    return own, rows(near, sums_a, sums_b), rows(near_x, sums_ax, sums_bx), rows(near_z, sums_az, sums_bz), pressure[0:1]
+    moved = jnp.where(row_is(0), 1.0, jnp.where(row_is(7), flux, pltpu.roll(base, 1, 0)))
+    sums_a = spread(base[6:7]) * moved
+    sums_b = jnp.where(row_is(0, 1, 2, 3), spread(base[7:8]) * moved, 0.0)
+    return own, rows(near, sums_a, sums_b)
+
 
 def prep_kernel(particles_ref, flags_ref, codes_ref, state_ref, lo_ref, hi_ref, flat):
     count = flags_ref.shape[0]
@@ -134,10 +132,11 @@
     def run(blocks):
         group = []
         for b in blocks:
-            own, g_self, _, _, pressure = features(state_ref[b + skip])
+            base, pressure = base_rows(state_ref[b + skip], 1.0)
+            own, g_self = features(base)
             side = own_side(own)
             side_ref[b] = side
-            self_ref[b, 16:24] = spread(pressure)
+            self_ref[b, 16:24] = pressure
             group.append((side,) + near_side(g_self))
         for b, t in zip(blocks, weighted_sums(group)):
             self_ref[b, 0:16] = t
@@ -148,26 +147,20 @@
     return (jax.ShapeDtypeStruct((count, 24, part), F32), jax.ShapeDtypeStruct((count, 48, part), BF16))
 
 
-def step_blocks(codes_ref, edge_ref, low_ref, mid_ref, high_ref, self_ref, side_ref, out_ref, b0, b1, b2):
-    ext = mid_ref.shape[0]
+def step_blocks(codes_ref, edge_ref, low_ref, mid_ref, high_ref, self_ref, side_ref, store, base_ref):
+    ext, _, part = mid_ref.shape
     count = ext - 2
-    sel = lax.broadcasted_iota(jnp.int32, (8, 1), 0) == 7
-    rim = edge_ref[5]
+    rim, skip = edge_ref[5], edge_ref[6]
+    along = row_is(0).astype(F32)
+    upward = row_is(2).astype(F32)
 
     def prep(i):
         rowon = jnp.where(i < rim, edge_ref[3], jnp.where(i >= ext - rim, edge_ref[4], 1))
         for col, ref in ((0, low_ref), (1, mid_ref), (2, high_ref)):
-            st = ref[i]
-            keep = (edge_ref[col] * rowon).astype(F32)
-            _, a, b, c, _ = features(jnp.where(sel, st * keep, st))
-            b0[col * ext + i] = a
-            b1[col * ext + i] = b
-            b2[col * ext + i] = c
+            base_ref[col * ext + i] = base_rows(ref[i], (edge_ref[col] * rowon).astype(F32))[0]
 
     for i in range(3):
         prep(i)
-    normrow = (lax.broadcasted_iota(jnp.int32, (24, 1), 0) == 4).astype(F32)
-    skip = edge_ref[6]
 
     def operands(b):
         st = mid_ref[b + 1]
@@ -180,7 +173,7 @@
             idx = dv1 * ext + b + ds1
             tx = 2.0 * (ds1 - 1).astype(F32)
             tz = 2.0 * (dv1 - 1).astype(F32)
-            gs.append(b0[idx] + tx * b1[idx] + tz * b2[idx] + normrow * (0.25 * (tx * tx + tz * tz)))
+            gs.append(features(base_ref[idx] + (tx * along + tz * upward))[1])
         prep(jnp.minimum(b + 3, ext - 1))
         near = [near_side(g) for g in gs]
         return st, (side_ref[b],) + tuple(jnp.concatenate(x, axis=1) for x in zip(*near))
@@ -197,7 +190,7 @@
         pos2 = st[0:3] + TIME_STEP * vel2
         rho = st[7:8]
         r2 = st[6:7] + TIME_STEP * dens / rho
-        out_ref[b] = rows(pos2, vel2, r2, rho)
+        store(b, rows(pos2, vel2, r2, rho))
 
     def run(blocks):
         group = [operands(b) for b in blocks]
@@ -207,15 +200,20 @@
 
 
 def step_scratch(ext, part):
-    return [pltpu.VMEM((3 * ext, 24, part), F32)] * 3
+    return [pltpu.VMEM((3 * ext, 8, part), F32)]
 
 
 def first_step(codes, edges, low, mid, high, inner):
     ext, _, part = mid.shape
     v = pl.BlockSpec(memory_space=pltpu.VMEM)
     sm = pl.BlockSpec(memory_space=pltpu.SMEM)
-    return pl.pallas_call(
-        step_blocks, out_shape=jax.ShapeDtypeStruct((ext - 2, 8, part), F32),
+    def kernel(codes_ref, edge_ref, low_ref, mid_ref, high_ref, self_ref, side_ref, out_ref, base_ref):
+        def store(b, value):
+            out_ref[b] = value
+        step_blocks(codes_ref, edge_ref, low_ref, mid_ref, high_ref, self_ref, side_ref, store, base_ref)
+
+    return pl.pallas_call(
+        kernel, out_shape=jax.ShapeDtypeStruct((ext - 2, 8, part), F32),
         in_specs=[sm, sm, v, v, v, v, v], out_specs=v,
         scratch_shapes=step_scratch(ext, part),
         compiler_params=pltpu.CompilerParams(vmem_limit_bytes=VMEM_LIMIT),
@@ -255,11 +253,7 @@
     return lax.dot_general(ones, by_snap, (((1,), (1,)), ((), ())), precision=HIGHEST, preferred_element_type=F32)[0:1]
 
 
-def load_new(ref, skip, count, flat):
-    def move(b, _):
-        flat[pl.ds(pl.multiple_of(8 * b, 8), 8), :] = ref[b + skip]
-        return 0
-    lax.fori_loop(0, count, move, 0, unroll=math.gcd(count, 8))
+def new_snapshot(flat, count):
     return [flat[pl.ds(3 + c, count, stride=8), :].astype(BF16).astype(F32) for c in range(3)]
 
 
@@ -291,18 +285,22 @@
     return rows(jnp.concatenate([left, below.T], axis=1), jnp.concatenate([below, right], axis=1))
 
 
-def second_step(codes, edges, low, mid, high, inner, hist, gram):
+def second_step(codes, edges, low, mid, high, inner, hist, first, gram):
     ext, _, part = mid.shape
     count = ext - 2
     snaps = gram.shape[0]
     v = pl.BlockSpec(memory_space=pltpu.VMEM)
     sm = pl.BlockSpec(memory_space=pltpu.SMEM)
 
-    def kernel(codes_ref, edge_ref, low_ref, mid_ref, high_ref, self_ref, side_ref, hist_ref, gram_ref, new_ref, state_ref, gram_out,
-               b0, b1, b2, flat, terms):
-        step_blocks(codes_ref, edge_ref, low_ref, mid_ref, high_ref, self_ref, side_ref, state_ref, b0, b1, b2)
-        first = load_new(mid_ref, 1, count, flat)
-        second = load_new(state_ref, 0, count, flat)
+    def kernel(codes_ref, edge_ref, low_ref, mid_ref, high_ref, self_ref, side_ref, hist_ref, first_ref, gram_ref,
+               new_ref, second_ref, gram_out, base_ref, flat, terms):
+        def store(b, value):
+            flat[pl.ds(pl.multiple_of(8 * b, 8), 8), :] = value
+        step_blocks(codes_ref, edge_ref, low_ref, mid_ref, high_ref, self_ref, side_ref, store, base_ref)
+        first = [first_ref[count * c:count * (c + 1)] for c in range(3)]
+        second = new_snapshot(flat, count)
+        for c in range(3):
+            second_ref[count * c:count * (c + 1)] = second[c]
         for i in range(7):
             new_ref[pl.ds(i, count, stride=7), :] = flat[pl.ds(i, count, stride=8), :]
         row = cross_row(hist_ref, second, (first, second), terms)
@@ -311,13 +309,13 @@
 
     return pl.pallas_call(
         kernel,
-        out_shape=(jax.ShapeDtypeStruct((count * 7, part), F32), jax.ShapeDtypeStruct((count, 8, part), F32),
+        out_shape=(jax.ShapeDtypeStruct((count * 7, part), F32), jax.ShapeDtypeStruct(first.shape, F32),
                    jax.ShapeDtypeStruct((snaps // 2 + 8, snaps), F32)),
-        in_specs=[sm, sm] + [v] * 7, out_specs=(v, v, v),
+        in_specs=[sm, sm] + [v] * 8, out_specs=(v, v, v),
         scratch_shapes=step_scratch(ext, part) + [
             pltpu.VMEM((count * 8, part), F32), pltpu.VMEM((snaps * 8, part), F32)],
         compiler_params=pltpu.CompilerParams(vmem_limit_bytes=VMEM_LIMIT),
-    )(codes, edges, low, mid, high, *inner, hist, gram)
+    )(codes, edges, low, mid, high, *inner, hist, first, gram)
 
 
 def inner_sums(mid):
@@ -367,14 +365,18 @@
     snaps = snaps_old + 2
     v = pl.BlockSpec(memory_space=pltpu.VMEM)
 
-    def kernel(hist_ref, first_ref, gram_ref, out_ref, flat, terms):
+    def kernel(hist_ref, first_ref, gram_ref, out_ref, new_ref, flat, terms):
         out_ref[...] = gram_ref[...]
-        new = load_new(first_ref, 1, count, flat)
+        for b in range(count):
+            flat[8 * b:8 * b + 8] = first_ref[b + 1]
+        new = new_snapshot(flat, count)
+        for c in range(3):
+            new_ref[count * c:count * (c + 1)] = new[c]
         out_ref[snaps_old:snaps_old + 1] = cross_row(hist_ref, new, (new,), terms)
 
     return pl.pallas_call(
-        kernel, out_shape=jax.ShapeDtypeStruct((snaps, snaps), F32),
-        in_specs=[v, v, v], out_specs=v,
+        kernel, out_shape=(jax.ShapeDtypeStruct((snaps, snaps), F32), jax.ShapeDtypeStruct((count * 3, part), F32)),
+        in_specs=[v, v, v], out_specs=(v, v),
         scratch_shapes=[pltpu.VMEM((count * 8, part), F32), pltpu.VMEM((snaps * 8, part), F32)],
         compiler_params=pltpu.CompilerParams(vmem_limit_bytes=VMEM_LIMIT),
         cost_estimate=pl.CostEstimate(flops=1 << 30, bytes_accessed=2 * comps * snaps * count * part, transcendentals=0),
@@ -503,14 +505,12 @@
     comps, snaps_old, count, part = hist.shape
     v = pl.BlockSpec(memory_space=pltpu.VMEM)
 
-    def kernel(gram_ref, b_ref, hist_ref, first_ref, second_ref, out_ref, g_ref, q_ref, flat, table):
+    def kernel(gram_ref, b_ref, hist_ref, first_ref, second_ref, out_ref, g_ref, q_ref, table):
         w = weigh(POD_ITERS, gram_ref, g_ref, b_ref, q_ref)
         table[...] = jnp.broadcast_to(w, table.shape).T
-        start = []
-        for k, (ref, skip) in enumerate(((first_ref, 1), (second_ref, 0))):
-            wk = table[snaps_old + k:snaps_old + k + 1]
-            new = [wk * x for x in load_new(ref, skip, count, flat)]
-            start = [x + y for x, y in zip(start, new)] if start else new
+        w1, w2 = (table[snaps_old + k:snaps_old + k + 1] for k in range(2))
+        parts = [slice(count * c, count * (c + 1)) for c in range(comps)]
+        start = [w1 * first_ref[p] + w2 * second_ref[p] for p in parts]
 
         def one(s, total):
             wk = table[pl.ds(s, 1), :]
@@ -523,7 +523,7 @@
         kernel, out_shape=jax.ShapeDtypeStruct((count * comps, part), F32),
         in_specs=[v, v, v, v, v], out_specs=v,
         scratch_shapes=[pltpu.VMEM((snaps_old + 2, snaps_old + 2), F32), pltpu.VMEM(basis_t.shape, F32),
-                        pltpu.VMEM((count * 8, part), F32), pltpu.VMEM((snaps_old + 2, snaps_old + 2), F32)],
+                        pltpu.VMEM((snaps_old + 2, snaps_old + 2), F32)],
         compiler_params=pltpu.CompilerParams(vmem_limit_bytes=VMEM_LIMIT),
     )(gram, basis_t, hist, first, second)
 
@@ -577,10 +577,10 @@
     first = first_step(wide_codes, edges1, low_mid, mid, high_mid, inner)
     low, high = shift(first, "vert", 1), shift(first, "vert", -1)
     inner = inner_sums(first)
-    gram = early_row(hist, first, hist_gram)
-    new_state, second, gram = second_step(wide_codes, edges2, low, first, high, inner, hist, gram)
+    gram, first_new = early_row(hist, first, hist_gram)
+    new_state, second_new, gram = second_step(wide_codes, edges2, low, first, high, inner, hist, first_new, gram)
     gram = reduce_all(gram)
-    out = filtered_field(gram, basis, hist, first, second)
+    out = filtered_field(gram, basis, hist, first_new, second_new)
     return (new_state.reshape(count, 1, 7, -1), out.reshape(count, 1, 3, -1))
 
 

time: 61.6 us -> 60.9 us (0.989)
  Pallas kernels: 33.5 us -> 32.7 us
where the time goes in v7:
time: 60.9 us; the launch traced here: 60.7 us
  Pallas kernels  32.7 us (54%)
  starting transfers between devices  15.3 us (25%)
  waiting for transfers between devices  11.7 us (19%)
  between operations  0.78 us (1%)
    pallas_call x1, Pallas kernels, filtered_field(): pl.pallas_call(kernel, out_shape=jax.ShapeDtypeStruct((count * comps, par...  9.04 us
    ppermute x7, starting transfers between devices, reduce_all(): lax.ppermute(x, axes, [(i * sizes[1] + j, (i ^ s) * sizes[1] + (j ^ v)) f...  7.94 us
    ppermute x6, starting transfers between devices, shift(): return lax.ppermute(x, axis, [(i, (i + by) % count) for i in range(count)])  7.32 us
    pallas_call x1, Pallas kernels, second_step(): pl.pallas_call(kernel, out_shape=(jax.ShapeDtypeStruct((count * 7, part),...  6.9 us
    ppermute x7, waiting for transfers between devices, reduce_all(): lax.ppermute(x, axes, [(i * sizes[1] + j, (i ^ s) * sizes[1] + (j ^ v)) f...  6.59 us
    pallas_call x1, Pallas kernels, first_step(): pl.pallas_call(kernel, out_shape=jax.ShapeDtypeStruct((ext - 2, 8, part),...  5.97 us
    ppermute x6, waiting for transfers between devices, shift(): return lax.ppermute(x, axis, [(i, (i + by) % count) for i in range(count)])  5.09 us
    pallas_call x1, Pallas kernels, start_basis(): pl.pallas_call(kernel, out_shape=jax.ShapeDtypeStruct(basis_t.shape, F32)...  3.42 us
  transfers between devices with their start and end apart: 13, of which 10 were waited for; matrix products, arithmetic and copies ran while one was open for 0% of the time, Pallas kernels for 15%

profile of v7, /device:TPU:0, one launch (start us, length us, event | category | flops | bytes accessed | tf_op | source)
XLA Modules:
  0.0 60.7 jit_solution(14794962592579196826)
XLA Ops:
  0.6 1.6 %shard_map.68 = (f32[32,8,128]{2,1,0:T(8,128)}, f32[3,8,128]{2,1,0:T(8,128)}, f32[3,8,128]{2,1,0:T(8,128)}) custom-call(f32[224,128]{1,0:T(8,128)} %bitcast.23, s32[32,128]{1,0:T(8,128)} %bitcast.25, s32[4,32]{1,0:T(4,128)} %bitcast.26), custom_call_target="tpu_custom_call" | custom-call | tf_op jit(solution)/shard_map/pallas_call | solution.py:84
  2.2 0.0 copy-start.2
  2.2 3.0 %collective-permute-start = (f32[3,8,128]{2,1,0:T(8,128)}, f32[3,8,128]{2,1,0:T(8,128)S(1)}, u32[]{:S(2)}, u32[]{:S(2)}) collective-permute-start(f32[3,8,128]{2,1,0:T(8,128)} %get-tuple-element.20), channel_id=1, source_target_pairs={{0,4},{4,8},{8,12},{12,16},{16,20},{20,24},{24,28},{28,0},{1,5},{5... | collective-permute-start | bytes 36872 | tf_op jit(solution)/shard_map/ppermute | solution.py:533
  5.2 3.1 %collective-permute-start.1 = (f32[3,8,128]{2,1,0:T(8,128)}, f32[3,8,128]{2,1,0:T(8,128)S(1)}, u32[]{:S(2)}, u32[]{:S(2)}) collective-permute-start(f32[3,8,128]{2,1,0:T(8,128)} %get-tuple-element.21), channel_id=1, source_target_pairs={{0,28},{4,0},{8,4},{12,8},{16,12},{20,16},{24,20},{28,24},{1,29},{... | collective-permute-start | bytes 36872 | tf_op jit(solution)/shard_map/ppermute | solution.py:533
  8.3 3.4 %shard_map.69.b_ref = f32[64,128]{1,0:T(8,128)} custom-call(f32[64,128]{1,0:T(8,128)} %bitcast.29), custom_call_target="tpu_custom_call" | custom-call | flops 1073741824 | bytes 1048576 | tf_op jit(solution)/shard_map/pallas_call | solution.py:460
  11.7 0.0 copy-start
  11.7 0.1 stack.42.edge_ref
  11.8 0.1 stack.43.edge_ref
  11.9 0.0 collective-permute-done
  11.9 0.0 collective-permute-done.1
  11.9 0.0 copy-done.2
  12.0 0.0 copy-start.3
  12.0 0.7 %collective-permute-start.3 = (f32[36,8,128]{2,1,0:T(8,128)S(1)}, f32[36,8,128]{2,1,0:T(8,128)S(1)}, u32[]{:S(2)}, u32[]{:S(2)}) collective-permute-start(f32[36,8,128]{2,1,0:T(8,128)S(1)} %pad_maximum_fusion.mid_ref), channel_id=1, source_target_pairs={{0,3},{1,0},{2,1},{3,2},{4,7},{5,4},{6,5},{7,6},{8,11},{9,8},{10,9... | collective-permute-start | bytes 442376 | tf_op jit(solution)/shard_map/ppermute | solution.py:533
  12.7 0.0 collective-permute-start.2
  12.7 1.3 %shard_map.70 = (f32[34,24,128]{2,1,0:T(8,128)S(1)}, bf16[34,48,128]{2,1,0:T(8,128)(2,1)S(1)}) custom-call(f32[36,8,128]{2,1,0:T(8,128)S(1)} %pad_maximum_fusion.mid_ref), custom_call_target="tpu_custom_call" | custom-call | flops 1073741824 | bytes 1048576 | tf_op jit(solution)/shard_map/pallas_call | solution.py:328
  14.0 0.0 copy-done
  14.1 2.2 %shard_map.71.gram_ref = f32[128,128]{1,0:T(8,128)S(1)} custom-call(bf16[3,126,32,128]{3,2,1,0:T(8,128)(2,1)S(1)} %bitcast.19), custom_call_target="tpu_custom_call" | custom-call | flops 402653184 | bytes 3145728 | tf_op jit(solution)/shard_map/pallas_call | solution.py:354
  16.3 0.0 copy-done.3
  16.3 0.1 pad_add_fusion.codes_ref
  16.3 0.2 collective-permute-done.3.high_ref
  16.5 1.8 %collective-permute-done.2.low_ref = f32[36,8,128]{2,1,0:T(8,128)S(1)} collective-permute-done((f32[36,8,128]{2,1,0:T(8,128)S(1)}, f32[36,8,128]{2,1,0:T(8,128)S(1)}, u32[]{:S(2)}, u32[]{:S(2)}) %collective-permute-start.2) | collective-permute-done | bytes 147488 | tf_op jit(solution)/shard_map/ppermute | solution.py:533
  18.3 6.0 %shard_map.72.mid_ref.first_ref = f32[34,8,128]{2,1,0:T(8,128)S(1)} custom-call(s32[4,34]{1,0:T(4,128)S(1)} %pad_add_fusion.codes_ref, s32[8]{0:T(128)S(1)} %stack.43.edge_ref, f32[36,8,128]{2,1,0:T(8,128)S(1)} %collective-permute-done.2.low_ref, f32[36,8,128]{2,1,0:T(8,128)S(1)} %pad_maximum_fusion.mid_ref, ...), custom_call_target="tpu_custom_call" | custom-call | tf_op jit(solution)/shard_map/pallas_call | solution.py:215
  24.3 0.5 collective-permute-start.5
  24.8 0.1 collective-permute-start.4
  24.9 1.3 %shard_map.73 = (f32[32,24,128]{2,1,0:T(8,128)S(1)}, bf16[32,48,128]{2,1,0:T(8,128)(2,1)S(1)}) custom-call(f32[34,8,128]{2,1,0:T(8,128)S(1)} %shard_map.72.mid_ref.first_ref), custom_call_target="tpu_custom_call" | custom-call | flops 1073741824 | bytes 1048576 | tf_op jit(solution)/shard_map/pallas_call | solution.py:328
  26.1 1.0 %shard_map.74 = (f32[128,128]{1,0:T(8,128)S(1)}, f32[96,128]{1,0:T(8,128)S(1)}) custom-call(bf16[3,126,32,128]{3,2,1,0:T(8,128)(2,1)S(1)} %bitcast.20, f32[34,8,128]{2,1,0:T(8,128)S(1)} %shard_map.72.mid_ref.first_ref, f32[128,128]{1,0:T(8,128)S(1)} %shard_map.71.gram_ref), custom_call_target="tpu_custom_call" | custom-call | flops 1073741824 | bytes 3145728 | tf_op jit(solution)/shard_map/pallas_call | solution.py:377
  27.1 0.0 copy-start.1
  27.1 1.4 %collective-permute-done.5.high_ref = f32[34,8,128]{2,1,0:T(8,128)S(1)} collective-permute-done((f32[34,8,128]{2,1,0:T(8,128)S(1)}, f32[34,8,128]{2,1,0:T(8,128)S(1)}, u32[]{:S(2)}, u32[]{:S(2)}) %collective-permute-start.5) | collective-permute-done | bytes 139296 | tf_op jit(solution)/shard_map/ppermute | solution.py:533
  28.5 1.7 %collective-permute-done.4.low_ref = f32[34,8,128]{2,1,0:T(8,128)S(1)} collective-permute-done((f32[34,8,128]{2,1,0:T(8,128)S(1)}, f32[34,8,128]{2,1,0:T(8,128)S(1)}, u32[]{:S(2)}, u32[]{:S(2)}) %collective-permute-start.4) | collective-permute-done | bytes 139296 | tf_op jit(solution)/shard_map/ppermute | solution.py:533
  30.2 6.9 %shard_map.75 = (f32[224,128]{1,0:T(8,128)}, f32[96,128]{1,0:T(8,128)S(1)}, f32[72,128]{1,0:T(8,128)S(1)}) custom-call(s32[4,34]{1,0:T(4,128)S(1)} %pad_add_fusion.codes_ref, s32[8]{0:T(128)S(1)} %stack.42.edge_ref, f32[34,8,128]{2,1,0:T(8,128)S(1)} %collective-permute-done.4.low_ref, f32[34,8,128]{2,1,0:T(8,128)S(1)} %shard_map.72.mid_ref.first_ref, ...), custom_call_target="tpu_custom_call" | custom-call | tf_op jit(solution)/shard_map/pallas_call | solution.py:310
  37.1 0.0 collective-permute-start.6
  37.1 1.2 %collective-permute-done.6 = f32[72,128]{1,0:T(8,128)S(1)} collective-permute-done((f32[72,128]{1,0:T(8,128)S(1)}, f32[72,128]{1,0:T(8,128)S(1)}, u32[]{:S(2)}, u32[]{:S(2)}) %collective-permute-start.6) | collective-permute-done | bytes 36896 | tf_op jit(solution)/shard_map/ppermute | solution.py:549
  38.3 0.0 collective-permute-start.9
  38.3 2.6 %collective-permute-start.8 = (f32[72,128]{1,0:T(8,128)S(1)}, f32[72,128]{1,0:T(8,128)S(1)}, u32[]{:S(2)}, u32[]{:S(2)}) collective-permute-start(f32[72,128]{1,0:T(8,128)S(1)} %add.21), channel_id=1, source_target_pairs={{0,4},{1,5},{2,6},{3,7},{4,0},{5,1},{6,2},{7,3},{8,12},{9,13},{10,... | collective-permute-start | bytes 110600 | tf_op jit(solution)/shard_map/ppermute | solution.py:549
  40.9 0.9 %collective-permute-start.7 = (f32[72,128]{1,0:T(8,128)S(1)}, f32[72,128]{1,0:T(8,128)S(1)}, u32[]{:S(2)}, u32[]{:S(2)}) collective-permute-start(f32[72,128]{1,0:T(8,128)S(1)} %add.21), channel_id=1, source_target_pairs={{0,2},{1,3},{2,0},{3,1},{4,6},{5,7},{6,4},{7,5},{8,10},{9,11},{10,... | collective-permute-start | bytes 110600 | tf_op jit(solution)/shard_map/ppermute | solution.py:549
  41.8 1.7 %collective-permute-done.9 = f32[72,128]{1,0:T(8,128)S(1)} collective-permute-done((f32[72,128]{1,0:T(8,128)S(1)}, f32[72,128]{1,0:T(8,128)S(1)}, u32[]{:S(2)}, u32[]{:S(2)}) %collective-permute-start.9) | collective-permute-done | bytes 36896 | tf_op jit(solution)/shard_map/ppermute | solution.py:549
  43.5 0.0 collective-permute-done.8
  43.5 1.3 %collective-permute-done.7 = f32[72,128]{1,0:T(8,128)S(1)} collective-permute-done((f32[72,128]{1,0:T(8,128)S(1)}, f32[72,128]{1,0:T(8,128)S(1)}, u32[]{:S(2)}, u32[]{:S(2)}) %collective-permute-start.7) | collective-permute-done | bytes 36896 | tf_op jit(solution)/shard_map/ppermute | solution.py:549
  44.9 1.5 %collective-permute-start.12 = (f32[72,128]{1,0:T(8,128)S(1)}, f32[72,128]{1,0:T(8,128)S(1)}, u32[]{:S(2)}, u32[]{:S(2)}) collective-permute-start(f32[72,128]{1,0:T(8,128)S(1)} %add_add_fusion.1), channel_id=1, source_target_pairs={{0,24},{1,25},{2,26},{3,27},{4,28},{5,29},{6,30},{7,31},{8,16},{9,... | collective-permute-start | bytes 110600 | tf_op jit(solution)/shard_map/ppermute | solution.py:549
  46.4 0.0 collective-permute-start.11
  46.4 2.9 %collective-permute-start.10 = (f32[72,128]{1,0:T(8,128)S(1)}, f32[72,128]{1,0:T(8,128)S(1)}, u32[]{:S(2)}, u32[]{:S(2)}) collective-permute-start(f32[72,128]{1,0:T(8,128)S(1)} %add_add_fusion.1), channel_id=1, source_target_pairs={{0,8},{1,9},{2,10},{3,11},{4,12},{5,13},{6,14},{7,15},{8,0},{9,1},... | collective-permute-start | bytes 110600 | tf_op jit(solution)/shard_map/ppermute | solution.py:549
  49.3 1.4 %collective-permute-done.12 = f32[72,128]{1,0:T(8,128)S(1)} collective-permute-done((f32[72,128]{1,0:T(8,128)S(1)}, f32[72,128]{1,0:T(8,128)S(1)}, u32[]{:S(2)}, u32[]{:S(2)}) %collective-permute-start.12) | collective-permute-done | bytes 36896 | tf_op jit(solution)/shard_map/ppermute | solution.py:549
  50.7 0.9 %collective-permute-done.11 = f32[72,128]{1,0:T(8,128)S(1)} collective-permute-done((f32[72,128]{1,0:T(8,128)S(1)}, f32[72,128]{1,0:T(8,128)S(1)}, u32[]{:S(2)}, u32[]{:S(2)}) %collective-permute-start.11) | collective-permute-done | bytes 36896 | tf_op jit(solution)/shard_map/ppermute | solution.py:549
  51.6 0.1 collective-permute-done.10
  51.7 0.0 copy-done.1
  51.7 9.0 %shard_map.76 = f32[96,128]{1,0:T(8,128)} custom-call(f32[72,128]{1,0:T(8,128)S(1)} %add_add_fusion.gram_ref, f32[64,128]{1,0:T(8,128)S(1)} %copy-done.1, bf16[3,126,32,128]{3,2,1,0:T(8,128)(2,1)S(1)} %bitcast.22, f32[96,128]{1,0:T(8,128)S(1)} %get-tuple-element.32.first_ref, f32[96,128]{1,0:T(8,128)S(1)} %get-tuple-element.37.second_ref), custom_call_target="tpu_custom_call" | custom-call | tf_op jit(solution)/shard_map/pallas_call | solution.py:522
  (9 shorter events, 0.1 us)
Async XLA Ops:
  2.2 9.7 %copy-start.2 = (f32[32,8,128]{2,1,0:T(8,128)S(1)}, f32[32,8,128]{2,1,0:T(8,128)}, u32[]{:S(2)}) copy-start(f32[32,8,128]{2,1,0:T(8,128)} %get-tuple-element.22) | copy-start | bytes 393220
  2.2 9.7 %collective-permute-start = (f32[3,8,128]{2,1,0:T(8,128)}, f32[3,8,128]{2,1,0:T(8,128)S(1)}, u32[]{:S(2)}, u32[]{:S(2)}) collective-permute-start(f32[3,8,128]{2,1,0:T(8,128)} %get-tuple-element.20), channel_id=1, source_target_pairs={{0,4},{4,8},{8,12},{12,16},{16,20},{20,24},{24,28},{28,0},{1,5},{5... | collective-permute-start | bytes 36872 | tf_op jit(solution)/shard_map/ppermute | solution.py:533
  5.2 6.7 %collective-permute-start.1 = (f32[3,8,128]{2,1,0:T(8,128)}, f32[3,8,128]{2,1,0:T(8,128)S(1)}, u32[]{:S(2)}, u32[]{:S(2)}) collective-permute-start(f32[3,8,128]{2,1,0:T(8,128)} %get-tuple-element.21), channel_id=1, source_target_pairs={{0,28},{4,0},{8,4},{12,8},{16,12},{20,16},{24,20},{28,24},{1,29},{... | collective-permute-start | bytes 36872 | tf_op jit(solution)/shard_map/ppermute | solution.py:533
  11.7 2.3 %copy-start = (bf16[32,1,3,126,128]{4,0,3,2,1:T(8,128)(2,1)S(1)}, bf16[32,1,3,126,128]{4,0,3,2,1:T(8,128)(2,1)}, u32[]{:S(2)}) copy-start(bf16[32,1,3,126,128]{4,0,3,2,1:T(8,128)(2,1)} %param.8) | copy-start | bytes 9289732
  12.0 4.3 %copy-start.3 = (s32[32,1,4]{0,2,1:T(4,128)S(1)}, s32[32,1,4]{0,2,1:T(4,128)}, u32[]{:S(2)}) copy-start(s32[32,1,4]{0,2,1:T(4,128)} %param.7) | copy-start | bytes 1540
  12.0 4.6 %collective-permute-start.3 = (f32[36,8,128]{2,1,0:T(8,128)S(1)}, f32[36,8,128]{2,1,0:T(8,128)S(1)}, u32[]{:S(2)}, u32[]{:S(2)}) collective-permute-start(f32[36,8,128]{2,1,0:T(8,128)S(1)} %pad_maximum_fusion.mid_ref), channel_id=1, source_target_pairs={{0,3},{1,0},{2,1},{3,2},{4,7},{5,4},{6,5},{7,6},{8,11},{9,8},{10,9... | collective-permute-start | bytes 442376 | tf_op jit(solution)/shard_map/ppermute | solution.py:533
  12.7 5.7 %collective-permute-start.2 = (f32[36,8,128]{2,1,0:T(8,128)S(1)}, f32[36,8,128]{2,1,0:T(8,128)S(1)}, u32[]{:S(2)}, u32[]{:S(2)}) collective-permute-start(f32[36,8,128]{2,1,0:T(8,128)S(1)} %pad_maximum_fusion.mid_ref), channel_id=1, source_target_pairs={{0,1},{1,2},{2,3},{3,0},{4,5},{5,6},{6,7},{7,4},{8,9},{9,10},{10,1... | collective-permute-start | bytes 442376 | tf_op jit(solution)/shard_map/ppermute | solution.py:533
  24.3 4.2 %collective-permute-start.5 = (f32[34,8,128]{2,1,0:T(8,128)S(1)}, f32[34,8,128]{2,1,0:T(8,128)S(1)}, u32[]{:S(2)}, u32[]{:S(2)}) collective-permute-start(f32[34,8,128]{2,1,0:T(8,128)S(1)} %shard_map.72.mid_ref.first_ref), channel_id=1, source_target_pairs={{0,3},{1,0},{2,1},{3,2},{4,7},{5,4},{6,5},{7,6},{8,11},{9,8},{10,9... | collective-permute-start | bytes 417800 | tf_op jit(solution)/shard_map/ppermute | solution.py:533
  24.8 5.4 %collective-permute-start.4 = (f32[34,8,128]{2,1,0:T(8,128)S(1)}, f32[34,8,128]{2,1,0:T(8,128)S(1)}, u32[]{:S(2)}, u32[]{:S(2)}) collective-permute-start(f32[34,8,128]{2,1,0:T(8,128)S(1)} %shard_map.72.mid_ref.first_ref), channel_id=1, source_target_pairs={{0,1},{1,2},{2,3},{3,0},{4,5},{5,6},{6,7},{7,4},{8,9},{9,10},{10,1... | collective-permute-start | bytes 417800 | tf_op jit(solution)/shard_map/ppermute | solution.py:533
  27.1 24.6 %copy-start.1 = (f32[64,128]{1,0:T(8,128)S(1)}, f32[64,128]{1,0:T(8,128)}, u32[]{:S(2)}) copy-start(f32[64,128]{1,0:T(8,128)} %shard_map.69.b_ref) | copy-start | bytes 98308
  37.1 1.2 %collective-permute-start.6 = (f32[72,128]{1,0:T(8,128)S(1)}, f32[72,128]{1,0:T(8,128)S(1)}, u32[]{:S(2)}, u32[]{:S(2)}) collective-permute-start(f32[72,128]{1,0:T(8,128)S(1)} %get-tuple-element.35), channel_id=1, source_target_pairs={{0,1},{1,0},{2,3},{3,2},{4,5},{5,4},{6,7},{7,6},{8,9},{9,8},{10,11... | collective-permute-start | bytes 110600 | tf_op jit(solution)/shard_map/ppermute | solution.py:549
  38.3 5.2 %collective-permute-start.9 = (f32[72,128]{1,0:T(8,128)S(1)}, f32[72,128]{1,0:T(8,128)S(1)}, u32[]{:S(2)}, u32[]{:S(2)}) collective-permute-start(f32[72,128]{1,0:T(8,128)S(1)} %add.21), channel_id=1, source_target_pairs={{0,6},{1,7},{2,4},{3,5},{4,2},{5,3},{6,0},{7,1},{8,14},{9,15},{10,... | collective-permute-start | bytes 110600 | tf_op jit(solution)/shard_map/ppermute | solution.py:549
  38.3 5.2 %collective-permute-start.8 = (f32[72,128]{1,0:T(8,128)S(1)}, f32[72,128]{1,0:T(8,128)S(1)}, u32[]{:S(2)}, u32[]{:S(2)}) collective-permute-start(f32[72,128]{1,0:T(8,128)S(1)} %add.21), channel_id=1, source_target_pairs={{0,4},{1,5},{2,6},{3,7},{4,0},{5,1},{6,2},{7,3},{8,12},{9,13},{10,... | collective-permute-start | bytes 110600 | tf_op jit(solution)/shard_map/ppermute | solution.py:549
  40.9 4.0 %collective-permute-start.7 = (f32[72,128]{1,0:T(8,128)S(1)}, f32[72,128]{1,0:T(8,128)S(1)}, u32[]{:S(2)}, u32[]{:S(2)}) collective-permute-start(f32[72,128]{1,0:T(8,128)S(1)} %add.21), channel_id=1, source_target_pairs={{0,2},{1,3},{2,0},{3,1},{4,6},{5,7},{6,4},{7,5},{8,10},{9,11},{10,... | collective-permute-start | bytes 110600 | tf_op jit(solution)/shard_map/ppermute | solution.py:549
  44.9 5.8 %collective-permute-start.12 = (f32[72,128]{1,0:T(8,128)S(1)}, f32[72,128]{1,0:T(8,128)S(1)}, u32[]{:S(2)}, u32[]{:S(2)}) collective-permute-start(f32[72,128]{1,0:T(8,128)S(1)} %add_add_fusion.1), channel_id=1, source_target_pairs={{0,24},{1,25},{2,26},{3,27},{4,28},{5,29},{6,30},{7,31},{8,16},{9,... | collective-permute-start | bytes 110600 | tf_op jit(solution)/shard_map/ppermute | solution.py:549
  46.4 5.2 %collective-permute-start.11 = (f32[72,128]{1,0:T(8,128)S(1)}, f32[72,128]{1,0:T(8,128)S(1)}, u32[]{:S(2)}, u32[]{:S(2)}) collective-permute-start(f32[72,128]{1,0:T(8,128)S(1)} %add_add_fusion.1), channel_id=1, source_target_pairs={{0,16},{1,17},{2,18},{3,19},{4,20},{5,21},{6,22},{7,23},{8,24},{9,... | collective-permute-start | bytes 110600 | tf_op jit(solution)/shard_map/ppermute | solution.py:549
  46.4 5.3 %collective-permute-start.10 = (f32[72,128]{1,0:T(8,128)S(1)}, f32[72,128]{1,0:T(8,128)S(1)}, u32[]{:S(2)}, u32[]{:S(2)}) collective-permute-start(f32[72,128]{1,0:T(8,128)S(1)} %add_add_fusion.1), channel_id=1, source_target_pairs={{0,8},{1,9},{2,10},{3,11},{4,12},{5,13},{6,14},{7,15},{8,0},{9,1},... | collective-permute-start | bytes 110600 | tf_op jit(solution)/shard_map/ppermute | solution.py:549

commit v8 on v7

--- a/solution.py
+++ b/solution.py
@@ -236,7 +236,7 @@
             total = total + hist_ref[c, s].astype(F32) * new[c]
         terms[pl.ds(pl.multiple_of(8 * s, 8), 8), :] = fold(total)
         return 0
-    lax.fori_loop(0, hist, one, 0, unroll=max(u for u in range(1, 10) if hist % u == 0))
+    lax.fori_loop(0, hist, one, 0, unroll=max(u for u in range(1, 43) if hist % u == 0))
     snaps = terms.shape[0] // 8
     for k in range(snaps - hist):
         if k < len(others):
@@ -344,7 +344,7 @@
             def expand(s, _):
                 wide[pl.ds(pl.multiple_of(pitch * s, 8), count), :] = hist_ref[c, s].astype(F32)
                 return 0
-            lax.fori_loop(0, snaps_old, expand, 0, unroll=max(u for u in range(1, 10) if snaps_old % u == 0))
+            lax.fori_loop(0, snaps_old, expand, 0, unroll=max(u for u in range(1, 43) if snaps_old % u == 0))
             for b in range(0, count, 8):
                 x = jnp.concatenate([wide[pl.ds(b + j, snaps_old, stride=pitch), :].astype(BF16) for j in range(8)], axis=1)
                 total = total + lax.dot_general(x, x, (((1,), (1,)), ((), ())), preferred_element_type=F32)
@@ -515,7 +515,7 @@
         def one(s, total):
             wk = table[pl.ds(s, 1), :]
             return [total[c] + wk * hist_ref[c, s].astype(F32) for c in range(comps)]
-        total = lax.fori_loop(0, snaps_old, one, start, unroll=max(u for u in range(1, 10) if snaps_old % u == 0))
+        total = lax.fori_loop(0, snaps_old, one, start, unroll=max(u for u in range(1, 43) if snaps_old % u == 0))
         for c in range(comps):
             out_ref[pl.ds(c, count, stride=comps), :] = total[c]
 

time: 60.9 us -> 60.5 us (level)
  Pallas kernels: 32.7 us -> 32 us
where the time goes in v8:
time: 60.5 us; the launch traced here: 60.3 us
  Pallas kernels  32 us (53%)
  starting transfers between devices  15.3 us (25%)
  waiting for transfers between devices  11.8 us (20%)
  between operations  0.79 us (1%)
    pallas_call x1, Pallas kernels, filtered_field(): pl.pallas_call(kernel, out_shape=jax.ShapeDtypeStruct((count * comps, par...  8.75 us
    ppermute x7, starting transfers between devices, reduce_all(): lax.ppermute(x, axes, [(i * sizes[1] + j, (i ^ s) * sizes[1] + (j ^ v)) f...  8.01 us
    ppermute x6, starting transfers between devices, shift(): return lax.ppermute(x, axis, [(i, (i + by) % count) for i in range(count)])  7.32 us
    pallas_call x1, Pallas kernels, second_step(): pl.pallas_call(kernel, out_shape=(jax.ShapeDtypeStruct((count * 7, part),...  6.72 us
    ppermute x7, waiting for transfers between devices, reduce_all(): lax.ppermute(x, axes, [(i * sizes[1] + j, (i ^ s) * sizes[1] + (j ^ v)) f...  6.58 us
    pallas_call x1, Pallas kernels, first_step(): pl.pallas_call(kernel, out_shape=jax.ShapeDtypeStruct((ext - 2, 8, part),...  5.97 us
    ppermute x6, waiting for transfers between devices, shift(): return lax.ppermute(x, axis, [(i, (i + by) % count) for i in range(count)])  5.24 us
    pallas_call x1, Pallas kernels, start_basis(): pl.pallas_call(kernel, out_shape=jax.ShapeDtypeStruct(basis_t.shape, F32)...  3.42 us
  transfers between devices with their start and end apart: 13, of which 10 were waited for; matrix products, arithmetic and copies ran while one was open for 0% of the time, Pallas kernels for 15%

profile of v8, /device:TPU:0, one launch (start us, length us, event | category | flops | bytes accessed | tf_op | source)
XLA Modules:
  0.0 60.3 jit_solution(7350065747503418493)
XLA Ops:
  0.6 1.6 %shard_map.68 = (f32[32,8,128]{2,1,0:T(8,128)}, f32[3,8,128]{2,1,0:T(8,128)}, f32[3,8,128]{2,1,0:T(8,128)}) custom-call(f32[224,128]{1,0:T(8,128)} %bitcast.23, s32[32,128]{1,0:T(8,128)} %bitcast.25, s32[4,32]{1,0:T(4,128)} %bitcast.26), custom_call_target="tpu_custom_call" | custom-call | tf_op jit(solution)/shard_map/pallas_call | solution.py:84
  2.2 0.0 copy-start.2
  2.2 3.0 %collective-permute-start = (f32[3,8,128]{2,1,0:T(8,128)}, f32[3,8,128]{2,1,0:T(8,128)S(1)}, u32[]{:S(2)}, u32[]{:S(2)}) collective-permute-start(f32[3,8,128]{2,1,0:T(8,128)} %get-tuple-element.20), channel_id=1, source_target_pairs={{0,4},{4,8},{8,12},{12,16},{16,20},{20,24},{24,28},{28,0},{1,5},{5... | collective-permute-start | bytes 36872 | tf_op jit(solution)/shard_map/ppermute | solution.py:533
  5.2 3.1 %collective-permute-start.1 = (f32[3,8,128]{2,1,0:T(8,128)}, f32[3,8,128]{2,1,0:T(8,128)S(1)}, u32[]{:S(2)}, u32[]{:S(2)}) collective-permute-start(f32[3,8,128]{2,1,0:T(8,128)} %get-tuple-element.21), channel_id=1, source_target_pairs={{0,28},{4,0},{8,4},{12,8},{16,12},{20,16},{24,20},{28,24},{1,29},{... | collective-permute-start | bytes 36872 | tf_op jit(solution)/shard_map/ppermute | solution.py:533
  8.3 3.4 %shard_map.69.b_ref = f32[64,128]{1,0:T(8,128)} custom-call(f32[64,128]{1,0:T(8,128)} %bitcast.29), custom_call_target="tpu_custom_call" | custom-call | flops 1073741824 | bytes 1048576 | tf_op jit(solution)/shard_map/pallas_call | solution.py:460
  11.7 0.0 copy-start
  11.7 0.1 stack.42.edge_ref
  11.8 0.1 stack.43.edge_ref
  11.9 0.0 collective-permute-done
  11.9 0.0 collective-permute-done.1
  11.9 0.0 copy-done.2
  12.0 0.0 copy-start.3
  12.0 0.7 %collective-permute-start.3 = (f32[36,8,128]{2,1,0:T(8,128)S(1)}, f32[36,8,128]{2,1,0:T(8,128)S(1)}, u32[]{:S(2)}, u32[]{:S(2)}) collective-permute-start(f32[36,8,128]{2,1,0:T(8,128)S(1)} %pad_maximum_fusion.mid_ref), channel_id=1, source_target_pairs={{0,3},{1,0},{2,1},{3,2},{4,7},{5,4},{6,5},{7,6},{8,11},{9,8},{10,9... | collective-permute-start | bytes 442376 | tf_op jit(solution)/shard_map/ppermute | solution.py:533
  12.7 0.0 collective-permute-start.2
  12.7 1.3 %shard_map.70 = (f32[34,24,128]{2,1,0:T(8,128)S(1)}, bf16[34,48,128]{2,1,0:T(8,128)(2,1)S(1)}) custom-call(f32[36,8,128]{2,1,0:T(8,128)S(1)} %pad_maximum_fusion.mid_ref), custom_call_target="tpu_custom_call" | custom-call | flops 1073741824 | bytes 1048576 | tf_op jit(solution)/shard_map/pallas_call | solution.py:328
  14.0 0.0 copy-done
  14.1 2.1 %shard_map.71.gram_ref = f32[128,128]{1,0:T(8,128)S(1)} custom-call(bf16[3,126,32,128]{3,2,1,0:T(8,128)(2,1)S(1)} %bitcast.19), custom_call_target="tpu_custom_call" | custom-call | flops 402653184 | bytes 3145728 | tf_op jit(solution)/shard_map/pallas_call | solution.py:354
  16.2 0.0 copy-done.3
  16.2 0.1 pad_add_fusion.codes_ref
  16.3 0.3 collective-permute-done.3.high_ref
  16.5 1.8 %collective-permute-done.2.low_ref = f32[36,8,128]{2,1,0:T(8,128)S(1)} collective-permute-done((f32[36,8,128]{2,1,0:T(8,128)S(1)}, f32[36,8,128]{2,1,0:T(8,128)S(1)}, u32[]{:S(2)}, u32[]{:S(2)}) %collective-permute-start.2) | collective-permute-done | bytes 147488 | tf_op jit(solution)/shard_map/ppermute | solution.py:533
  18.3 6.0 %shard_map.72.mid_ref.first_ref = f32[34,8,128]{2,1,0:T(8,128)S(1)} custom-call(s32[4,34]{1,0:T(4,128)S(1)} %pad_add_fusion.codes_ref, s32[8]{0:T(128)S(1)} %stack.43.edge_ref, f32[36,8,128]{2,1,0:T(8,128)S(1)} %collective-permute-done.2.low_ref, f32[36,8,128]{2,1,0:T(8,128)S(1)} %pad_maximum_fusion.mid_ref, ...), custom_call_target="tpu_custom_call" | custom-call | tf_op jit(solution)/shard_map/pallas_call | solution.py:215
  24.3 0.5 collective-permute-start.5
  24.8 0.1 collective-permute-start.4
  24.9 1.3 %shard_map.73 = (f32[32,24,128]{2,1,0:T(8,128)S(1)}, bf16[32,48,128]{2,1,0:T(8,128)(2,1)S(1)}) custom-call(f32[34,8,128]{2,1,0:T(8,128)S(1)} %shard_map.72.mid_ref.first_ref), custom_call_target="tpu_custom_call" | custom-call | flops 1073741824 | bytes 1048576 | tf_op jit(solution)/shard_map/pallas_call | solution.py:328
  26.1 0.9 %shard_map.74 = (f32[128,128]{1,0:T(8,128)S(1)}, f32[96,128]{1,0:T(8,128)S(1)}) custom-call(bf16[3,126,32,128]{3,2,1,0:T(8,128)(2,1)S(1)} %bitcast.20, f32[34,8,128]{2,1,0:T(8,128)S(1)} %shard_map.72.mid_ref.first_ref, f32[128,128]{1,0:T(8,128)S(1)} %shard_map.71.gram_ref), custom_call_target="tpu_custom_call" | custom-call | flops 1073741824 | bytes 3145728 | tf_op jit(solution)/shard_map/pallas_call | solution.py:377
  27.0 0.0 copy-start.1
  27.0 1.5 %collective-permute-done.5.high_ref = f32[34,8,128]{2,1,0:T(8,128)S(1)} collective-permute-done((f32[34,8,128]{2,1,0:T(8,128)S(1)}, f32[34,8,128]{2,1,0:T(8,128)S(1)}, u32[]{:S(2)}, u32[]{:S(2)}) %collective-permute-start.5) | collective-permute-done | bytes 139296 | tf_op jit(solution)/shard_map/ppermute | solution.py:533
  28.5 1.7 %collective-permute-done.4.low_ref = f32[34,8,128]{2,1,0:T(8,128)S(1)} collective-permute-done((f32[34,8,128]{2,1,0:T(8,128)S(1)}, f32[34,8,128]{2,1,0:T(8,128)S(1)}, u32[]{:S(2)}, u32[]{:S(2)}) %collective-permute-start.4) | collective-permute-done | bytes 139296 | tf_op jit(solution)/shard_map/ppermute | solution.py:533
  30.2 6.7 %shard_map.75 = (f32[224,128]{1,0:T(8,128)}, f32[96,128]{1,0:T(8,128)S(1)}, f32[72,128]{1,0:T(8,128)S(1)}) custom-call(s32[4,34]{1,0:T(4,128)S(1)} %pad_add_fusion.codes_ref, s32[8]{0:T(128)S(1)} %stack.42.edge_ref, f32[34,8,128]{2,1,0:T(8,128)S(1)} %collective-permute-done.4.low_ref, f32[34,8,128]{2,1,0:T(8,128)S(1)} %shard_map.72.mid_ref.first_ref, ...), custom_call_target="tpu_custom_call" | custom-call | tf_op jit(solution)/shard_map/pallas_call | solution.py:310
  36.9 0.1 collective-permute-start.6
  37.0 1.2 %collective-permute-done.6 = f32[72,128]{1,0:T(8,128)S(1)} collective-permute-done((f32[72,128]{1,0:T(8,128)S(1)}, f32[72,128]{1,0:T(8,128)S(1)}, u32[]{:S(2)}, u32[]{:S(2)}) %collective-permute-start.6) | collective-permute-done | bytes 36896 | tf_op jit(solution)/shard_map/ppermute | solution.py:549
  38.2 0.0 collective-permute-start.9
  38.2 2.6 %collective-permute-start.8 = (f32[72,128]{1,0:T(8,128)S(1)}, f32[72,128]{1,0:T(8,128)S(1)}, u32[]{:S(2)}, u32[]{:S(2)}) collective-permute-start(f32[72,128]{1,0:T(8,128)S(1)} %add.21), channel_id=1, source_target_pairs={{0,4},{1,5},{2,6},{3,7},{4,0},{5,1},{6,2},{7,3},{8,12},{9,13},{10,... | collective-permute-start | bytes 110600 | tf_op jit(solution)/shard_map/ppermute | solution.py:549
  40.8 0.9 %collective-permute-start.7 = (f32[72,128]{1,0:T(8,128)S(1)}, f32[72,128]{1,0:T(8,128)S(1)}, u32[]{:S(2)}, u32[]{:S(2)}) collective-permute-start(f32[72,128]{1,0:T(8,128)S(1)} %add.21), channel_id=1, source_target_pairs={{0,2},{1,3},{2,0},{3,1},{4,6},{5,7},{6,4},{7,5},{8,10},{9,11},{10,... | collective-permute-start | bytes 110600 | tf_op jit(solution)/shard_map/ppermute | solution.py:549
  41.7 1.7 %collective-permute-done.9 = f32[72,128]{1,0:T(8,128)S(1)} collective-permute-done((f32[72,128]{1,0:T(8,128)S(1)}, f32[72,128]{1,0:T(8,128)S(1)}, u32[]{:S(2)}, u32[]{:S(2)}) %collective-permute-start.9) | collective-permute-done | bytes 36896 | tf_op jit(solution)/shard_map/ppermute | solution.py:549
  43.4 0.0 collective-permute-done.8
  43.4 1.3 %collective-permute-done.7 = f32[72,128]{1,0:T(8,128)S(1)} collective-permute-done((f32[72,128]{1,0:T(8,128)S(1)}, f32[72,128]{1,0:T(8,128)S(1)}, u32[]{:S(2)}, u32[]{:S(2)}) %collective-permute-start.7) | collective-permute-done | bytes 36896 | tf_op jit(solution)/shard_map/ppermute | solution.py:549
  44.8 1.5 %collective-permute-start.12 = (f32[72,128]{1,0:T(8,128)S(1)}, f32[72,128]{1,0:T(8,128)S(1)}, u32[]{:S(2)}, u32[]{:S(2)}) collective-permute-start(f32[72,128]{1,0:T(8,128)S(1)} %add_add_fusion.1), channel_id=1, source_target_pairs={{0,24},{1,25},{2,26},{3,27},{4,28},{5,29},{6,30},{7,31},{8,16},{9,... | collective-permute-start | bytes 110600 | tf_op jit(solution)/shard_map/ppermute | solution.py:549
  46.3 0.0 collective-permute-start.11
  46.3 2.9 %collective-permute-start.10 = (f32[72,128]{1,0:T(8,128)S(1)}, f32[72,128]{1,0:T(8,128)S(1)}, u32[]{:S(2)}, u32[]{:S(2)}) collective-permute-start(f32[72,128]{1,0:T(8,128)S(1)} %add_add_fusion.1), channel_id=1, source_target_pairs={{0,8},{1,9},{2,10},{3,11},{4,12},{5,13},{6,14},{7,15},{8,0},{9,1},... | collective-permute-start | bytes 110600 | tf_op jit(solution)/shard_map/ppermute | solution.py:549
  49.2 1.4 %collective-permute-done.12 = f32[72,128]{1,0:T(8,128)S(1)} collective-permute-done((f32[72,128]{1,0:T(8,128)S(1)}, f32[72,128]{1,0:T(8,128)S(1)}, u32[]{:S(2)}, u32[]{:S(2)}) %collective-permute-start.12) | collective-permute-done | bytes 36896 | tf_op jit(solution)/shard_map/ppermute | solution.py:549
  50.6 0.9 %collective-permute-done.11 = f32[72,128]{1,0:T(8,128)S(1)} collective-permute-done((f32[72,128]{1,0:T(8,128)S(1)}, f32[72,128]{1,0:T(8,128)S(1)}, u32[]{:S(2)}, u32[]{:S(2)}) %collective-permute-start.11) | collective-permute-done | bytes 36896 | tf_op jit(solution)/shard_map/ppermute | solution.py:549
  51.5 0.1 collective-permute-done.10
  51.5 0.0 copy-done.1
  51.6 8.7 %shard_map.76 = f32[96,128]{1,0:T(8,128)} custom-call(f32[72,128]{1,0:T(8,128)S(1)} %add_add_fusion.gram_ref, f32[64,128]{1,0:T(8,128)S(1)} %copy-done.1, bf16[3,126,32,128]{3,2,1,0:T(8,128)(2,1)S(1)} %bitcast.22, f32[96,128]{1,0:T(8,128)S(1)} %get-tuple-element.32.first_ref, f32[96,128]{1,0:T(8,128)S(1)} %get-tuple-element.37.second_ref), custom_call_target="tpu_custom_call" | custom-call | tf_op jit(solution)/shard_map/pallas_call | solution.py:522
  (9 shorter events, 0.1 us)
Async XLA Ops:
  2.2 9.7 %copy-start.2 = (f32[32,8,128]{2,1,0:T(8,128)S(1)}, f32[32,8,128]{2,1,0:T(8,128)}, u32[]{:S(2)}) copy-start(f32[32,8,128]{2,1,0:T(8,128)} %get-tuple-element.22) | copy-start | bytes 393220
  2.2 9.7 %collective-permute-start = (f32[3,8,128]{2,1,0:T(8,128)}, f32[3,8,128]{2,1,0:T(8,128)S(1)}, u32[]{:S(2)}, u32[]{:S(2)}) collective-permute-start(f32[3,8,128]{2,1,0:T(8,128)} %get-tuple-element.20), channel_id=1, source_target_pairs={{0,4},{4,8},{8,12},{12,16},{16,20},{20,24},{24,28},{28,0},{1,5},{5... | collective-permute-start | bytes 36872 | tf_op jit(solution)/shard_map/ppermute | solution.py:533
  5.2 6.7 %collective-permute-start.1 = (f32[3,8,128]{2,1,0:T(8,128)}, f32[3,8,128]{2,1,0:T(8,128)S(1)}, u32[]{:S(2)}, u32[]{:S(2)}) collective-permute-start(f32[3,8,128]{2,1,0:T(8,128)} %get-tuple-element.21), channel_id=1, source_target_pairs={{0,28},{4,0},{8,4},{12,8},{16,12},{20,16},{24,20},{28,24},{1,29},{... | collective-permute-start | bytes 36872 | tf_op jit(solution)/shard_map/ppermute | solution.py:533
  11.7 2.3 %copy-start = (bf16[32,1,3,126,128]{4,0,3,2,1:T(8,128)(2,1)S(1)}, bf16[32,1,3,126,128]{4,0,3,2,1:T(8,128)(2,1)}, u32[]{:S(2)}) copy-start(bf16[32,1,3,126,128]{4,0,3,2,1:T(8,128)(2,1)} %param.8) | copy-start | bytes 9289732
  12.0 4.2 %copy-start.3 = (s32[32,1,4]{0,2,1:T(4,128)S(1)}, s32[32,1,4]{0,2,1:T(4,128)}, u32[]{:S(2)}) copy-start(s32[32,1,4]{0,2,1:T(4,128)} %param.7) | copy-start | bytes 1540
  12.0 4.6 %collective-permute-start.3 = (f32[36,8,128]{2,1,0:T(8,128)S(1)}, f32[36,8,128]{2,1,0:T(8,128)S(1)}, u32[]{:S(2)}, u32[]{:S(2)}) collective-permute-start(f32[36,8,128]{2,1,0:T(8,128)S(1)} %pad_maximum_fusion.mid_ref), channel_id=1, source_target_pairs={{0,3},{1,0},{2,1},{3,2},{4,7},{5,4},{6,5},{7,6},{8,11},{9,8},{10,9... | collective-permute-start | bytes 442376 | tf_op jit(solution)/shard_map/ppermute | solution.py:533
  12.7 5.7 %collective-permute-start.2 = (f32[36,8,128]{2,1,0:T(8,128)S(1)}, f32[36,8,128]{2,1,0:T(8,128)S(1)}, u32[]{:S(2)}, u32[]{:S(2)}) collective-permute-start(f32[36,8,128]{2,1,0:T(8,128)S(1)} %pad_maximum_fusion.mid_ref), channel_id=1, source_target_pairs={{0,1},{1,2},{2,3},{3,0},{4,5},{5,6},{6,7},{7,4},{8,9},{9,10},{10,1... | collective-permute-start | bytes 442376 | tf_op jit(solution)/shard_map/ppermute | solution.py:533
  24.3 4.2 %collective-permute-start.5 = (f32[34,8,128]{2,1,0:T(8,128)S(1)}, f32[34,8,128]{2,1,0:T(8,128)S(1)}, u32[]{:S(2)}, u32[]{:S(2)}) collective-permute-start(f32[34,8,128]{2,1,0:T(8,128)S(1)} %shard_map.72.mid_ref.first_ref), channel_id=1, source_target_pairs={{0,3},{1,0},{2,1},{3,2},{4,7},{5,4},{6,5},{7,6},{8,11},{9,8},{10,9... | collective-permute-start | bytes 417800 | tf_op jit(solution)/shard_map/ppermute | solution.py:533
  24.8 5.4 %collective-permute-start.4 = (f32[34,8,128]{2,1,0:T(8,128)S(1)}, f32[34,8,128]{2,1,0:T(8,128)S(1)}, u32[]{:S(2)}, u32[]{:S(2)}) collective-permute-start(f32[34,8,128]{2,1,0:T(8,128)S(1)} %shard_map.72.mid_ref.first_ref), channel_id=1, source_target_pairs={{0,1},{1,2},{2,3},{3,0},{4,5},{5,6},{6,7},{7,4},{8,9},{9,10},{10,1... | collective-permute-start | bytes 417800 | tf_op jit(solution)/shard_map/ppermute | solution.py:533
  27.0 24.5 %copy-start.1 = (f32[64,128]{1,0:T(8,128)S(1)}, f32[64,128]{1,0:T(8,128)}, u32[]{:S(2)}) copy-start(f32[64,128]{1,0:T(8,128)} %shard_map.69.b_ref) | copy-start | bytes 98308
  36.9 1.3 %collective-permute-start.6 = (f32[72,128]{1,0:T(8,128)S(1)}, f32[72,128]{1,0:T(8,128)S(1)}, u32[]{:S(2)}, u32[]{:S(2)}) collective-permute-start(f32[72,128]{1,0:T(8,128)S(1)} %get-tuple-element.35), channel_id=1, source_target_pairs={{0,1},{1,0},{2,3},{3,2},{4,5},{5,4},{6,7},{7,6},{8,9},{9,8},{10,11... | collective-permute-start | bytes 110600 | tf_op jit(solution)/shard_map/ppermute | solution.py:549
  38.2 5.2 %collective-permute-start.9 = (f32[72,128]{1,0:T(8,128)S(1)}, f32[72,128]{1,0:T(8,128)S(1)}, u32[]{:S(2)}, u32[]{:S(2)}) collective-permute-start(f32[72,128]{1,0:T(8,128)S(1)} %add.21), channel_id=1, source_target_pairs={{0,6},{1,7},{2,4},{3,5},{4,2},{5,3},{6,0},{7,1},{8,14},{9,15},{10,... | collective-permute-start | bytes 110600 | tf_op jit(solution)/shard_map/ppermute | solution.py:549
  38.2 5.2 %collective-permute-start.8 = (f32[72,128]{1,0:T(8,128)S(1)}, f32[72,128]{1,0:T(8,128)S(1)}, u32[]{:S(2)}, u32[]{:S(2)}) collective-permute-start(f32[72,128]{1,0:T(8,128)S(1)} %add.21), channel_id=1, source_target_pairs={{0,4},{1,5},{2,6},{3,7},{4,0},{5,1},{6,2},{7,3},{8,12},{9,13},{10,... | collective-permute-start | bytes 110600 | tf_op jit(solution)/shard_map/ppermute | solution.py:549
  40.8 4.0 %collective-permute-start.7 = (f32[72,128]{1,0:T(8,128)S(1)}, f32[72,128]{1,0:T(8,128)S(1)}, u32[]{:S(2)}, u32[]{:S(2)}) collective-permute-start(f32[72,128]{1,0:T(8,128)S(1)} %add.21), channel_id=1, source_target_pairs={{0,2},{1,3},{2,0},{3,1},{4,6},{5,7},{6,4},{7,5},{8,10},{9,11},{10,... | collective-permute-start | bytes 110600 | tf_op jit(solution)/shard_map/ppermute | solution.py:549
  44.8 5.8 %collective-permute-start.12 = (f32[72,128]{1,0:T(8,128)S(1)}, f32[72,128]{1,0:T(8,128)S(1)}, u32[]{:S(2)}, u32[]{:S(2)}) collective-permute-start(f32[72,128]{1,0:T(8,128)S(1)} %add_add_fusion.1), channel_id=1, source_target_pairs={{0,24},{1,25},{2,26},{3,27},{4,28},{5,29},{6,30},{7,31},{8,16},{9,... | collective-permute-start | bytes 110600 | tf_op jit(solution)/shard_map/ppermute | solution.py:549
  46.3 5.2 %collective-permute-start.11 = (f32[72,128]{1,0:T(8,128)S(1)}, f32[72,128]{1,0:T(8,128)S(1)}, u32[]{:S(2)}, u32[]{:S(2)}) collective-permute-start(f32[72,128]{1,0:T(8,128)S(1)} %add_add_fusion.1), channel_id=1, source_target_pairs={{0,16},{1,17},{2,18},{3,19},{4,20},{5,21},{6,22},{7,23},{8,24},{9,... | collective-permute-start | bytes 110600 | tf_op jit(solution)/shard_map/ppermute | solution.py:549
  46.3 5.3 %collective-permute-start.10 = (f32[72,128]{1,0:T(8,128)S(1)}, f32[72,128]{1,0:T(8,128)S(1)}, u32[]{:S(2)}, u32[]{:S(2)}) collective-permute-start(f32[72,128]{1,0:T(8,128)S(1)} %add_add_fusion.1), channel_id=1, source_target_pairs={{0,8},{1,9},{2,10},{3,11},{4,12},{5,13},{6,14},{7,15},{8,0},{9,1},... | collective-permute-start | bytes 110600 | tf_op jit(solution)/shard_map/ppermute | solution.py:549

commit v9 on v8

--- a/solution.py
+++ b/solution.py
@@ -388,8 +388,18 @@
 JOIN_ABOVE = 1e-4
 
 
+def left_pieces(x, axis):
+    a, b, c = pieces(x)
+    return jnp.concatenate([a, a, b, b, a, c], axis=axis).astype(BF16)
+
+
+def right_pieces(x, axis):
+    a, b, c = pieces(x)
+    return jnp.concatenate([a, b, a, b, c, a], axis=axis).astype(BF16)
+
+
 def gram_of(m):
-    return lax.dot_general(m, m, (((1,), (1,)), ((), ())), precision=HIGHEST, preferred_element_type=F32)
+    return lax.dot_general(left_pieces(m, 1), right_pieces(m, 1), (((1,), (1,)), ((), ())), preferred_element_type=F32)
 
 
 def orthonormal(m):
@@ -463,7 +473,7 @@
     )(basis_t)
 
 
-def weigh(iters, packed_ref, g_ref, b_ref, q_ref):
+def weigh(iters, packed_ref, g_ref, split_ref, b_ref, q_ref):
     snaps = g_ref.shape[0]
     rows_in, cols_in = corner(snaps)
     g = unpack(packed_ref)
@@ -471,8 +481,10 @@
     g_ref[...] = g * (1.0 / trace)
     q_ref[...] = b_ref[...]
 
+    split_ref[...] = right_pieces(g_ref[...], 0)
+
     def product(q):
-        return jnp.dot(q, g_ref[...], precision=HIGHEST, preferred_element_type=F32)
+        return jnp.dot(left_pieces(q, 1), split_ref[...], preferred_element_type=F32)
 
     q, checks = b_ref[...], []
     for k in range(iters - 1):
@@ -505,8 +517,8 @@
     comps, snaps_old, count, part = hist.shape
     v = pl.BlockSpec(memory_space=pltpu.VMEM)
 
-    def kernel(gram_ref, b_ref, hist_ref, first_ref, second_ref, out_ref, g_ref, q_ref, table):
-        w = weigh(POD_ITERS, gram_ref, g_ref, b_ref, q_ref)
+    def kernel(gram_ref, b_ref, hist_ref, first_ref, second_ref, out_ref, g_ref, split_ref, q_ref, table):
+        w = weigh(POD_ITERS, gram_ref, g_ref, split_ref, b_ref, q_ref)
         table[...] = jnp.broadcast_to(w, table.shape).T
         w1, w2 = (table[snaps_old + k:snaps_old + k + 1] for k in range(2))
         parts = [slice(count * c, count * (c + 1)) for c in range(comps)]
@@ -522,7 +534,8 @@
     return pl.pallas_call(
         kernel, out_shape=jax.ShapeDtypeStruct((count * comps, part), F32),
         in_specs=[v, v, v, v, v], out_specs=v,
-        scratch_shapes=[pltpu.VMEM((snaps_old + 2, snaps_old + 2), F32), pltpu.VMEM(basis_t.shape, F32),
+        scratch_shapes=[pltpu.VMEM((snaps_old + 2, snaps_old + 2), F32), pltpu.VMEM((6 * (snaps_old + 2), snaps_old + 2), BF16),
+                        pltpu.VMEM(basis_t.shape, F32),
                         pltpu.VMEM((snaps_old + 2, snaps_old + 2), F32)],
         compiler_params=pltpu.CompilerParams(vmem_limit_bytes=VMEM_LIMIT),
     )(gram, basis_t, hist, first, second)

time: 60.5 us -> 60.3 us (level)
  no operation moved by 1% of the time
where the time goes in v9:
time: 60.3 us; the launch traced here: 60.1 us
  Pallas kernels  31.8 us (53%)
  starting transfers between devices  15.3 us (25%)
  waiting for transfers between devices  11.8 us (20%)
  between operations  0.79 us (1%)
    pallas_call x1, Pallas kernels, filtered_field(): pl.pallas_call(kernel, out_shape=jax.ShapeDtypeStruct((count * comps, par...  8.5 us
    ppermute x7, starting transfers between devices, reduce_all(): lax.ppermute(x, axes, [(i * sizes[1] + j, (i ^ s) * sizes[1] + (j ^ v)) f...  8.01 us
    ppermute x6, starting transfers between devices, shift(): return lax.ppermute(x, axis, [(i, (i + by) % count) for i in range(count)])  7.32 us
    pallas_call x1, Pallas kernels, second_step(): pl.pallas_call(kernel, out_shape=(jax.ShapeDtypeStruct((count * 7, part),...  6.71 us
    ppermute x7, waiting for transfers between devices, reduce_all(): lax.ppermute(x, axes, [(i * sizes[1] + j, (i ^ s) * sizes[1] + (j ^ v)) f...  6.59 us
    pallas_call x1, Pallas kernels, first_step(): pl.pallas_call(kernel, out_shape=jax.ShapeDtypeStruct((ext - 2, 8, part),...  5.97 us
    ppermute x6, waiting for transfers between devices, shift(): return lax.ppermute(x, axis, [(i, (i + by) % count) for i in range(count)])  5.26 us
    pallas_call x1, Pallas kernels, start_basis(): pl.pallas_call(kernel, out_shape=jax.ShapeDtypeStruct(basis_t.shape, F32)...  3.42 us
  transfers between devices with their start and end apart: 13, of which 10 were waited for; matrix products, arithmetic and copies ran while one was open for 0% of the time, Pallas kernels for 15%

profile of v9, /device:TPU:0, one launch (start us, length us, event | category | flops | bytes accessed | tf_op | source)
XLA Modules:
  0.0 60.1 jit_solution(5475806902626641768)
XLA Ops:
  0.6 1.6 %shard_map.68 = (f32[32,8,128]{2,1,0:T(8,128)}, f32[3,8,128]{2,1,0:T(8,128)}, f32[3,8,128]{2,1,0:T(8,128)}) custom-call(f32[224,128]{1,0:T(8,128)} %bitcast.23, s32[32,128]{1,0:T(8,128)} %bitcast.25, s32[4,32]{1,0:T(4,128)} %bitcast.26), custom_call_target="tpu_custom_call" | custom-call | tf_op jit(solution)/shard_map/pallas_call | solution.py:84
  2.2 0.0 copy-start.2
  2.2 3.0 %collective-permute-start = (f32[3,8,128]{2,1,0:T(8,128)}, f32[3,8,128]{2,1,0:T(8,128)S(1)}, u32[]{:S(2)}, u32[]{:S(2)}) collective-permute-start(f32[3,8,128]{2,1,0:T(8,128)} %get-tuple-element.20), channel_id=1, source_target_pairs={{0,4},{4,8},{8,12},{12,16},{16,20},{20,24},{24,28},{28,0},{1,5},{5... | collective-permute-start | bytes 36872 | tf_op jit(solution)/shard_map/ppermute | solution.py:546
  5.2 3.1 %collective-permute-start.1 = (f32[3,8,128]{2,1,0:T(8,128)}, f32[3,8,128]{2,1,0:T(8,128)S(1)}, u32[]{:S(2)}, u32[]{:S(2)}) collective-permute-start(f32[3,8,128]{2,1,0:T(8,128)} %get-tuple-element.21), channel_id=1, source_target_pairs={{0,28},{4,0},{8,4},{12,8},{16,12},{20,16},{24,20},{28,24},{1,29},{... | collective-permute-start | bytes 36872 | tf_op jit(solution)/shard_map/ppermute | solution.py:546
  8.3 3.4 %shard_map.69.b_ref = f32[64,128]{1,0:T(8,128)} custom-call(f32[64,128]{1,0:T(8,128)} %bitcast.29), custom_call_target="tpu_custom_call" | custom-call | flops 1073741824 | bytes 1048576 | tf_op jit(solution)/shard_map/pallas_call | solution.py:470
  11.7 0.0 copy-start
  11.7 0.1 stack.42.edge_ref
  11.8 0.1 stack.43.edge_ref
  11.9 0.0 collective-permute-done
  11.9 0.0 collective-permute-done.1
  11.9 0.0 copy-done.2
  12.0 0.0 copy-start.3
  12.0 0.7 %collective-permute-start.3 = (f32[36,8,128]{2,1,0:T(8,128)S(1)}, f32[36,8,128]{2,1,0:T(8,128)S(1)}, u32[]{:S(2)}, u32[]{:S(2)}) collective-permute-start(f32[36,8,128]{2,1,0:T(8,128)S(1)} %pad_maximum_fusion.mid_ref), channel_id=1, source_target_pairs={{0,3},{1,0},{2,1},{3,2},{4,7},{5,4},{6,5},{7,6},{8,11},{9,8},{10,9... | collective-permute-start | bytes 442376 | tf_op jit(solution)/shard_map/ppermute | solution.py:546
  12.7 0.0 collective-permute-start.2
  12.7 1.3 %shard_map.70 = (f32[34,24,128]{2,1,0:T(8,128)S(1)}, bf16[34,48,128]{2,1,0:T(8,128)(2,1)S(1)}) custom-call(f32[36,8,128]{2,1,0:T(8,128)S(1)} %pad_maximum_fusion.mid_ref), custom_call_target="tpu_custom_call" | custom-call | flops 1073741824 | bytes 1048576 | tf_op jit(solution)/shard_map/pallas_call | solution.py:328
  14.0 0.0 copy-done
  14.1 2.1 %shard_map.71.gram_ref = f32[128,128]{1,0:T(8,128)S(1)} custom-call(bf16[3,126,32,128]{3,2,1,0:T(8,128)(2,1)S(1)} %bitcast.19), custom_call_target="tpu_custom_call" | custom-call | flops 402653184 | bytes 3145728 | tf_op jit(solution)/shard_map/pallas_call | solution.py:354
  16.2 0.0 copy-done.3
  16.2 0.1 pad_add_fusion.codes_ref
  16.2 0.3 collective-permute-done.3.high_ref
  16.5 1.8 %collective-permute-done.2.low_ref = f32[36,8,128]{2,1,0:T(8,128)S(1)} collective-permute-done((f32[36,8,128]{2,1,0:T(8,128)S(1)}, f32[36,8,128]{2,1,0:T(8,128)S(1)}, u32[]{:S(2)}, u32[]{:S(2)}) %collective-permute-start.2) | collective-permute-done | bytes 147488 | tf_op jit(solution)/shard_map/ppermute | solution.py:546
  18.3 6.0 %shard_map.72.mid_ref.first_ref = f32[34,8,128]{2,1,0:T(8,128)S(1)} custom-call(s32[4,34]{1,0:T(4,128)S(1)} %pad_add_fusion.codes_ref, s32[8]{0:T(128)S(1)} %stack.43.edge_ref, f32[36,8,128]{2,1,0:T(8,128)S(1)} %collective-permute-done.2.low_ref, f32[36,8,128]{2,1,0:T(8,128)S(1)} %pad_maximum_fusion.mid_ref, ...), custom_call_target="tpu_custom_call" | custom-call | tf_op jit(solution)/shard_map/pallas_call | solution.py:215
  24.3 0.5 collective-permute-start.5
  24.8 0.1 collective-permute-start.4
  24.9 1.3 %shard_map.73 = (f32[32,24,128]{2,1,0:T(8,128)S(1)}, bf16[32,48,128]{2,1,0:T(8,128)(2,1)S(1)}) custom-call(f32[34,8,128]{2,1,0:T(8,128)S(1)} %shard_map.72.mid_ref.first_ref), custom_call_target="tpu_custom_call" | custom-call | flops 1073741824 | bytes 1048576 | tf_op jit(solution)/shard_map/pallas_call | solution.py:328
  26.1 0.9 %shard_map.74 = (f32[128,128]{1,0:T(8,128)S(1)}, f32[96,128]{1,0:T(8,128)S(1)}) custom-call(bf16[3,126,32,128]{3,2,1,0:T(8,128)(2,1)S(1)} %bitcast.20, f32[34,8,128]{2,1,0:T(8,128)S(1)} %shard_map.72.mid_ref.first_ref, f32[128,128]{1,0:T(8,128)S(1)} %shard_map.71.gram_ref), custom_call_target="tpu_custom_call" | custom-call | flops 1073741824 | bytes 3145728 | tf_op jit(solution)/shard_map/pallas_call | solution.py:377
  27.0 0.0 copy-start.1
  27.0 1.5 %collective-permute-done.5.high_ref = f32[34,8,128]{2,1,0:T(8,128)S(1)} collective-permute-done((f32[34,8,128]{2,1,0:T(8,128)S(1)}, f32[34,8,128]{2,1,0:T(8,128)S(1)}, u32[]{:S(2)}, u32[]{:S(2)}) %collective-permute-start.5) | collective-permute-done | bytes 139296 | tf_op jit(solution)/shard_map/ppermute | solution.py:546
  28.5 1.7 %collective-permute-done.4.low_ref = f32[34,8,128]{2,1,0:T(8,128)S(1)} collective-permute-done((f32[34,8,128]{2,1,0:T(8,128)S(1)}, f32[34,8,128]{2,1,0:T(8,128)S(1)}, u32[]{:S(2)}, u32[]{:S(2)}) %collective-permute-start.4) | collective-permute-done | bytes 139296 | tf_op jit(solution)/shard_map/ppermute | solution.py:546
  30.2 6.7 %shard_map.75 = (f32[224,128]{1,0:T(8,128)}, f32[96,128]{1,0:T(8,128)S(1)}, f32[72,128]{1,0:T(8,128)S(1)}) custom-call(s32[4,34]{1,0:T(4,128)S(1)} %pad_add_fusion.codes_ref, s32[8]{0:T(128)S(1)} %stack.42.edge_ref, f32[34,8,128]{2,1,0:T(8,128)S(1)} %collective-permute-done.4.low_ref, f32[34,8,128]{2,1,0:T(8,128)S(1)} %shard_map.72.mid_ref.first_ref, ...), custom_call_target="tpu_custom_call" | custom-call | tf_op jit(solution)/shard_map/pallas_call | solution.py:310
  36.9 0.1 collective-permute-start.6
  37.0 1.2 %collective-permute-done.6 = f32[72,128]{1,0:T(8,128)S(1)} collective-permute-done((f32[72,128]{1,0:T(8,128)S(1)}, f32[72,128]{1,0:T(8,128)S(1)}, u32[]{:S(2)}, u32[]{:S(2)}) %collective-permute-start.6) | collective-permute-done | bytes 36896 | tf_op jit(solution)/shard_map/ppermute | solution.py:562
  38.2 0.0 collective-permute-start.9
  38.2 2.6 %collective-permute-start.8 = (f32[72,128]{1,0:T(8,128)S(1)}, f32[72,128]{1,0:T(8,128)S(1)}, u32[]{:S(2)}, u32[]{:S(2)}) collective-permute-start(f32[72,128]{1,0:T(8,128)S(1)} %add.21), channel_id=1, source_target_pairs={{0,4},{1,5},{2,6},{3,7},{4,0},{5,1},{6,2},{7,3},{8,12},{9,13},{10,... | collective-permute-start | bytes 110600 | tf_op jit(solution)/shard_map/ppermute | solution.py:562
  40.8 0.9 %collective-permute-start.7 = (f32[72,128]{1,0:T(8,128)S(1)}, f32[72,128]{1,0:T(8,128)S(1)}, u32[]{:S(2)}, u32[]{:S(2)}) collective-permute-start(f32[72,128]{1,0:T(8,128)S(1)} %add.21), channel_id=1, source_target_pairs={{0,2},{1,3},{2,0},{3,1},{4,6},{5,7},{6,4},{7,5},{8,10},{9,11},{10,... | collective-permute-start | bytes 110600 | tf_op jit(solution)/shard_map/ppermute | solution.py:562
  41.7 1.7 %collective-permute-done.9 = f32[72,128]{1,0:T(8,128)S(1)} collective-permute-done((f32[72,128]{1,0:T(8,128)S(1)}, f32[72,128]{1,0:T(8,128)S(1)}, u32[]{:S(2)}, u32[]{:S(2)}) %collective-permute-start.9) | collective-permute-done | bytes 36896 | tf_op jit(solution)/shard_map/ppermute | solution.py:562
  43.4 0.0 collective-permute-done.8
  43.4 1.3 %collective-permute-done.7 = f32[72,128]{1,0:T(8,128)S(1)} collective-permute-done((f32[72,128]{1,0:T(8,128)S(1)}, f32[72,128]{1,0:T(8,128)S(1)}, u32[]{:S(2)}, u32[]{:S(2)}) %collective-permute-start.7) | collective-permute-done | bytes 36896 | tf_op jit(solution)/shard_map/ppermute | solution.py:562
  44.8 1.5 %collective-permute-start.12 = (f32[72,128]{1,0:T(8,128)S(1)}, f32[72,128]{1,0:T(8,128)S(1)}, u32[]{:S(2)}, u32[]{:S(2)}) collective-permute-start(f32[72,128]{1,0:T(8,128)S(1)} %add_add_fusion.1), channel_id=1, source_target_pairs={{0,24},{1,25},{2,26},{3,27},{4,28},{5,29},{6,30},{7,31},{8,16},{9,... | collective-permute-start | bytes 110600 | tf_op jit(solution)/shard_map/ppermute | solution.py:562
  46.3 0.0 collective-permute-start.11
  46.3 2.9 %collective-permute-start.10 = (f32[72,128]{1,0:T(8,128)S(1)}, f32[72,128]{1,0:T(8,128)S(1)}, u32[]{:S(2)}, u32[]{:S(2)}) collective-permute-start(f32[72,128]{1,0:T(8,128)S(1)} %add_add_fusion.1), channel_id=1, source_target_pairs={{0,8},{1,9},{2,10},{3,11},{4,12},{5,13},{6,14},{7,15},{8,0},{9,1},... | collective-permute-start | bytes 110600 | tf_op jit(solution)/shard_map/ppermute | solution.py:562
  49.2 1.4 %collective-permute-done.12 = f32[72,128]{1,0:T(8,128)S(1)} collective-permute-done((f32[72,128]{1,0:T(8,128)S(1)}, f32[72,128]{1,0:T(8,128)S(1)}, u32[]{:S(2)}, u32[]{:S(2)}) %collective-permute-start.12) | collective-permute-done | bytes 36896 | tf_op jit(solution)/shard_map/ppermute | solution.py:562
  50.6 0.9 %collective-permute-done.11 = f32[72,128]{1,0:T(8,128)S(1)} collective-permute-done((f32[72,128]{1,0:T(8,128)S(1)}, f32[72,128]{1,0:T(8,128)S(1)}, u32[]{:S(2)}, u32[]{:S(2)}) %collective-permute-start.11) | collective-permute-done | bytes 36896 | tf_op jit(solution)/shard_map/ppermute | solution.py:562
  51.5 0.1 collective-permute-done.10
  51.6 0.0 copy-done.1
  51.6 8.5 %shard_map.76 = f32[96,128]{1,0:T(8,128)} custom-call(f32[72,128]{1,0:T(8,128)S(1)} %add_add_fusion.gram_ref, f32[64,128]{1,0:T(8,128)S(1)} %copy-done.1, bf16[3,126,32,128]{3,2,1,0:T(8,128)(2,1)S(1)} %bitcast.22, f32[96,128]{1,0:T(8,128)S(1)} %get-tuple-element.32.first_ref, f32[96,128]{1,0:T(8,128)S(1)} %get-tuple-element.37.second_ref), custom_call_target="tpu_custom_call" | custom-call | tf_op jit(solution)/shard_map/pallas_call | solution.py:534
  (9 shorter events, 0.1 us)
Async XLA Ops:
  2.2 9.7 %copy-start.2 = (f32[32,8,128]{2,1,0:T(8,128)S(1)}, f32[32,8,128]{2,1,0:T(8,128)}, u32[]{:S(2)}) copy-start(f32[32,8,128]{2,1,0:T(8,128)} %get-tuple-element.22) | copy-start | bytes 393220
  2.2 9.7 %collective-permute-start = (f32[3,8,128]{2,1,0:T(8,128)}, f32[3,8,128]{2,1,0:T(8,128)S(1)}, u32[]{:S(2)}, u32[]{:S(2)}) collective-permute-start(f32[3,8,128]{2,1,0:T(8,128)} %get-tuple-element.20), channel_id=1, source_target_pairs={{0,4},{4,8},{8,12},{12,16},{16,20},{20,24},{24,28},{28,0},{1,5},{5... | collective-permute-start | bytes 36872 | tf_op jit(solution)/shard_map/ppermute | solution.py:546
  5.2 6.7 %collective-permute-start.1 = (f32[3,8,128]{2,1,0:T(8,128)}, f32[3,8,128]{2,1,0:T(8,128)S(1)}, u32[]{:S(2)}, u32[]{:S(2)}) collective-permute-start(f32[3,8,128]{2,1,0:T(8,128)} %get-tuple-element.21), channel_id=1, source_target_pairs={{0,28},{4,0},{8,4},{12,8},{16,12},{20,16},{24,20},{28,24},{1,29},{... | collective-permute-start | bytes 36872 | tf_op jit(solution)/shard_map/ppermute | solution.py:546
  11.7 2.3 %copy-start = (bf16[32,1,3,126,128]{4,0,3,2,1:T(8,128)(2,1)S(1)}, bf16[32,1,3,126,128]{4,0,3,2,1:T(8,128)(2,1)}, u32[]{:S(2)}) copy-start(bf16[32,1,3,126,128]{4,0,3,2,1:T(8,128)(2,1)} %param.8) | copy-start | bytes 9289732
  12.0 4.2 %copy-start.3 = (s32[32,1,4]{0,2,1:T(4,128)S(1)}, s32[32,1,4]{0,2,1:T(4,128)}, u32[]{:S(2)}) copy-start(s32[32,1,4]{0,2,1:T(4,128)} %param.7) | copy-start | bytes 1540
  12.0 4.6 %collective-permute-start.3 = (f32[36,8,128]{2,1,0:T(8,128)S(1)}, f32[36,8,128]{2,1,0:T(8,128)S(1)}, u32[]{:S(2)}, u32[]{:S(2)}) collective-permute-start(f32[36,8,128]{2,1,0:T(8,128)S(1)} %pad_maximum_fusion.mid_ref), channel_id=1, source_target_pairs={{0,3},{1,0},{2,1},{3,2},{4,7},{5,4},{6,5},{7,6},{8,11},{9,8},{10,9... | collective-permute-start | bytes 442376 | tf_op jit(solution)/shard_map/ppermute | solution.py:546
  12.7 5.7 %collective-permute-start.2 = (f32[36,8,128]{2,1,0:T(8,128)S(1)}, f32[36,8,128]{2,1,0:T(8,128)S(1)}, u32[]{:S(2)}, u32[]{:S(2)}) collective-permute-start(f32[36,8,128]{2,1,0:T(8,128)S(1)} %pad_maximum_fusion.mid_ref), channel_id=1, source_target_pairs={{0,1},{1,2},{2,3},{3,0},{4,5},{5,6},{6,7},{7,4},{8,9},{9,10},{10,1... | collective-permute-start | bytes 442376 | tf_op jit(solution)/shard_map/ppermute | solution.py:546
  24.3 4.2 %collective-permute-start.5 = (f32[34,8,128]{2,1,0:T(8,128)S(1)}, f32[34,8,128]{2,1,0:T(8,128)S(1)}, u32[]{:S(2)}, u32[]{:S(2)}) collective-permute-start(f32[34,8,128]{2,1,0:T(8,128)S(1)} %shard_map.72.mid_ref.first_ref), channel_id=1, source_target_pairs={{0,3},{1,0},{2,1},{3,2},{4,7},{5,4},{6,5},{7,6},{8,11},{9,8},{10,9... | collective-permute-start | bytes 417800 | tf_op jit(solution)/shard_map/ppermute | solution.py:546
  24.8 5.4 %collective-permute-start.4 = (f32[34,8,128]{2,1,0:T(8,128)S(1)}, f32[34,8,128]{2,1,0:T(8,128)S(1)}, u32[]{:S(2)}, u32[]{:S(2)}) collective-permute-start(f32[34,8,128]{2,1,0:T(8,128)S(1)} %shard_map.72.mid_ref.first_ref), channel_id=1, source_target_pairs={{0,1},{1,2},{2,3},{3,0},{4,5},{5,6},{6,7},{7,4},{8,9},{9,10},{10,1... | collective-permute-start | bytes 417800 | tf_op jit(solution)/shard_map/ppermute | solution.py:546
  27.0 24.5 %copy-start.1 = (f32[64,128]{1,0:T(8,128)S(1)}, f32[64,128]{1,0:T(8,128)}, u32[]{:S(2)}) copy-start(f32[64,128]{1,0:T(8,128)} %shard_map.69.b_ref) | copy-start | bytes 98308
  36.9 1.3 %collective-permute-start.6 = (f32[72,128]{1,0:T(8,128)S(1)}, f32[72,128]{1,0:T(8,128)S(1)}, u32[]{:S(2)}, u32[]{:S(2)}) collective-permute-start(f32[72,128]{1,0:T(8,128)S(1)} %get-tuple-element.35), channel_id=1, source_target_pairs={{0,1},{1,0},{2,3},{3,2},{4,5},{5,4},{6,7},{7,6},{8,9},{9,8},{10,11... | collective-permute-start | bytes 110600 | tf_op jit(solution)/shard_map/ppermute | solution.py:562
  38.2 5.2 %collective-permute-start.9 = (f32[72,128]{1,0:T(8,128)S(1)}, f32[72,128]{1,0:T(8,128)S(1)}, u32[]{:S(2)}, u32[]{:S(2)}) collective-permute-start(f32[72,128]{1,0:T(8,128)S(1)} %add.21), channel_id=1, source_target_pairs={{0,6},{1,7},{2,4},{3,5},{4,2},{5,3},{6,0},{7,1},{8,14},{9,15},{10,... | collective-permute-start | bytes 110600 | tf_op jit(solution)/shard_map/ppermute | solution.py:562
  38.2 5.2 %collective-permute-start.8 = (f32[72,128]{1,0:T(8,128)S(1)}, f32[72,128]{1,0:T(8,128)S(1)}, u32[]{:S(2)}, u32[]{:S(2)}) collective-permute-start(f32[72,128]{1,0:T(8,128)S(1)} %add.21), channel_id=1, source_target_pairs={{0,4},{1,5},{2,6},{3,7},{4,0},{5,1},{6,2},{7,3},{8,12},{9,13},{10,... | collective-permute-start | bytes 110600 | tf_op jit(solution)/shard_map/ppermute | solution.py:562
  40.8 4.0 %collective-permute-start.7 = (f32[72,128]{1,0:T(8,128)S(1)}, f32[72,128]{1,0:T(8,128)S(1)}, u32[]{:S(2)}, u32[]{:S(2)}) collective-permute-start(f32[72,128]{1,0:T(8,128)S(1)} %add.21), channel_id=1, source_target_pairs={{0,2},{1,3},{2,0},{3,1},{4,6},{5,7},{6,4},{7,5},{8,10},{9,11},{10,... | collective-permute-start | bytes 110600 | tf_op jit(solution)/shard_map/ppermute | solution.py:562
  44.8 5.8 %collective-permute-start.12 = (f32[72,128]{1,0:T(8,128)S(1)}, f32[72,128]{1,0:T(8,128)S(1)}, u32[]{:S(2)}, u32[]{:S(2)}) collective-permute-start(f32[72,128]{1,0:T(8,128)S(1)} %add_add_fusion.1), channel_id=1, source_target_pairs={{0,24},{1,25},{2,26},{3,27},{4,28},{5,29},{6,30},{7,31},{8,16},{9,... | collective-permute-start | bytes 110600 | tf_op jit(solution)/shard_map/ppermute | solution.py:562
  46.3 5.2 %collective-permute-start.11 = (f32[72,128]{1,0:T(8,128)S(1)}, f32[72,128]{1,0:T(8,128)S(1)}, u32[]{:S(2)}, u32[]{:S(2)}) collective-permute-start(f32[72,128]{1,0:T(8,128)S(1)} %add_add_fusion.1), channel_id=1, source_target_pairs={{0,16},{1,17},{2,18},{3,19},{4,20},{5,21},{6,22},{7,23},{8,24},{9,... | collective-permute-start | bytes 110600 | tf_op jit(solution)/shard_map/ppermute | solution.py:562
  46.3 5.3 %collective-permute-start.10 = (f32[72,128]{1,0:T(8,128)S(1)}, f32[72,128]{1,0:T(8,128)S(1)}, u32[]{:S(2)}, u32[]{:S(2)}) collective-permute-start(f32[72,128]{1,0:T(8,128)S(1)} %add_add_fusion.1), channel_id=1, source_target_pairs={{0,8},{1,9},{2,10},{3,11},{4,12},{5,13},{6,14},{7,15},{8,0},{9,1},... | collective-permute-start | bytes 110600 | tf_op jit(solution)/shard_map/ppermute | solution.py:562
